TPU v7x, 128 devices: a whole 4x4x4 slice. The times are simulated.
128 devices in a mesh: row: 16 (over z, y), col: 8 (over x, core).
Axes of the slice: x: 4, y: 4, z: 4, core: 2. Of those that a mesh axis runs over, the one named last changes fastest.
Arguments:
- queries: bfloat16 [4096, 480], P('row'), may hold values from -64 to 64
- keys: bfloat16 [4096, 960], P(('col', 'row')), may hold values from -32 to 32
- frame_table: float32 [12, 4096], replicated, may hold values from -6 to 6, as said below
- frame_index: int32 [4096], replicated, may hold values from 0 to 4095, each once
- pair_list: int32 [16, 8, 2], P('row', 'col'), may hold values from 0 to 8, as said below
- pair: bfloat16 [16, 8, 2, 128, 128, 128], P('row', 'col'), may hold values from -6 to 6
- pair_weight: bfloat16 [128, 12], replicated, may hold values from -0.5 to 0.5
- point_weight: float32 [12], replicated, may hold values from -2.5 to 1
- out_weight: bfloat16 [2016, 384], replicated, may hold values from -0.125 to 0.125
- cotangent: bfloat16 [4096, 384], P('row'), may hold values from -6 to 6
Outputs:
- update: bfloat16 [4096, 384], P(('row', 'col'))
- grad_queries: bfloat16 [4096, 480], P(('row', 'col'))
- grad_keys: bfloat16 [4096, 960], P(('col', 'row'))
- grad_pair: bfloat16 [16, 8, 2, 128, 128, 128], P('row', 'col')
Inputs may be any that keep to these rules, and one draw needn't show every extreme that they name: `pair_list`: A value below 8 names a local pair (query block value // 4 of the row index, key block value % 4 of the col index); 8 marks an empty slot. The slots of one device name distinct pairs, and every query block's own block is listed as a key block. Listed pairs lie near the diagonal, with a few far ones. `frame_table`: rotation rows form orthonormal matrices.
All inputs are finite; a program needn't handle non-finite values.
Results may differ from a plain program's by a relative error of at most 0.03.
Values may be sent and summed in bfloat16 or wider, within the bound.
No kernel may reach another device: no remote copies, remote signals or barrier semaphores. Data moves between devices by JAX's collectives and lax.ppermute only.
A program may use at most 128 MiB of HBM per device.

v0:
```python
import math

import jax
import jax.numpy as jnp
from jax import lax
from jax.sharding import PartitionSpec as P

H = 12
C = 16
P_SIZE = 8
PV = 8
PW = 128
BLK = 128
QB_DEV = 2
QF = 480
KF = 960


NEG_FILL = -1e30
HIGH = lax.Precision.HIGHEST


def frame_parts(columns):
    rotation = columns[:9].T.reshape(-1, 3, 3)
    return (rotation, columns[9:].T)


def to_global(local, rotation, offset):
    return jnp.einsum("nab,nbk->nak", rotation, local, precision=HIGH) + offset[:, :, None]


def to_local(vector, rotation):
    return jnp.einsum("nab,nak->nbk", rotation, vector, precision=HIGH)


def add_rows(total, part, start):
    older = lax.dynamic_slice_in_dim(total, start, part.shape[0], 0)
    return lax.dynamic_update_slice_in_dim(total, older + part, start, 0)


def block_rows(array, start):
    return lax.dynamic_slice_in_dim(array, start, BLK, 0)


def attention_out(totals):
    denominator, scalar_sum, value_sum, pair_sum = totals
    row_total = denominator.shape[0]
    out_scalar = scalar_sum.reshape(row_total, H, C) / denominator[:, :, None]
    out_value = value_sum.reshape(row_total, 3, H, PV) / denominator[:, None, :, None]
    out_pair = pair_sum.reshape(row_total, H, PW) / denominator[:, :, None]
    return (out_scalar, out_value, out_pair)


def feature_rows(outputs, rotation, offset):
    out_scalar, out_value, out_pair = outputs
    row_total = out_scalar.shape[0]
    local_value = to_local(out_value.reshape(row_total, 3, H * PV) - offset[:, :, None], rotation)
    return jnp.concatenate(
        [
            out_scalar.reshape(row_total, H * C),
            local_value.reshape(row_total, 3 * H * PV),
            out_pair.reshape(row_total, H * PW),
        ],
        axis=1,
    ).astype(jnp.bfloat16)


def delta_rows(outputs, grads):
    out_scalar, out_value, out_pair = outputs
    grad_s, grad_v, grad_z = grads
    return (
        jnp.sum(grad_s.astype(jnp.float32) * out_scalar, axis=2)
        + jnp.sum(grad_v.astype(jnp.float32) * out_value, axis=(1, 3))
        + jnp.sum(grad_z.astype(jnp.float32) * out_pair, axis=2)
    )


def on_device(
    queries,
    keys,
    frame_table,
    frame_index,
    pair_list,
    pair,
    pair_weight,
    point_weight,
    out_weight,
    cotangent,
):
    rows_total = lax.axis_size("row")
    cols_total = lax.axis_size("col")
    row_index = lax.axis_index("row")
    col_index = lax.axis_index("col")
    query_count = queries.shape[0]
    key_count = keys.shape[0]
    share_rows = query_count // cols_total
    key_blocks = key_count * rows_total // BLK
    width_scalar = H * C
    width_point = 3 * H * P_SIZE
    width_value = 3 * H * PV
    width_pair = H * PW
    scale_scalar = 1.0 / math.sqrt(C)
    scale_point = math.sqrt(2.0 / (9.0 * P_SIZE))
    scale_logit = math.sqrt(1.0 / 3.0)
    empty_code = QB_DEV * key_blocks
    head_gamma = jax.nn.softplus(point_weight)
    gamma_point = head_gamma[None, None, :, None]
    query_ids = row_index * query_count + jnp.arange(query_count, dtype=jnp.int32)
    key_ids = (col_index * rows_total + row_index) * key_count + jnp.arange(
        key_count, dtype=jnp.int32
    )
    rot_query, off_query = frame_parts(
        jnp.take(frame_table, jnp.take(frame_index, query_ids), axis=1)
    )
    rot_key, off_key = frame_parts(jnp.take(frame_table, jnp.take(frame_index, key_ids), axis=1))
    share_start = col_index * share_rows

    def own_rows(array):
        return lax.dynamic_slice_in_dim(array, share_start, share_rows, 0)

    query_scalar = queries[:, :width_scalar].reshape(query_count, H, C)
    query_point = (
        to_global(
            queries[:, width_scalar:].astype(jnp.float32).reshape(query_count, 3, H * P_SIZE),
            rot_query,
            off_query,
        )
        .astype(jnp.bfloat16)
        .reshape(query_count, 3, H, P_SIZE)
    )
    point_start = 2 * width_scalar
    key_point = to_global(
        keys[:, point_start : point_start + width_point]
        .astype(jnp.float32)
        .reshape(key_count, 3, H * P_SIZE),
        rot_key,
        off_key,
    ).astype(jnp.bfloat16)
    value_point = to_global(
        keys[:, point_start + width_point :].astype(jnp.float32).reshape(key_count, 3, H * PV),
        rot_key,
        off_key,
    ).astype(jnp.bfloat16)
    key_wire = jnp.concatenate(
        [
            keys[:, :point_start],
            key_point.reshape(key_count, width_point),
            value_point.reshape(key_count, width_value),
        ],
        axis=1,
    )
    key_all = lax.all_gather(key_wire, "row", axis=0, tiled=True)
    grad_feat = jnp.einsum(
        "ns,fs->nf", cotangent, out_weight, preferred_element_type=jnp.float32
    ).astype(jnp.bfloat16)
    grad_scalar = grad_feat[:, :width_scalar].reshape(query_count, H, C)
    grad_value = (
        jnp.einsum(
            "nab,nbk->nak",
            rot_query,
            grad_feat[:, width_scalar : width_scalar + width_value]
            .astype(jnp.float32)
            .reshape(query_count, 3, H * PV),
            precision=HIGH,
        )
        .astype(jnp.bfloat16)
        .reshape(query_count, 3, H, PV)
    )
    grad_pairout = grad_feat[:, width_scalar + width_value :].reshape(query_count, H, PW)
    codes = pair_list.reshape(-1)
    tiles = pair.reshape(-1, BLK, BLK, PW)
    slot_total = codes.shape[0]
    pieces = []
    row_max = jnp.full((query_count, H), NEG_FILL, jnp.float32)
    for slot_index in range(slot_total):
        slot_code = codes[slot_index]
        is_listed = slot_code < empty_code
        safe_code = jnp.where(is_listed, slot_code, 0)
        query_start = safe_code // key_blocks * BLK
        key_start = safe_code % key_blocks * BLK
        key_rows = lax.dynamic_slice_in_dim(key_all, key_start, BLK, 0)
        query_block = block_rows(query_scalar, query_start)
        query_spot = block_rows(query_point, query_start)
        key_block = key_rows[:, :width_scalar].reshape(BLK, H, C)
        value_block = key_rows[:, width_scalar:point_start].reshape(BLK, H, C)
        key_spot = key_rows[:, point_start : point_start + width_point].reshape(BLK, 3, H, P_SIZE)
        value_spot = key_rows[:, point_start + width_point :].reshape(BLK, 3, H, PV)
        pair_tile = tiles[slot_index]
        scalar_term = jnp.einsum(
            "ihc,jhc->hij", query_block, key_block, preferred_element_type=jnp.float32
        )
        cross_term = jnp.einsum(
            "idhp,jdhp->hij", query_spot, key_spot, preferred_element_type=jnp.float32
        )
        query_square = jnp.sum(jnp.square(query_spot.astype(jnp.float32)), axis=(1, 3))
        key_square = jnp.sum(jnp.square(key_spot.astype(jnp.float32)), axis=(1, 3))
        distance = query_square.T[:, :, None] + key_square.T[:, None, :] - 2.0 * cross_term
        bias_term = jnp.einsum(
            "ijc,ch->hij", pair_tile, pair_weight, preferred_element_type=jnp.float32
        )
        logit_block = scale_logit * (
            scale_scalar * scalar_term
            + bias_term
            - 0.5 * scale_point * head_gamma[:, None, None] * distance
        )
        logit_block = jnp.where(is_listed, logit_block, NEG_FILL)
        older = block_rows(row_max, query_start)
        row_max = lax.dynamic_update_slice_in_dim(
            row_max, jnp.maximum(older, jnp.max(logit_block, axis=2).T), query_start, 0
        )
        pieces.append(
            (
                is_listed,
                query_start,
                key_start,
                query_block,
                query_spot,
                key_block,
                value_block,
                key_spot,
                value_spot,
                pair_tile,
                logit_block,
            )
        )
    global_max = lax.pmax(row_max, "col")
    denominator = jnp.zeros((query_count, H), jnp.float32)
    scalar_sum = jnp.zeros((query_count, width_scalar), jnp.float32)
    value_sum = jnp.zeros((query_count, width_value), jnp.float32)
    pair_sum = jnp.zeros((query_count, width_pair), jnp.float32)
    for piece in pieces:
        (
            is_listed,
            query_start,
            key_start,
            query_block,
            query_spot,
            key_block,
            value_block,
            key_spot,
            value_spot,
            pair_tile,
            logit_block,
        ) = piece
        max_block = block_rows(global_max, query_start)
        weights = jnp.where(is_listed, jnp.exp(logit_block - max_block.T[:, :, None]), 0.0)
        rounded = weights.astype(jnp.bfloat16)
        denominator = add_rows(denominator, jnp.sum(weights, axis=2).T, query_start)
        scalar_sum = add_rows(
            scalar_sum,
            jnp.einsum(
                "hij,jhc->ihc", rounded, value_block, preferred_element_type=jnp.float32
            ).reshape(BLK, width_scalar),
            query_start,
        )
        value_sum = add_rows(
            value_sum,
            jnp.einsum(
                "hij,jdhp->idhp", rounded, value_spot, preferred_element_type=jnp.float32
            ).reshape(BLK, width_value),
            query_start,
        )
        pair_sum = add_rows(
            pair_sum,
            jnp.einsum(
                "hij,ijc->ihc", rounded, pair_tile, preferred_element_type=jnp.float32
            ).reshape(BLK, width_pair),
            query_start,
        )
    totals = lax.psum((denominator, scalar_sum, value_sum, pair_sum), "col")
    outputs = attention_out(totals)
    feat_own = feature_rows(
        tuple((own_rows(item) for item in outputs)), own_rows(rot_query), own_rows(off_query)
    )
    log_total = global_max + jnp.log(totals[0])
    delta_all = delta_rows(outputs, (grad_scalar, grad_value, grad_pairout))
    update = jnp.dot(feat_own, out_weight, preferred_element_type=jnp.float32).astype(jnp.bfloat16)
    query_total = jnp.zeros((query_count, QF), jnp.float32)
    key_total = jnp.zeros((key_blocks * BLK, KF), jnp.float32)
    tile_grads = []
    for piece in pieces:
        (
            is_listed,
            query_start,
            key_start,
            query_block,
            query_spot,
            key_block,
            value_block,
            key_spot,
            value_spot,
            pair_tile,
            logit_block,
        ) = piece
        lse_block = block_rows(log_total, query_start)
        delta_block = block_rows(delta_all, query_start)
        grad_s_block = block_rows(grad_scalar, query_start)
        grad_v_block = block_rows(grad_value, query_start)
        grad_z_block = block_rows(grad_pairout, query_start)
        weights = jnp.where(is_listed, jnp.exp(logit_block - lse_block.T[:, :, None]), 0.0)
        rounded = weights.astype(jnp.bfloat16)
        touch = jnp.einsum(
            "ihc,jhc->hij", grad_s_block, value_block, preferred_element_type=jnp.float32
        )
        touch = touch + jnp.einsum(
            "idhp,jdhp->hij", grad_v_block, value_spot, preferred_element_type=jnp.float32
        )
        touch = touch + jnp.einsum(
            "ihc,ijc->hij", grad_z_block, pair_tile, preferred_element_type=jnp.float32
        )
        score_grad = (scale_logit * weights * (touch - delta_block.T[:, :, None])).astype(
            jnp.bfloat16
        )
        tile_grad = jnp.einsum(
            "hij,ihc->ijc", rounded, grad_z_block, preferred_element_type=jnp.float32
        ) + jnp.einsum("hij,ch->ijc", score_grad, pair_weight, preferred_element_type=jnp.float32)
        tile_grads.append(tile_grad.astype(jnp.bfloat16))
        score_float = score_grad.astype(jnp.float32)
        row_sum = jnp.sum(score_float, axis=2).T
        col_sum = jnp.sum(score_float, axis=1).T
        grad_q_scalar = scale_scalar * jnp.einsum(
            "hij,jhc->ihc", score_grad, key_block, preferred_element_type=jnp.float32
        )
        grad_q_point = (
            -scale_point
            * gamma_point
            * (
                row_sum[:, None, :, None] * query_spot.astype(jnp.float32)
                - jnp.einsum(
                    "hij,jdhp->idhp", score_grad, key_spot, preferred_element_type=jnp.float32
                )
            )
        )
        grad_k_scalar = scale_scalar * jnp.einsum(
            "hij,ihc->jhc", score_grad, query_block, preferred_element_type=jnp.float32
        )
        grad_k_point = (
            -scale_point
            * gamma_point
            * (
                col_sum[:, None, :, None] * key_spot.astype(jnp.float32)
                - jnp.einsum(
                    "hij,idhp->jdhp", score_grad, query_spot, preferred_element_type=jnp.float32
                )
            )
        )
        grad_v_scalar = jnp.einsum(
            "hij,ihc->jhc", rounded, grad_s_block, preferred_element_type=jnp.float32
        )
        grad_v_point = jnp.einsum(
            "hij,idhp->jdhp", rounded, grad_v_block, preferred_element_type=jnp.float32
        )
        query_part = jnp.concatenate(
            [grad_q_scalar.reshape(BLK, width_scalar), grad_q_point.reshape(BLK, width_point)],
            axis=1,
        )
        key_part = jnp.concatenate(
            [
                grad_k_scalar.reshape(BLK, width_scalar),
                grad_v_scalar.reshape(BLK, width_scalar),
                grad_k_point.reshape(BLK, width_point),
                grad_v_point.reshape(BLK, width_value),
            ],
            axis=1,
        )
        query_total = add_rows(query_total, query_part, query_start)
        key_total = add_rows(key_total, key_part, key_start)
    query_share = lax.psum_scatter(query_total, "col", scatter_dimension=0, tiled=True)
    key_share = lax.psum_scatter(key_total, "row", scatter_dimension=0, tiled=True)
    query_local = to_local(
        query_share[:, width_scalar:].reshape(share_rows, 3, H * P_SIZE), own_rows(rot_query)
    )
    grad_queries = jnp.concatenate(
        [query_share[:, :width_scalar], query_local.reshape(share_rows, width_point)], axis=1
    ).astype(jnp.bfloat16)
    key_local = to_local(
        key_share[:, point_start : point_start + width_point].reshape(key_count, 3, H * P_SIZE),
        rot_key,
    )
    value_local = to_local(
        key_share[:, point_start + width_point :].reshape(key_count, 3, H * PV), rot_key
    )
    grad_keys = jnp.concatenate(
        [
            key_share[:, :point_start],
            key_local.reshape(key_count, width_point),
            value_local.reshape(key_count, width_value),
        ],
        axis=1,
    ).astype(jnp.bfloat16)
    grad_pair = jnp.stack(tile_grads, axis=0).reshape(pair.shape)
    return (update, grad_queries, grad_keys, grad_pair)


def solution(mesh):
    in_specs = (
        P("row", None),
        P(("col", "row"), None),
        P(),
        P(),
        P("row", "col", None),
        P("row", "col", None, None, None, None),
        P(),
        P(),
        P(),
        P("row", None),
    )
    out_specs = (
        P(("row", "col"), None),
        P(("row", "col"), None),
        P(("col", "row"), None),
        P("row", "col", None, None, None, None),
    )
    return jax.shard_map(
        on_device, mesh=mesh, in_specs=in_specs, out_specs=out_specs, check_vma=False
    )
```

profile of v0, /device:TPU:2, one launch (start us, length us, event | category | flops | bytes accessed | tf_op | source)
XLA Modules:
  0.0 354.9 jit_solution(18007644100101141875)
XLA Ops:
  14.6 4.4 %fusion.6 = f32[12,128,128]{2,0,1:T(8,128)} fusion(bf16[1,1,2,128,128,128]{5,4,3,2,1,0:T(8,128)(2,1)} %param.15, bf16[128,12]{0,1:T(8,128)(2,1)} %param.16), kind=kOutput, calls=%fused_computation.13 | convolution fusion | flops 50331648 | bytes 4984832 | tf_op jit(solution)/shard_map/ijc,ch->hij/dot_general | solution.py:198
  19.0 3.4 fusion.12
  22.5 2.0 copy.158
  24.4 2.2 gather_fusion.1
  27.4 1.7 gather_fusion.2
  29.2 2.3 gather_fusion.3
  35.9 2.4 copy.173
  42.6 2.2 fusion.42
  45.7 26.4 %all_gather.3 = bf16[512,960]{1,0:T(8,128)(2,1)S(1)} all-gather(bf16[32,960]{1,0:T(8,128)(2,1)S(1)} %pad_maximum_fusion), channel_id=1, replica_groups=mesh['row'=16,'col'=8] {'row'}, dimensions={0}, use_global_device_ids=true | all-gather | bytes 1044480 | tf_op jit(solution)/shard_map/all_gather | solution.py:152
  73.7 1.6 copy.302
  75.3 1.5 copy.299
  78.8 1.6 copy.291
  82.5 1.6 copy.301
  86.7 1.5 fusion.133
  88.2 20.8 %pmax.7 = f32[256,12]{0,1:T(8,128)S(1)} all-reduce(f32[256,12]{0,1:T(8,128)S(1)} %constant_dynamic-update-slice_fusion.8), channel_id=1, replica_groups=mesh['row'=16,'col'=8] {'col'}, use_global_device_ids=true, to_apply=%region_6.7 | all-reduce | flops 3072 | bytes 24576 | tf_op jit(solution)/shard_map/pmax | solution.py:226
  111.0 1.7 fusion.135
  116.5 1.7 fusion.134
  120.0 4.5 %fusion.10 = f32[128,12,128]{2,1,0:T(8,128)} fusion(bf16[12,128,128]{2,0,1:T(8,128)(2,1)} %copy.188, bf16[1,1,2,128,128,128]{5,4,3,2,1,0:T(8,128)(2,1)} %param.15), kind=kOutput, calls=%fused_computation.17 | convolution fusion | flops 50331648 | bytes 5505024 | tf_op jit(solution)/shard_map/hij,ijc->ihc/dot_general | solution.py:265
  124.5 2.4 copy.189
  126.9 4.6 %fusion.4 = f32[128,12,128]{2,1,0:T(8,128)} fusion(bf16[12,128,128]{2,0,1:T(8,128)(2,1)} %copy.190, bf16[1,1,2,128,128,128]{5,4,3,2,1,0:T(8,128)(2,1)} %param.15), kind=kOutput, calls=%fused_computation.11 | convolution fusion | flops 50331648 | bytes 5505024 | tf_op jit(solution)/shard_map/hij,ijc->ihc/dot_general | solution.py:265
  131.5 2.4 copy.191
  137.4 2.1 constant_dynamic-update-slice_fusion.1
  139.4 2.1 constant_dynamic-update-slice_fusion
  141.6 23.6 %psum.29 = f32[256,12]{0,1:T(8,128)S(1)} all-reduce(f32[256,12]{0,1:T(8,128)S(1)} %constant_dynamic-update-slice_fusion.4), channel_id=1, replica_groups=mesh['row'=16,'col'=8] {'col'}, use_global_device_ids=true, to_apply=%region_10.11 | all-reduce | flops 3072 | bytes 24576 | tf_op jit(solution)/shard_map/psum | solution.py:270
  166.5 1.7 convolution_convert_fusion
  170.1 2.2 copy.306
  173.5 5.7 %fusion.8 = f32[128,12,128]{2,1,0:T(8,128)} fusion(bf16[128,12,128]{2,1,0:T(8,128)(2,1)} %copy.304, bf16[1,1,2,128,128,128]{5,4,3,2,1,0:T(8,128)(2,1)} %param.15), kind=kOutput, calls=%fused_computation.15 | convolution fusion | flops 50331648 | bytes 5505024 | tf_op jit(solution)/shard_map/ihc,ijc->hij/dot_general | solution.py:308
  179.2 5.6 %fusion.2 = f32[128,12,128]{2,1,0:T(8,128)} fusion(bf16[128,12,128]{2,1,0:T(8,128)(2,1)S(1)} %copy-done.7, bf16[1,1,2,128,128,128]{5,4,3,2,1,0:T(8,128)(2,1)} %param.15), kind=kOutput, calls=%fused_computation.9 | convolution fusion | flops 50331648 | bytes 5373952 | tf_op jit(solution)/shard_map/ihc,ijc->hij/dot_general | solution.py:308
  185.7 2.4 copy.202
  188.1 2.4 copy.215
  193.3 1.8 fusion.95
  195.1 9.7 %all-reduce.3.cloned.1.call-done = (f32[256,12,16]{0,2,1:T(8,128)}, f32[256,288]{0,1:T(8,128)}, f32[256,12,128]{0,2,1:T(8,128)}) async-done(((f32[256,12,16]{0,2,1:T(8,128)}, f32[256,288]{0,1:T(8,128)}, f32[256,12,128]{0,2,1:T(8,128)}), (f32[256,12,16]{0,2,1:T(8,128)}, f32[256,288]{0,1:T(8,128)}, f32[256,12,128]{0,2,1:T(8,128)})) %all-reduce.3.cloned.1.call-update) | async-done | bytes 2064400 | tf_op jit(solution)/shard_map/psum | solution.py:270
  204.8 2.0 copy.204
  206.8 3.9 %fusion.59 = (f32[256,96]{1,0:T(8,128)}, bf16[256,3,96]{2,1,0:T(4,128)(2,1)}) fusion(f32[256,3,96]{2,1,0:T(4,128)} %copy.204, f32[256,96]{1,0:T(8,128)} %copy.203, f32[256,3,3]{2,1,0:T(4,128)} %copy-done.34, bf16[256,3,96]{2,1,0:T(4,128)(2,1)} %copy.195), kind=kOutput, calls=%fused_computation.109 | convolution fusion | flops 2998272 | bytes 795648 | tf_op jit(solution)/shard_map/nab,nbk->nak/dot_general | solution.py:158
  210.7 1.8 copy.196
  212.4 1.6 constant_dynamic-slice_fusion.4
  215.0 2.1 convolution_bitcast_fusion.1
  217.1 2.3 multiply_reduce_fusion.1
  219.4 2.8 multiply_reduce_fusion
  225.3 1.9 convert_reduce_fusion
  229.4 1.9 fusion.44
  231.4 1.4 convert_reduce_fusion.2
  238.5 1.5 broadcast_in_dim.108
  241.2 1.9 fusion.60
  243.1 2.9 copy.288
  258.8 3.4 fusion.1
  262.2 6.4 %maximum_bitcast_fusion = bf16[1,1,2,128,128,128]{5,4,3,2,1,0:T(8,128)(2,1)} fusion(bf16[1,128,128,128]{3,2,1,0:T(8,128)(2,1)} %fusion.1, bf16[1,128,128,128]{3,2,1,0:T(8,128)(2,1)S(1)} %fusion), kind=kLoop, calls=%fused_computation.4 | loop fusion | flops 4194304 | bytes 16777216 | tf_op jit(solution)/shard_map/reshape | solution.py:391
  271.7 72.7 %reduce-scatter.9.cloned.1.call-done = f32[32,960]{1,0:T(8,128)} async-done(((f32[512,960]{1,0:T(8,128)}), f32[32,960]{1,0:T(8,128)}) %reduce-scatter.9.cloned.1.call-update) | async-done | bytes 122896
  (271 shorter events, 74.8 us)
Async XLA Ops:
  7.2 159.3 %copy-start = (bf16[2016,384]{1,0:T(8,128)(2,1)S(1)}, bf16[2016,384]{1,0:T(8,128)(2,1)}, u32[]{:S(2)}) copy-start(bf16[2016,384]{1,0:T(8,128)(2,1)} %param.18) | copy-start | bytes 4644868
  7.2 11.8 %copy-start.50 = (bf16[128,12]{0,1:T(8,128)(2,1)S(1)}, bf16[128,12]{0,1:T(8,128)(2,1)}, u32[]{:S(2)}) copy-start(bf16[128,12]{0,1:T(8,128)(2,1)} %param.16) | copy-start | bytes 9220
  7.2 197.6 %all-reduce.3.cloned.1.call-start = ((), (), s32[]{:S(2)}) async-start(), calls=%async_computation.4 | async-start | bytes 4128768 | tf_op jit(solution)/shard_map/psum | solution.py:270
  14.5 72.1 %copy-start.28 = (bf16[256,192]{0,1:T(8,128)(2,1)}, bf16[256,192]{0,1:T(8,128)(2,1)S(1)}, u32[]{:S(2)}) copy-start(bf16[256,192]{0,1:T(8,128)(2,1)S(1)} %slice.100) | copy-start | bytes 294916
  14.5 7.9 %copy-start.43 = (f32[12,4096]{1,0:T(8,128)S(1)}, f32[12,4096]{1,0:T(8,128)}, u32[]{:S(2)}) copy-start(f32[12,4096]{1,0:T(8,128)} %param.12) | copy-start | bytes 589828
  19.0 8.4 %copy-start.1 = (s32[4096]{0:T(1024)S(1)}, s32[4096]{0:T(1024)}, u32[]{:S(2)}) copy-start(s32[4096]{0:T(1024)} %param.13) | copy-start | bytes 49156
  19.0 14.0 %copy-start.52 = (f32[12]{0:T(128)S(1)}, f32[12]{0:T(128)}, u32[]{:S(2)}) copy-start(f32[12]{0:T(128)} %param.17) | copy-start | bytes 148
  19.0 16.1 %slice-start.1 = ((bf16[256,480]{0,1:T(8,128)(2,1)}), bf16[256,288]{0,1:T(8,128)(2,1)S(1)}, s32[]{:S(2)}) async-start(bf16[256,480]{0,1:T(8,128)(2,1)} %param.10), calls=%async_computation.6 | async-start | bytes 294912 | tf_op jit(solution)/shard_map/slice | solution.py:124
  32.3 13.4 %slice-start.2 = ((bf16[32,960]{1,0:T(8,128)(2,1)}), bf16[32,384]{1,0:T(8,128)(2,1)S(1)}, s32[]{:S(2)}) async-start(bf16[32,960]{1,0:T(8,128)(2,1)} %param.11), calls=%async_computation.7 | async-start | bytes 49152 | tf_op jit(solution)/shard_map/slice | solution.py:146
  38.7 46.5 %copy-start.51 = (f32[12]{0:T(128)S(1)}, f32[12]{0:T(128)}, u32[]{:S(2)}) copy-start(f32[12]{0:T(128)} %broadcast_multiply_fusion.1) | copy-start | bytes 148
  38.9 6.7 %copy-start.30 = (f32[32,3,3]{1,2,0:T(4,128)}, f32[32,3,3]{1,2,0:T(4,128)S(1)}, u32[]{:S(2)}) copy-start(f32[32,3,3]{1,2,0:T(4,128)S(1)} %copy.235) | copy-start | bytes 3460
  42.3 3.3 copy-start.47
  77.8 31.8 %copy-start.37 = (bf16[128,192]{0,1:T(8,128)(2,1)}, bf16[128,192]{0,1:T(8,128)(2,1)S(1)}, u32[]{:S(2)}) copy-start(bf16[128,192]{0,1:T(8,128)(2,1)S(1)} %copy.296) | copy-start | bytes 147460
  78.8 7.8 %copy-start.35 = (bf16[128,192]{0,1:T(8,128)(2,1)}, bf16[128,192]{0,1:T(8,128)(2,1)S(1)}, u32[]{:S(2)}) copy-start(bf16[128,192]{0,1:T(8,128)(2,1)S(1)} %copy.292) | copy-start | bytes 147460
  81.4 5.2 %copy-start.23 = (bf16[128,288]{0,1:T(8,128)(2,1)}, bf16[128,288]{0,1:T(8,128)(2,1)S(1)}, u32[]{:S(2)}) copy-start(bf16[128,288]{0,1:T(8,128)(2,1)S(1)} %copy.298) | copy-start | bytes 221188
  82.5 3.2 copy-start.17
  126.9 7.0 %copy-start.40 = (f32[12,16,128]{2,1,0:T(8,128)S(1)}, f32[12,16,128]{2,1,0:T(8,128)}, u32[]{:S(2)}) copy-start(f32[12,16,128]{2,1,0:T(8,128)} %fusion.134) | copy-start | bytes 294916
  126.9 7.1 %copy-start.41 = (f32[12,16,128]{2,1,0:T(8,128)S(1)}, f32[12,16,128]{2,1,0:T(8,128)}, u32[]{:S(2)}) copy-start(f32[12,16,128]{2,1,0:T(8,128)} %fusion.135) | copy-start | bytes 294916
  133.9 5.5 %copy-start.12 = (f32[128,12,128]{0,2,1:T(8,128)S(1)}, f32[128,12,128]{0,2,1:T(8,128)}, u32[]{:S(2)}) copy-start(f32[128,12,128]{0,2,1:T(8,128)} %copy.191) | copy-start | bytes 2359300
  134.0 7.5 %copy-start.27 = (f32[256,192]{0,1:T(8,128)}, f32[256,192]{0,1:T(8,128)S(1)}, u32[]{:S(2)}) copy-start(f32[256,192]{0,1:T(8,128)S(1)} %constant_dynamic-update-slice_fusion.6) | copy-start | bytes 589828
  134.1 31.1 %copy-start.46 = (f32[256,12]{0,1:T(8,128)S(1)}, f32[256,12]{0,1:T(8,128)}, u32[]{:S(2)}) copy-start(f32[256,12]{0,1:T(8,128)} %copy-done.45) | copy-start | bytes 36868
  136.1 5.4 %copy-start.25 = (f32[256,288]{0,1:T(8,128)}, f32[256,288]{0,1:T(8,128)S(1)}, u32[]{:S(2)}) copy-start(f32[256,288]{0,1:T(8,128)S(1)} %constant_dynamic-update-slice_fusion.2) | copy-start | bytes 884740
  141.5 127.1 %reduce-scatter.7.cloned.1.call-start = ((), (), s32[]{:S(2)}) async-start(), calls=%async_computation.2 | async-start | bytes 589824 | tf_op jit(solution)/shard_map/reduce_scatter | solution.py:368
  173.5 5.7 %copy-start.7 = (bf16[128,12,128]{2,1,0:T(8,128)(2,1)S(1)}, bf16[128,12,128]{2,1,0:T(8,128)(2,1)}, u32[]{:S(2)}) copy-start(bf16[128,12,128]{2,1,0:T(8,128)(2,1)} %copy.306) | copy-start | bytes 1179652
  179.2 5.6 %copy-start.49 = (f32[256,12]{0,1:T(8,128)S(1)}, f32[256,12]{0,1:T(8,128)}, u32[]{:S(2)}) copy-start(f32[256,12]{0,1:T(8,128)} %log_add_fusion) | copy-start | bytes 36868
  179.2 5.6 %copy-start.11 = (bf16[256,2016]{0,1:T(8,128)(2,1)S(1)}, bf16[256,2016]{0,1:T(8,128)(2,1)}, u32[]{:S(2)}) copy-start(bf16[256,2016]{0,1:T(8,128)(2,1)} %copy-done.10) | copy-start | bytes 3096580
  179.2 5.6 %slice-start = ((bf16[256,2016]{0,1:T(8,128)(2,1)}), bf16[256,288]{0,1:T(8,128)(2,1)S(1)}, s32[]{:S(2)}) async-start(bf16[256,2016]{0,1:T(8,128)(2,1)} %copy-done.10), calls=%async_computation.5 | async-start | bytes 294912 | tf_op jit(solution)/shard_map/slice | solution.py:161
  179.2 11.3 %copy-start.39 = (f32[256,96]{0,1:T(8,128)S(1)}, f32[256,96]{0,1:T(8,128)}, u32[]{:S(2)}) copy-start(f32[256,96]{0,1:T(8,128)} %broadcast_bitcast_fusion) | copy-start | bytes 294916
  184.8 8.3 %copy-start.26 = (bf16[256,192]{0,1:T(8,128)(2,1)}, bf16[256,192]{0,1:T(8,128)(2,1)S(1)}, u32[]{:S(2)}) copy-start(bf16[256,192]{0,1:T(8,128)(2,1)S(1)} %slice.134) | copy-start | bytes 294916
  193.3 26.1 %copy-start.5 = (bf16[12,128,128]{1,2,0:T(8,128)(2,1)}, bf16[12,128,128]{1,2,0:T(8,128)(2,1)S(1)}, u32[]{:S(2)}) copy-start(bf16[12,128,128]{1,2,0:T(8,128)(2,1)S(1)} %fusion.57) | copy-start | bytes 1179652
  223.2 8.2 %copy-start.13 = (f32[128,12,128]{0,2,1:T(8,128)S(1)}, f32[128,12,128]{0,2,1:T(8,128)}, u32[]{:S(2)}) copy-start(f32[128,12,128]{0,2,1:T(8,128)} %copy.202) | copy-start | bytes 2359300
  223.2 8.2 %copy-start.14 = (f32[12,128,128]{1,2,0:T(8,128)S(1)}, f32[12,128,128]{1,2,0:T(8,128)}, u32[]{:S(2)}) copy-start(f32[12,128,128]{1,2,0:T(8,128)} %convolution_bitcast_fusion.1) | copy-start | bytes 2359300
  225.3 7.5 %copy-start.36 = (bf16[128,192]{0,1:T(8,128)(2,1)S(1)}, bf16[128,192]{0,1:T(8,128)(2,1)}, u32[]{:S(2)}) copy-start(bf16[128,192]{0,1:T(8,128)(2,1)} %copy-done.35) | copy-start | bytes 147460
  225.3 7.7 %copy-start.18 = (bf16[128,288]{0,1:T(8,128)(2,1)S(1)}, bf16[128,288]{0,1:T(8,128)(2,1)}, u32[]{:S(2)}) copy-start(bf16[128,288]{0,1:T(8,128)(2,1)} %copy-done.17) | copy-start | bytes 221188
  225.3 7.7 %copy-start.21 = (bf16[128,3,12,8]{0,3,2,1:T(8,128)(2,1)S(1)}, bf16[128,3,12,8]{0,3,2,1:T(8,128)(2,1)}, u32[]{:S(2)}) copy-start(bf16[128,3,12,8]{0,3,2,1:T(8,128)(2,1)} %copy-done.20) | copy-start | bytes 221188
  229.4 5.4 %copy-start.4 = (bf16[12,128,128]{1,2,0:T(8,128)(2,1)S(1)}, bf16[12,128,128]{1,2,0:T(8,128)(2,1)}, u32[]{:S(2)}) copy-start(bf16[12,128,128]{1,2,0:T(8,128)(2,1)} %copy-done.3) | copy-start | bytes 1179652
  232.8 5.0 %copy-start.19 = (bf16[128,288]{0,1:T(8,128)(2,1)S(1)}, bf16[128,288]{0,1:T(8,128)(2,1)}, u32[]{:S(2)}) copy-start(bf16[128,288]{0,1:T(8,128)(2,1)} %copy-done.17) | copy-start | bytes 221188
  232.8 5.0 %copy-start.22 = (bf16[128,3,12,8]{0,3,2,1:T(8,128)(2,1)S(1)}, bf16[128,3,12,8]{0,3,2,1:T(8,128)(2,1)}, u32[]{:S(2)}) copy-start(bf16[128,3,12,8]{0,3,2,1:T(8,128)(2,1)} %copy-done.20) | copy-start | bytes 221188
  232.8 5.4 %copy-start.29 = (bf16[256,192]{0,1:T(8,128)(2,1)S(1)}, bf16[256,192]{0,1:T(8,128)(2,1)}, u32[]{:S(2)}) copy-start(bf16[256,192]{0,1:T(8,128)(2,1)} %copy-done.28) | copy-start | bytes 294916
  234.4 5.6 %copy-start.38 = (f32[12,16,128]{2,1,0:T(8,128)S(1)}, f32[12,16,128]{2,1,0:T(8,128)}, u32[]{:S(2)}) copy-start(f32[12,16,128]{2,1,0:T(8,128)} %fusion.95) | copy-start | bytes 294916
  234.4 6.7 %copy-start.42 = (f32[12,16,128]{2,1,0:T(8,128)S(1)}, f32[12,16,128]{2,1,0:T(8,128)}, u32[]{:S(2)}) copy-start(f32[12,16,128]{2,1,0:T(8,128)} %fusion.92) | copy-start | bytes 294916
  234.5 109.9 %reduce-scatter.9.cloned.1.call-start = ((), (), s32[]{:S(2)}) async-start(), calls=%async_computation.3 | async-start | bytes 2228224
  240.9 5.2 %copy-start.6 = (bf16[12,128,128]{1,2,0:T(8,128)(2,1)S(1)}, bf16[12,128,128]{1,2,0:T(8,128)(2,1)}, u32[]{:S(2)}) copy-start(bf16[12,128,128]{1,2,0:T(8,128)(2,1)} %copy-done.5) | copy-start | bytes 1179652
  243.1 5.4 %copy-start.48 = (f32[256,3,3]{0,2,1:T(4,128)S(1)}, f32[256,3,3]{0,2,1:T(4,128)}, u32[]{:S(2)}) copy-start(f32[256,3,3]{0,2,1:T(4,128)} %copy-done.47) | copy-start | bytes 27652
  243.1 7.4 %copy-start.44 = (bf16[256,12,16]{0,2,1:T(8,128)(2,1)S(1)}, bf16[256,12,16]{0,2,1:T(8,128)(2,1)}, u32[]{:S(2)}) copy-start(bf16[256,12,16]{0,2,1:T(8,128)(2,1)} %get-tuple-element.18) | copy-start | bytes 294916
  248.7 3.6 %copy-start.32 = (f32[32,3,3]{1,2,0:T(4,128)}, f32[32,3,3]{1,2,0:T(4,128)S(1)}, u32[]{:S(2)}) copy-start(f32[32,3,3]{1,2,0:T(4,128)S(1)} %copy.300) | copy-start | bytes 3460
  262.2 7.5 %copy-start.33 = (f32[32,3,3]{1,2,0:T(4,128)S(1)}, f32[32,3,3]{1,2,0:T(4,128)}, u32[]{:S(2)}) copy-start(f32[32,3,3]{1,2,0:T(4,128)} %copy-done.32) | copy-start | bytes 3460
  262.2 84.3 %copy-start.31 = (f32[32,3,3]{1,2,0:T(4,128)S(1)}, f32[32,3,3]{1,2,0:T(4,128)}, u32[]{:S(2)}) copy-start(f32[32,3,3]{1,2,0:T(4,128)} %copy-done.30) | copy-start | bytes 3460
  (11 other events, 15.1 us)
Sparse Core Ops, SparseCore 0:
  141.7 63.0 all-reduce.2
  234.6 29.7 reduce-scatter.6
  268.0 76.3 reduce-scatter.8
where the time goes:
time: 358 us; the launch traced here: 355 us
  local copies, waits for them, and re-layouts  87 us (24%)
  waiting for transfers between devices  82.4 us (23%)
  matrix products  73.3 us (20%)
  blocking collectives  70.7 us (20%)
  other arithmetic  23.6 us (7%)
  between operations  17.6 us (5%)
    unnamed x4, waiting for transfers between devices  72.8 us
    all_gather x1, blocking collectives, on_device(): key_all = lax.all_gather(key_wire, 'row', axis=0, tiled=True)  26.4 us
    psum x1, blocking collectives, on_device(): totals = lax.psum((denominator, scalar_sum, value_sum, pair_sum), 'col')  23.6 us
    unnamed x124, local copies, waits for them, and re-layouts  22.2 us
    pmax x1, blocking collectives, on_device(): global_max = lax.pmax(row_max, 'col')  20.8 us
    dot_general x2, matrix products, on_device(): jnp.einsum('ihc,ijc->hij', grad_z_block, pair_tile, preferred_element_typ...  11.3 us
    psum x1, waiting for transfers between devices, on_device(): totals = lax.psum((denominator, scalar_sum, value_sum, pair_sum), 'col')  9.65 us
    dot_general x2, matrix products, on_device(): jnp.einsum('hij,ijc->ihc', rounded, pair_tile, preferred_element_type=jnp...  9.09 us
  transfers between devices with their start and end apart: 3, of which 2 were waited for; matrix products, arithmetic and copies ran while one was open for 18% of the time, Pallas kernels for 0%

commit v1 on v0

v1 whole, which is shorter than its diff:
```python
import functools
import math

import jax
import jax.numpy as jnp
import numpy as np
from jax import lax
from jax.experimental import pallas as pl
from jax.experimental.pallas import tpu as pltpu
from jax.sharding import PartitionSpec as P

H = 12
C = 16
PV = 8
PW = 128
BLK = 128
SW = 384
QR = 256
KR = 512
NRES = 4096
KEYB = 4
CAP = 2
F = 480
WS = 192
WP = 288
HJ = H * BLK
N_ROW = 16
N_COL = 8
OWN = 32
IB = 32
EMPTY = 8
NEG = -1e30
SC = 1.0 / math.sqrt(C)
WC = math.sqrt(2.0 / 72.0)
WL = math.sqrt(1.0 / 3.0)
F32 = jnp.float32
BF16 = jnp.bfloat16
VMEM_LIMIT = 56 * 1024 * 1024

NN = (((1,), (0,)), ((), ()))
NT = (((1,), (1,)), ((), ()))
TN = (((0,), (0,)), ((), ()))


def head_rows():
    f = np.arange(F)
    head = np.where(f < WS, f // C, ((f - WS) % (H * PV)) // PV)
    return (head[None, :] == np.arange(16)[:, None]).astype(np.float32)


def dot(a, b, dims=NN):
    return lax.dot_general(a, b, dims, preferred_element_type=F32)


def split3(x):
    hi = x.astype(BF16)
    rest = x - hi.astype(F32)
    mid = rest.astype(BF16)
    lo = (rest - mid.astype(F32)).astype(BF16)
    return hi, mid, lo


def rotate(x, frame, shift):
    parts = [x[:, 96 * b : 96 * b + 96] for b in range(3)]
    out = []
    for a in range(3):
        y = sum(frame[:, 3 * a + b : 3 * a + b + 1] * parts[b] for b in range(3))
        if shift:
            y = y + frame[:, 9 + a : 10 + a]
        out.append(y)
    return jnp.concatenate(out, axis=1)


def rotate_back(x, frame, shift):
    parts = [x[:, 96 * a : 96 * a + 96] for a in range(3)]
    if shift:
        parts = [parts[a] - frame[:, 9 + a : 10 + a] for a in range(3)]
    out = []
    for b in range(3):
        out.append(sum(frame[:, 3 * a + b : 3 * a + b + 1] * parts[a] for a in range(3)))
    return jnp.concatenate(out, axis=1)


def slot_of(codes_ref, s):
    code = codes_ref[s]
    listed = code < EMPTY
    safe = jnp.where(listed, code, 0)
    return listed, safe // KEYB, safe % KEYB


def rows_of(block):
    return pl.ds(pl.multiple_of(block * BLK, BLK), BLK)


def prep_kernel(pos_ref, q_ref, table_ref, index_ref, cot_ref, ow_ref, pwt_ref,
                qf_ref, df_ref, dzp_ref, frame_ref):
    row = pos_ref[0]
    col = pos_ref[1]
    ids = jnp.concatenate(
        [
            index_ref[:, pl.ds(pl.multiple_of(row * QR, QR), QR)],
            index_ref[:, pl.ds(pl.multiple_of(col * KR, KR), KR)],
        ],
        axis=1,
    )
    table = jnp.concatenate([table_ref[...], jnp.zeros((4, NRES), F32)], axis=0)
    table = jnp.concatenate(split3(table), axis=0)
    found = jnp.zeros((48, QR + KR), F32)
    step = 512
    for first in range(0, NRES, step):
        at = lax.broadcasted_iota(jnp.int32, (step, QR + KR), 0) + first
        hot = jnp.where(at == ids, 1.0, 0.0).astype(BF16)
        found = found + dot(table[:, first : first + step], hot)
    frame_t = found[0:16] + found[16:32] + found[32:48]
    frame_ref[...] = frame_t
    frame = jnp.transpose(frame_t[:, :QR])
    q = q_ref[...]
    gq = rotate(q[:, WS:].astype(F32), frame, True).astype(BF16)
    qf_ref[...] = jnp.concatenate([q[:, :WS], gq], axis=1)
    cot = cot_ref[...]
    head = dot(cot, ow_ref[0:F], NT).astype(BF16)
    gd = rotate(head[:, WS:].astype(F32), frame, False).astype(BF16)
    df_ref[...] = jnp.concatenate([head[:, :WS], gd], axis=1)
    tail = dot(cot, ow_ref[F:], NT).astype(BF16).astype(F32)
    pwt = pwt_ref[...].astype(F32)
    for h in range(H):
        dzp_ref[:, h, :] = jnp.broadcast_to(pwt[h : h + 1], (QR, PW))
        dzp_ref[:, H + h, :] = tail[:, h * PW : (h + 1) * PW]


def pair_in_kernel(codes_ref, pair_ref, dzp_ref, out_ref):
    _, qb, _ = slot_of(codes_ref, pl.program_id(0))
    first = qb * BLK + pl.program_id(1) * IB
    for i in range(IB):
        lhs = dzp_ref[first + i].astype(BF16)
        out_ref[0, :, i, :] = dot(lhs, pair_ref[0, i], NT)


def logit_kernel(codes_ref, keys_ref, frame_ref, qf_ref, df_ref, bz_ref, e_ref, gam_ref,
                 logit_ref, da_ref, kf_ref, vf_ref, stat_ref):
    e = e_ref[...]
    lane = lax.broadcasted_iota(jnp.int32, (BLK, BLK), 1)
    stats = []
    for s in range(CAP):
        listed, qb, kb = slot_of(codes_ref, s)
        raw = keys_ref[rows_of(kb), :]
        frame = jnp.transpose(frame_ref[:, pl.ds(pl.multiple_of(QR + kb * BLK, BLK), BLK)])
        spot = raw[:, 2 * WS :].astype(F32)
        gk = rotate(spot[:, :WP], frame, True).astype(BF16)
        gv = rotate(spot[:, WP:], frame, True).astype(BF16)
        kf = jnp.concatenate([raw[:, :WS], gk], axis=1)
        vf = jnp.concatenate([raw[:, WS : 2 * WS], gv], axis=1)
        kf_ref[s] = kf
        vf_ref[s] = vf
        qf = qf_ref[rows_of(qb), :]
        df = df_ref[rows_of(qb), :]
        qp = qf[:, WS:]
        ep = e[:, WS:]
        qsq = jnp.square(qp.astype(F32))
        ksq = jnp.square(gk.astype(F32))
        qhi = qsq.astype(BF16)
        qlo = (qsq - qhi.astype(F32)).astype(BF16)
        khi = ksq.astype(BF16)
        klo = (ksq - khi.astype(F32)).astype(BF16)
        qn = dot(qhi, ep, NT) + dot(qlo, ep, NT)
        kn = dot(ep, khi, NT) + dot(ep, klo, NT)
        held = jnp.zeros((BLK, BLK), F32)
        for h in range(H):
            eh = e[h : h + 1]
            kh = kf * eh
            vh = vf * eh
            scal = dot(qf[:, :WS], kh[:, :WS], NT)
            cross = dot(qp, kh[:, WS:], NT)
            dist = qn[:, h : h + 1] + kn[h : h + 1, :] - 2.0 * cross
            logit = (WL * SC) * scal + WL * bz_ref[s, h] - (0.5 * WL * WC) * gam_ref[h : h + 1] * dist
            da = bz_ref[s, H + h] + dot(df, vh, NT)
            logit_ref[s, h] = logit
            da_ref[s, h] = da
            top = jnp.max(logit, axis=1, keepdims=True)
            p = jnp.exp(logit - top)
            total = jnp.sum(p, axis=1, keepdims=True)
            mean = jnp.sum(p * da, axis=1, keepdims=True) / total
            held = jnp.where(lane == h, top + jnp.log(total), held)
            held = jnp.where(lane == 16 + h, mean, held)
        stats.append((listed, qb, jnp.transpose(held)))
    for b in range(2):
        lse = []
        for listed, qb, held in stats:
            lse.append(jnp.where(jnp.logical_and(listed, qb == b), held[0:16], NEG))
        top = jnp.maximum(lse[0], lse[1])
        w0 = jnp.exp(lse[0] - top)
        w1 = jnp.exp(lse[1] - top)
        total = w0 + w1
        stat_ref[0:16, b * BLK : (b + 1) * BLK] = top + jnp.log(total)
        stat_ref[16:32, b * BLK : (b + 1) * BLK] = (
            w0 * stats[0][2][16:32] + w1 * stats[1][2][16:32]
        ) / total


def out_kernel(codes_ref, pair_ref, logit_ref, vf_ref, stat_ref, e_ref, o_ref, p_ref, nz_ref, cat_ref, bd_ref):
    s = pl.program_id(0)
    step = pl.program_id(1)
    listed, qb, _ = slot_of(codes_ref, s)

    @pl.when(jnp.logical_and(s == 0, step == 0))
    def _():
        o_ref[...] = jnp.zeros_like(o_ref)

    @pl.when(step == 0)
    def _():
        lse = jnp.transpose(stat_ref[0:16, rows_of(qb)])
        lse = jnp.where(listed, lse, -NEG)
        vf = vf_ref[0]
        for h in range(H):
            p = jnp.exp(logit_ref[0, h] - lse[:, h : h + 1])
            p_ref[h] = p
            cat_ref[:, h * BLK : (h + 1) * BLK] = p.astype(BF16)
            bd_ref[h * BLK : (h + 1) * BLK, :] = vf * e_ref[h : h + 1, :]
        o_ref[rows_of(qb), 0:F] += dot(cat_ref[...], bd_ref[...])

    first = step * IB
    for i in range(IB):
        w = p_ref[:, first + i, :].astype(BF16)
        nz_ref[:, first + i, :] = dot(w, pair_ref[0, i])

    @pl.when(step == pl.num_programs(1) - 1)
    def _():
        for h in range(H):
            o_ref[rows_of(qb), 512 + h * PW : 512 + (h + 1) * PW] += nz_ref[h]


def back_kernel(codes_ref, all_ref, stat_ref, logit_ref, da_ref, kf_ref, vf_ref, qf_ref, df_ref, e_ref, gam_ref,
                o_ref, ga_ref, msg_ref, kg_ref, kg_acc, gcat, gstk, astk, kbd, qbd, dbd, ebd, dq_acc):
    top = all_ref[0, 0:16]
    for d in range(1, N_COL):
        top = jnp.maximum(top, all_ref[d, 0:16])
    total = jnp.zeros((16, QR), F32)
    mean = jnp.zeros((16, QR), F32)
    for d in range(N_COL):
        w = jnp.exp(all_ref[d, 0:16] - top)
        total = total + w
        mean = mean + w * all_ref[d, 16:32]
    lse = top + jnp.log(total)
    delta = mean / total
    alpha = jnp.transpose(jnp.exp(stat_ref[0:16] - lse))
    both = jnp.transpose(jnp.concatenate([lse, delta], axis=0))
    e = e_ref[...]
    ahi = alpha.astype(BF16)
    alo = (alpha - ahi.astype(F32)).astype(BF16)
    spread = dot(ahi, e) + dot(alo, e)
    msg_ref[:, 0:F] = (o_ref[:, 0:F] * spread).astype(BF16)
    for h in range(H):
        msg_ref[:, 512 + h * PW : 512 + (h + 1) * PW] = (
            o_ref[:, 512 + h * PW : 512 + (h + 1) * PW] * alpha[:, h : h + 1]
        ).astype(BF16)
    gam_f = jnp.sum(e.astype(F32) * gam_ref[:, 0:1], axis=0, keepdims=True)
    point = lax.broadcasted_iota(jnp.int32, (1, F), 1) >= WS
    fa = jnp.where(point, WC * gam_f, SC)
    fb = jnp.where(point, -WC * gam_f, 0.0)
    kg_acc[...] = jnp.zeros_like(kg_acc)
    dq_acc[...] = jnp.zeros_like(dq_acc)
    for h in range(H):
        ebd[h * BLK : (h + 1) * BLK, :] = jnp.broadcast_to(e[h : h + 1], (BLK, F))
    for s in range(CAP):
        listed, qb, kb = slot_of(codes_ref, s)
        stat_ref_b = jnp.where(qb == 0, both[0:BLK], both[BLK:])
        kf = kf_ref[s]
        vf = vf_ref[s]
        qf = qf_ref[rows_of(qb), :]
        df = df_ref[rows_of(qb), :]
        for h in range(H):
            block = slice(h * BLK, (h + 1) * BLK)
            a = jnp.exp(logit_ref[s, h] - jnp.where(listed, stat_ref_b[:, h : h + 1], -NEG))
            g = WL * a * (da_ref[s, h] - stat_ref_b[:, 16 + h : 17 + h])
            gr = g.astype(BF16)
            ar = a.astype(BF16)
            ga_ref[s, h] = g
            ga_ref[s, H + h] = a
            gcat[:, block] = gr
            gstk[block, :] = gr
            astk[block, :] = ar
            eh = e[h : h + 1]
            kbd[block, :] = kf * eh
            qbd[block, :] = qf * eh
            dbd[block, :] = df * eh
        dq_raw = dot(gcat[...], kbd[...])
        row_sum = dot(gcat[...], ebd[...])
        dq_acc[rows_of(qb), :] += fa * dq_raw + fb * row_sum * qf.astype(F32)
        dk_raw = dot(gstk[...], qbd[...], TN)
        col_sum = dot(gstk[...], ebd[...], TN)
        kg_acc[rows_of(kb), 0:F] += fa * dk_raw + fb * col_sum * kf.astype(F32)
        kg_acc[rows_of(kb), 512 : 512 + F] += dot(astk[...], dbd[...], TN)
    kg_ref[...] = kg_acc[...].astype(BF16)
    msg_ref[:, 2048 : 2048 + F] = dq_acc[...].astype(BF16)


def pair_out_kernel(codes_ref, ga_ref, dzp_ref, out_ref):
    _, qb, _ = slot_of(codes_ref, pl.program_id(0))
    first = qb * BLK + pl.program_id(1) * IB
    for i in range(IB):
        lhs = ga_ref[0, :, i, :].astype(BF16)
        rhs = dzp_ref[first + i].astype(BF16)
        out_ref[0, i] = dot(lhs, rhs, TN).astype(BF16)


def final_kernel(pos_ref, kg_ref, msg_ref, frame_ref, ow_ref, up_ref, gq_ref, gk_ref):
    row = pos_ref[0]
    col = pos_ref[1]
    total = kg_ref[0].astype(F32)
    for d in range(1, N_ROW):
        total = total + kg_ref[d].astype(F32)
    frames = jnp.transpose(frame_ref[...])
    frame_ref_rows = frames
    del frame_ref_rows
    pick_q = lax.broadcasted_iota(jnp.int32, (OWN, QR + KR), 1) == (
        lax.broadcasted_iota(jnp.int32, (OWN, QR + KR), 0) + col * OWN
    )
    pick_k = lax.broadcasted_iota(jnp.int32, (OWN, QR + KR), 1) == (
        lax.broadcasted_iota(jnp.int32, (OWN, QR + KR), 0) + QR + row * OWN
    )
    pick = jnp.concatenate([pick_q, pick_k], axis=0).astype(F32).astype(BF16)
    hi, mid, lo = split3(frame_ref[...])
    own = dot(pick, hi, NT) + dot(pick, mid, NT) + dot(pick, lo, NT)
    fq = own[0:OWN]
    fk = own[OWN:]
    dgk = rotate_back(total[:, WS:F], fk, False)
    dgv = rotate_back(total[:, 512 + WS : 512 + F], fk, False)
    gk_ref[...] = jnp.concatenate([total[:, 0:WS], total[:, 512 : 512 + WS], dgk, dgv], axis=1).astype(BF16)
    msg = msg_ref[0].astype(F32)
    for d in range(1, N_COL):
        msg = msg + msg_ref[d].astype(F32)
    local = rotate_back(msg[:, WS:F], fq, True)
    head = jnp.concatenate([msg[:, 0:WS], local], axis=1).astype(BF16)
    tail = msg[:, 512:2048].astype(BF16)
    up_ref[...] = (dot(head, ow_ref[0:F]) + dot(tail, ow_ref[F:])).astype(BF16)
    dgq = rotate_back(msg[:, 2048 + WS : 2048 + F], fq, False)
    gq_ref[...] = jnp.concatenate([msg[:, 2048 : 2048 + WS], dgq], axis=1).astype(BF16)


SMEM = pl.BlockSpec(memory_space=pltpu.SMEM)
FULL = pl.BlockSpec(memory_space=pltpu.VMEM)


def params(**more):
    return pltpu.CompilerParams(vmem_limit_bytes=VMEM_LIMIT, **more)


def shape(dims, kind):
    return jax.ShapeDtypeStruct(dims, kind)


def on_device(queries, keys, frame_table, frame_index, pair_list, pair, pair_weight, point_weight, out_weight, cotangent):
    row = lax.axis_index("row")
    col = lax.axis_index("col")
    pos = jnp.stack([row, col]).astype(jnp.int32)
    codes = pair_list.reshape(CAP)
    tiles = pair.reshape(CAP, BLK, BLK, PW)
    e = jnp.asarray(head_rows(), BF16)
    gam = jnp.broadcast_to(jnp.pad(jax.nn.softplus(point_weight), (0, 4))[:, None], (16, BLK))

    key_wire = jnp.broadcast_to(keys[None], (N_ROW, OWN, 2 * F))
    key_all = lax.all_to_all(key_wire, "row", split_axis=0, concat_axis=0).reshape(KR, 2 * F)

    qf, df, dzp, frame = pl.pallas_call(
        prep_kernel,
        name="prep",
        in_specs=[SMEM] + [FULL] * 6,
        out_specs=[FULL] * 4,
        out_shape=[shape((QR, F), BF16), shape((QR, F), BF16), shape((QR, 2 * H, PW), F32), shape((16, QR + KR), F32)],
        compiler_params=params(),
        cost_estimate=pl.CostEstimate(flops=2 * QR * SW * 2016, bytes_accessed=6_000_000, transcendentals=0),
    )(pos, queries, frame_table, frame_index.reshape(1, NRES), cotangent, out_weight, pair_weight.T)

    grid = (CAP, BLK // IB)
    tile_spec = pl.BlockSpec((1, IB, BLK, PW), lambda s, i: (s, i, 0, 0))
    bz = pl.pallas_call(
        pair_in_kernel,
        name="pair_in",
        grid=grid,
        in_specs=[SMEM, tile_spec, FULL],
        out_specs=pl.BlockSpec((1, 2 * H, IB, BLK), lambda s, i: (s, 0, i, 0)),
        out_shape=shape((CAP, 2 * H, BLK, BLK), F32),
        compiler_params=params(),
        cost_estimate=pl.CostEstimate(flops=2 * CAP * BLK * BLK * PW * 32, bytes_accessed=14_000_000, transcendentals=0),
    )(codes, tiles, dzp)

    planes = (CAP, H, BLK, BLK)
    logit, da, kf, vf, stat = pl.pallas_call(
        logit_kernel,
        name="logit",
        in_specs=[SMEM] + [FULL] * 7,
        out_specs=[FULL] * 5,
        out_shape=[
            shape(planes, F32),
            shape(planes, F32),
            shape((CAP, BLK, F), BF16),
            shape((CAP, BLK, F), BF16),
            shape((32, QR), F32),
        ],
        compiler_params=params(),
    )(codes, key_all, frame, qf, df, bz, e, gam)

    stat_all = lax.all_to_all(jnp.broadcast_to(stat[None], (N_COL, 32, QR)), "col", split_axis=0, concat_axis=0)

    out = pl.pallas_call(
        out_kernel,
        name="local_out",
        grid=grid,
        in_specs=[
            SMEM,
            tile_spec,
            pl.BlockSpec((1, H, BLK, BLK), lambda s, i: (s, 0, 0, 0)),
            pl.BlockSpec((1, BLK, F), lambda s, i: (s, 0, 0)),
            FULL,
            FULL,
        ],
        out_specs=pl.BlockSpec((QR, 2048), lambda s, i: (0, 0)),
        out_shape=shape((QR, 2048), F32),
        scratch_shapes=[
            pltpu.VMEM((H, BLK, BLK), F32),
            pltpu.VMEM((H, BLK, PW), F32),
            pltpu.VMEM((BLK, HJ), BF16),
            pltpu.VMEM((HJ, F), BF16),
        ],
        compiler_params=params(),
        cost_estimate=pl.CostEstimate(flops=2 * CAP * BLK * BLK * PW * 32, bytes_accessed=14_000_000, transcendentals=0),
    )(codes, tiles, logit, vf, stat, e)

    ga, msg, kg = pl.pallas_call(
        back_kernel,
        name="back",
        in_specs=[SMEM] + [FULL] * 11,
        out_specs=[FULL] * 3,
        out_shape=[
            shape((CAP, 2 * H, BLK, BLK), F32),
            shape((QR, 2560), BF16),
            shape((KR, 1024), BF16),
        ],
        scratch_shapes=[
            pltpu.VMEM((KR, 1024), F32),
            pltpu.VMEM((BLK, HJ), BF16),
            pltpu.VMEM((HJ, BLK), BF16),
            pltpu.VMEM((HJ, BLK), BF16),
            pltpu.VMEM((HJ, F), BF16),
            pltpu.VMEM((HJ, F), BF16),
            pltpu.VMEM((HJ, F), BF16),
            pltpu.VMEM((HJ, F), BF16),
            pltpu.VMEM((QR, F), F32),
        ],
        compiler_params=params(),
    )(codes, stat_all, stat, logit, da, kf, vf, qf, df, e, gam, out)

    kg_all = lax.all_to_all(kg.reshape(N_ROW, OWN, 1024), "row", split_axis=0, concat_axis=0)
    msg_all = lax.all_to_all(msg.reshape(N_COL, OWN, 2560), "col", split_axis=0, concat_axis=0)

    grad_tiles = pl.pallas_call(
        pair_out_kernel,
        name="pair_out",
        grid=grid,
        in_specs=[SMEM, pl.BlockSpec((1, 2 * H, IB, BLK), lambda s, i: (s, 0, i, 0)), FULL],
        out_specs=tile_spec,
        out_shape=shape((CAP, BLK, BLK, PW), BF16),
        compiler_params=params(),
        cost_estimate=pl.CostEstimate(flops=2 * CAP * BLK * BLK * PW * 32, bytes_accessed=14_000_000, transcendentals=0),
    )(codes, ga, dzp)

    update, grad_queries, grad_keys = pl.pallas_call(
        final_kernel,
        name="final",
        in_specs=[SMEM] + [FULL] * 4,
        out_specs=[FULL] * 3,
        out_shape=[shape((OWN, SW), BF16), shape((OWN, F), BF16), shape((OWN, 2 * F), BF16)],
        compiler_params=params(),
    )(pos, kg_all, msg_all, frame, out_weight)
    return update, grad_queries, grad_keys, grad_tiles.reshape(pair.shape)


def solution(mesh):
    in_specs = (
        P("row", None),
        P(("col", "row"), None),
        P(),
        P(),
        P("row", "col", None),
        P("row", "col", None, None, None, None),
        P(),
        P(),
        P(),
        P("row", None),
    )
    out_specs = (
        P(("row", "col"), None),
        P(("row", "col"), None),
        P(("col", "row"), None),
        P("row", "col", None, None, None, None),
    )
    return jax.shard_map(on_device, mesh=mesh, in_specs=in_specs, out_specs=out_specs, check_vma=False)
```

time: 358 us -> 127 us (0.35)
  the two profiles are of different devices: /device:TPU:2 before, /device:TPU:1 now
where the time goes in v1:
time: 127 us; the launch traced here: 126 us
  Pallas kernels  66.5 us (52%)
  blocking collectives  23.8 us (19%)
  starting transfers between devices  19.8 us (16%)
  local copies, waits for them, and re-layouts  7.11 us (6%)
  waiting for transfers between devices  7.11 us (6%)
    all_to_all x1, blocking collectives, on_device(): lax.all_to_all(kg.reshape(N_ROW, OWN, 1024), 'row', split_axis=0, concat_...  23.8 us
    pallas_call x1, Pallas kernels, on_device(): pl.pallas_call(logit_kernel, name='logit', in_specs=[SMEM] + [FULL] * 7,...  14.6 us
    pallas_call x1, Pallas kernels, on_device(): pl.pallas_call(pair_in_kernel, name='pair_in', grid=grid, in_specs=[SMEM,...  11 us
    pallas_call x1, Pallas kernels, on_device(): pl.pallas_call(pair_out_kernel, name='pair_out', grid=grid, in_specs=[SME...  10.8 us
    pallas_call x1, Pallas kernels, on_device(): pl.pallas_call(out_kernel, name='local_out', grid=grid, in_specs=[SMEM, t...  10.7 us
    all_to_all x1, starting transfers between devices, on_device(): lax.all_to_all(key_wire, 'row', split_axis=0, concat_axis=0)  8.6 us
    pallas_call x1, Pallas kernels, on_device(): pl.pallas_call(back_kernel, name='back', in_specs=[SMEM] + [FULL] * 11, o...  8.58 us
    pallas_call x1, Pallas kernels, on_device(): pl.pallas_call(prep_kernel, name='prep', in_specs=[SMEM] + [FULL] * 6, ou...  7.23 us
  transfers between devices with their start and end apart: 3, of which 1 were waited for; matrix products, arithmetic and copies ran while one was open for 1% of the time, Pallas kernels for 32%

profile of v1, /device:TPU:1, one launch (start us, length us, event | category | flops | bytes accessed | tf_op | source)
XLA Modules:
  0.0 125.7 jit_solution(13192368035681822417)
XLA Ops:
  0.6 0.0 copy-start.3
  0.6 0.0 copy-start.4
  0.7 2.0 %broadcast_in_dim.6 = bf16[16,32,960]{2,1,0:T(8,128)(2,1)} broadcast(bf16[32,960]{1,0:T(8,128)(2,1)} %param.12), dimensions={1,2} | broadcast | bytes 1044480 | tf_op jit(solution)/shard_map/broadcast_in_dim | solution.py:361
  2.6 8.6 %all-to-all-start = ((bf16[16,32,960]{2,1,0:T(8,128)(2,1)}), bf16[16,32,960]{2,1,0:T(8,128)(2,1)S(1)}, u32[]{:S(2)}, u32[]{:S(2)}) async-start(bf16[16,32,960]{2,1,0:T(8,128)(2,1)} %broadcast_in_dim.6), calls=%async_computation | async-start | bytes 2097152 | tf_op jit(solution)/shard_map/all_to_all | solution.py:362
  11.3 0.0 copy-done.3
  11.3 0.8 copy.15.q_ref
  12.1 0.0 copy-done.4
  12.1 0.6 pad_add_fusion.pos_ref
  12.8 7.2 %prep.1 = (bf16[256,480]{1,0:T(8,128)(2,1)}, bf16[256,480]{1,0:T(8,128)(2,1)}, f32[256,24,128]{2,1,0:T(8,128)}, f32[16,768]{1,0:T(8,128)}) custom-call(s32[2]{0:T(128)} %pad_add_fusion.pos_ref, bf16[256,480]{1,0:T(8,128)(2,1)} %copy.15.q_ref, f32[12,4096]{1,0:T(8,128)} %table_ref.1, s32[1,4096]{1,0:T(1,128)} %bitcast.15, bf16[256,384]{1,0:T(8,128)(2,1)} %cot_ref.1, ...), custom_call_target="tpu_custom_call" | custom-call | flops 396361728 | bytes 6000000 | tf_op jit(solution)/shard_map/prep/pallas_call | solution.py:364
  20.0 11.0 %pair_in.1.bz_ref = f32[2,24,128,128]{3,2,1,0:T(8,128)} custom-call(s32[2]{0:T(128)} %bitcast.16, bf16[2,128,128,128]{3,2,1,0:T(8,128)(2,1)} %bitcast.10, f32[256,24,128]{2,1,0:T(8,128)} %get-tuple-element.22.dzp_ref), custom_call_target="tpu_custom_call" | custom-call | flops 268435456 | bytes 14000000 | tf_op jit(solution)/shard_map/pair_in/pallas_call | solution.py:376
  31.0 0.0 all-to-all-done
  31.0 0.0 copy-start.1
  31.0 0.7 broadcast_in_dim.7.gam_ref
  31.7 0.2 copy-done.1
  32.0 14.6 %logit.1 = (f32[2,12,128,128]{3,2,1,0:T(8,128)}, f32[2,12,128,128]{3,2,1,0:T(8,128)}, bf16[2,128,480]{2,1,0:T(8,128)(2,1)}, bf16[2,128,480]{2,1,0:T(8,128)(2,1)}, f32[32,256]{1,0:T(8,128)}) custom-call(s32[2]{0:T(128)} %bitcast.17, bf16[512,960]{1,0:T(8,128)(2,1)} %bitcast.13, f32[16,768]{1,0:T(8,128)} %get-tuple-element.19.frame_ref, ...), custom_call_target="tpu_custom_call" | custom-call | tf_op jit(solution)/shard_map/logit/pallas_call | solution.py:388
  46.5 1.5 %broadcast_in_dim.8 = f32[8,32,256]{2,1,0:T(8,128)} broadcast(f32[32,256]{1,0:T(8,128)} %get-tuple-element.23.stat_ref), dimensions={1,2} | broadcast | bytes 294912 | tf_op jit(solution)/shard_map/broadcast_in_dim | solution.py:403
  48.0 5.4 %all-to-all-start.1 = ((f32[8,32,256]{2,1,0:T(8,128)}), f32[8,32,256]{2,1,0:T(8,128)S(1)}, u32[]{:S(2)}, u32[]{:S(2)}) async-start(f32[8,32,256]{2,1,0:T(8,128)} %broadcast_in_dim.8), calls=%async_computation.1 | async-start | bytes 524288 | tf_op jit(solution)/shard_map/all_to_all | solution.py:403
  53.4 10.7 %local_out.1.o_ref = f32[256,2048]{1,0:T(8,128)} custom-call(s32[2]{0:T(128)} %bitcast.18, bf16[2,128,128,128]{3,2,1,0:T(8,128)(2,1)} %bitcast.11, f32[2,12,128,128]{3,2,1,0:T(8,128)} %get-tuple-element.24.logit_ref, bf16[2,128,480]{2,1,0:T(8,128)(2,1)} %get-tuple-element.27.vf_ref, f32[32,256]{1,0:T(8,128)} %get-tuple-element.23.stat_ref, ...), custom_call_target="tpu_custom_call" | custom-call | flops 268435456 | bytes 14000000 | tf_op jit(solution)/shard_map/local_out/pallas_call | solution.py:405
  64.2 0.0 all-to-all-done.1.all_ref
  64.2 0.0 copy-start.2
  64.2 0.7 copy-done.2
  64.9 8.6 %back.1 = (f32[2,24,128,128]{3,2,1,0:T(8,128)}, bf16[256,2560]{1,0:T(8,128)(2,1)}, bf16[512,1024]{1,0:T(8,128)(2,1)}) custom-call(s32[2]{0:T(128)} %bitcast.19, f32[8,32,256]{2,1,0:T(8,128)} %copy-done.2, f32[32,256]{1,0:T(8,128)} %get-tuple-element.23.stat_ref, f32[2,12,128,128]{3,2,1,0:T(8,128)} %get-tuple-element.24.logit_ref, ...), custom_call_target="tpu_custom_call" | custom-call | tf_op jit(solution)/shard_map/back/pallas_call | solution.py:429
  73.5 23.8 %all_to_all.20.kg_ref = bf16[16,32,1024]{2,1,0:T(8,128)(2,1)} all-to-all(bf16[16,32,1024]{2,1,0:T(8,128)(2,1)} %bitcast.14), channel_id=1, replica_groups=mesh['row'=16,'col'=8] {'row'}, dimensions={0} | all-to-all | bytes 2097152 | tf_op jit(solution)/shard_map/all_to_all | solution.py:453
  97.3 5.8 %all-to-all-start.3 = ((bf16[8,32,2560]{2,1,0:T(8,128)(2,1)}), bf16[8,32,2560]{2,1,0:T(8,128)(2,1)S(1)}, u32[]{:S(2)}, u32[]{:S(2)}) async-start(bf16[8,32,2560]{2,1,0:T(8,128)(2,1)} %bitcast.8), calls=%async_computation.3 | async-start | bytes 2621440 | tf_op jit(solution)/shard_map/all_to_all | solution.py:454
  103.1 10.8 %pair_out.1 = bf16[2,128,128,128]{3,2,1,0:T(8,128)(2,1)} custom-call(s32[2]{0:T(128)} %bitcast.20, f32[2,24,128,128]{3,2,1,0:T(8,128)} %get-tuple-element.33.ga_ref, f32[256,24,128]{2,1,0:T(8,128)} %get-tuple-element.22.dzp_ref), custom_call_target="tpu_custom_call" | custom-call | flops 268435456 | bytes 14000000 | tf_op jit(solution)/shard_map/pair_out/pallas_call | solution.py:456
  113.9 7.1 %all-to-all-done.3.msg_ref = bf16[8,32,2560]{2,1,0:T(8,128)(2,1)S(1)} async-done(((bf16[8,32,2560]{2,1,0:T(8,128)(2,1)}), bf16[8,32,2560]{2,1,0:T(8,128)(2,1)S(1)}, u32[]{:S(2)}, u32[]{:S(2)}) %all-to-all-start.3) | async-done | bytes 1310752 | tf_op jit(solution)/shard_map/all_to_all | solution.py:454
  121.0 0.0 copy-start
  121.0 1.1 copy-done
  122.1 3.6 %final.1 = (bf16[32,384]{1,0:T(8,128)(2,1)}, bf16[32,480]{1,0:T(8,128)(2,1)}, bf16[32,960]{1,0:T(8,128)(2,1)}) custom-call(s32[2]{0:T(128)} %pad_add_fusion.pos_ref, bf16[16,32,1024]{2,1,0:T(8,128)(2,1)} %all_to_all.20.kg_ref, bf16[8,32,2560]{2,1,0:T(8,128)(2,1)} %copy-done, f32[16,768]{1,0:T(8,128)} %get-tuple-element.19.frame_ref, bf16[2016,384]{1,0:T(8,128)(2,1)} %ow_ref.3), custom_call_target="tpu_custom_call" | custom-call | tf_op jit(solution)/shard_map/final/pallas_call | solution.py:467
  (2 shorter events, 0.0 us)
Async XLA Ops:
  0.6 10.6 %copy-start.3 = (bf16[256,480]{0,1:T(8,128)(2,1)S(1)}, bf16[256,480]{0,1:T(8,128)(2,1)}, u32[]{:S(2)}) copy-start(bf16[256,480]{0,1:T(8,128)(2,1)} %param.11) | copy-start | bytes 737284
  0.6 11.5 %copy-start.4 = (f32[12]{0:T(128)S(1)}, f32[12]{0:T(128)}, u32[]{:S(2)}) copy-start(f32[12]{0:T(128)} %param.18) | copy-start | bytes 148
  2.6 28.3 %all-to-all-start = ((bf16[16,32,960]{2,1,0:T(8,128)(2,1)}), bf16[16,32,960]{2,1,0:T(8,128)(2,1)S(1)}, u32[]{:S(2)}, u32[]{:S(2)}) async-start(bf16[16,32,960]{2,1,0:T(8,128)(2,1)} %broadcast_in_dim.6), calls=%async_computation | async-start | bytes 2097152 | tf_op jit(solution)/shard_map/all_to_all | solution.py:362
  31.0 1.0 copy-start.1
  48.0 16.2 %all-to-all-start.1 = ((f32[8,32,256]{2,1,0:T(8,128)}), f32[8,32,256]{2,1,0:T(8,128)S(1)}, u32[]{:S(2)}, u32[]{:S(2)}) async-start(f32[8,32,256]{2,1,0:T(8,128)} %broadcast_in_dim.8), calls=%async_computation.1 | async-start | bytes 524288 | tf_op jit(solution)/shard_map/all_to_all | solution.py:403
  64.2 0.7 copy-start.2
  97.3 23.7 %all-to-all-start.3 = ((bf16[8,32,2560]{2,1,0:T(8,128)(2,1)}), bf16[8,32,2560]{2,1,0:T(8,128)(2,1)S(1)}, u32[]{:S(2)}, u32[]{:S(2)}) async-start(bf16[8,32,2560]{2,1,0:T(8,128)(2,1)} %bitcast.8), calls=%async_computation.3 | async-start | bytes 2621440 | tf_op jit(solution)/shard_map/all_to_all | solution.py:454
  121.0 1.1 copy-start

commit v2 on v1

v2 whole, which is shorter than its diff:
```python
import functools
import math

import jax
import jax.numpy as jnp
import numpy as np
from jax import lax
from jax.experimental import pallas as pl
from jax.experimental.pallas import tpu as pltpu
from jax.sharding import PartitionSpec as P

H = 12
C = 16
PV = 8
PW = 128
BLK = 128
SW = 384
QR = 256
KR = 512
NRES = 4096
KEYB = 4
CAP = 2
F = 480
WS = 192
WP = 288
HJ = H * BLK
GJ = 6 * BLK
N_ROW = 16
N_COL = 8
OWN = 32
EMPTY = 8
NEG = -1e30
SC = 1.0 / math.sqrt(C)
WC = math.sqrt(2.0 / 72.0)
WL = math.sqrt(1.0 / 3.0)
F32 = jnp.float32
BF16 = jnp.bfloat16
MB = 1024 * 1024
G = 2
GH = 6
GF = 256
FG = G * GF
CHUNK = 32

NN = (((1,), (0,)), ((), ()))
NT = (((1,), (1,)), ((), ()))
TN = (((0,), (0,)), ((), ()))


def head_rows():
    f = np.arange(FG)
    group, at = f // GF, f % GF
    head = np.where(at < 96, at // C, ((at - 96) % 48) // PV) + GH * group
    mine = (head[None, :] == np.arange(16)[:, None]) & (at < 240)[None, :]
    scalar, point = mine & (at < 96)[None, :], mine & (at >= 96)[None, :]
    return np.concatenate([scalar, point, mine], axis=0).astype(np.float32)


def dot(a, b, dims=NN):
    return lax.dot_general(a, b, dims, preferred_element_type=F32)


def split3(x):
    hi = x.astype(BF16)
    rest = x - hi.astype(F32)
    mid = rest.astype(BF16)
    lo = (rest - mid.astype(F32)).astype(BF16)
    return hi, mid, lo


def split2(x):
    hi = x.astype(BF16)
    return hi, (x - hi.astype(F32)).astype(BF16)


def rotate(parts, frame, shift):
    out = []
    for a in range(3):
        y = sum(frame[:, 3 * a + b : 3 * a + b + 1] * parts[b] for b in range(3))
        if shift:
            y = y + frame[:, 9 + a : 10 + a]
        out.append(y)
    return out


def rotate_back(parts, frame, shift):
    if shift:
        parts = [parts[a] - frame[:, 9 + a : 10 + a] for a in range(3)]
    return [sum(frame[:, 3 * a + b : 3 * a + b + 1] * parts[a] for a in range(3)) for b in range(3)]


def components(x):
    return [x[:, 96 * b : 96 * b + 96] for b in range(3)]


def grouped(scalar, parts):
    pad = jnp.zeros((scalar.shape[0], 16), F32)
    pieces = []
    for g in range(G):
        pieces.append(scalar[:, 96 * g : 96 * g + 96])
        pieces.extend(part[:, 48 * g : 48 * g + 48] for part in parts)
        pieces.append(pad)
    return jnp.concatenate(pieces, axis=1).astype(BF16)


def ungrouped(x):
    scalar = jnp.concatenate([x[:, GF * g : GF * g + 96] for g in range(G)], axis=1)
    parts = []
    for a in range(3):
        first = 96 + 48 * a
        parts.append(jnp.concatenate([x[:, GF * g + first : GF * g + first + 48] for g in range(G)], axis=1))
    return scalar, parts


def slot_of(codes_ref, s):
    code = codes_ref[s]
    listed = code < EMPTY
    safe = jnp.where(listed, code, 0)
    return listed, safe // KEYB, safe % KEYB


def rows_of(block):
    return pl.ds(pl.multiple_of(block * BLK, BLK), BLK)


def fetch(refs, held, sems, first=0):
    copies = [pltpu.make_async_copy(ref, buf, sems.at[first + n]) for n, (ref, buf) in enumerate(zip(refs, held))]
    for copy in copies:
        copy.start()
    return copies


def look_up(table_ref, ids):
    count = ids.shape[1]
    found = jnp.zeros((48, count), F32)
    step = 512
    pad = jnp.zeros((4, step), F32)
    for first in range(0, NRES, step):
        table = jnp.concatenate([table_ref[:, first : first + step], pad], axis=0)
        table = jnp.concatenate(split3(table), axis=0)
        at = lax.broadcasted_iota(jnp.int32, (step, count), 0) + first
        found = found + dot(table, jnp.where(at == ids, 1.0, 0.0).astype(BF16))
    return found[0:16] + found[16:32] + found[32:48]


def key_kernel(keys_hbm, table_hbm, index_hbm, wire_hbm, frame_ref, held_ref, keys_ref, table_ref, index_ref, wire_ref, sems):
    copies = fetch((keys_hbm, table_hbm, index_hbm), (keys_ref, table_ref, index_ref), sems)
    for copy in copies:
        copy.wait()
    at = lax.axis_index("col") * N_ROW + lax.axis_index("row")
    window = at // 4
    ids = index_ref[:, pl.ds(pl.multiple_of(window * BLK, BLK), BLK)]
    held_ref[...] = jnp.transpose(jnp.concatenate([look_up(table_ref, ids), jnp.zeros((112, BLK), F32)], axis=0))
    frame = held_ref[pl.ds(pl.multiple_of((at % 4) * OWN, OWN), OWN), :]
    frame_ref[...] = frame
    keys = keys_ref[...].astype(F32)
    gk = rotate(components(keys[:, 2 * WS : 2 * WS + WP]), frame, True)
    gv = rotate(components(keys[:, 2 * WS + WP :]), frame, True)
    wire = jnp.concatenate([grouped(keys[:, :WS], gk), grouped(keys[:, WS : 2 * WS], gv)], axis=1)
    wire_ref[...] = wire
    copies = [pltpu.make_async_copy(wire_ref, wire_hbm.at[d], sems.at[3 + d]) for d in range(N_ROW)]
    for copy in copies:
        copy.start()
    for copy in copies:
        copy.wait()


def pair_copy(pair_ref, held, sems, k):
    rows = pl.ds(k * CHUNK, CHUNK)
    return pltpu.make_async_copy(pair_ref.at[rows], held.at[rows], sems.at[k])


CHUNKS = CAP * BLK // CHUNK


def prep_kernel(codes_ref, q_hbm, pw_hbm, gam_hbm, table_hbm, index_hbm, cot_hbm, ow_hbm, pair_ref,
                qf_hbm, df_hbm, frame_hbm, gamma_hbm, dzp_hbm, bz_hbm,
                held, sems, table_ref, index_ref, gam_ref, q_ref, cot_ref, ow_ref, pw_ref, more,
                qf_ref, df_ref, frame_ref, gamma_ref, dzp_ref, bz_ref, outs):
    loads = fetch((table_hbm, index_hbm, gam_hbm, q_hbm, cot_hbm, ow_hbm, pw_hbm),
                  (table_ref, index_ref, gam_ref, q_ref, cot_ref, ow_ref, pw_ref), more)
    for k in range(CHUNKS):
        pair_copy(pair_ref, held, sems, k).start()
    row = lax.axis_index("row")
    for copy in loads[:3]:
        copy.wait()
    frame_t = look_up(table_ref, index_ref[:, pl.ds(pl.multiple_of(row * QR, QR), QR)])
    frame = jnp.transpose(jnp.concatenate([frame_t, jnp.zeros((112, QR), F32)], axis=0))
    frame_ref[...] = frame
    raw = gam_ref[...]
    soft = jnp.maximum(raw, 0.0) + jnp.log(1.0 + jnp.exp(-jnp.abs(raw)))
    diag = lax.broadcasted_iota(jnp.int32, (16, H), 0) == lax.broadcasted_iota(jnp.int32, (16, H), 1)
    gamma_ref[...] = jnp.broadcast_to(jnp.sum(jnp.where(diag, soft, 0.0), axis=1, keepdims=True), (16, BLK))
    for copy in loads[3:]:
        copy.wait()
    q = jnp.transpose(q_ref[...].astype(F32))
    qf_ref[...] = grouped(q[:, :WS], rotate(components(q[:, WS:]), frame, True))
    cot = cot_ref[...]
    head = dot(cot, ow_ref[0:F], NT).astype(BF16).astype(F32)
    df_ref[...] = grouped(head[:, :WS], rotate(components(head[:, WS:]), frame, False))
    tail = dot(cot, ow_ref[F:], NT).astype(BF16).astype(F32)
    pwt = pw_ref[...].astype(F32)
    for h in range(H):
        dzp_ref[:, h, :] = jnp.broadcast_to(pwt[h : h + 1], (QR, PW))
        dzp_ref[:, H + h, :] = tail[:, h * PW : (h + 1) * PW]
    stores = fetch((qf_ref, df_ref, frame_ref, gamma_ref, dzp_ref), (qf_hbm, df_hbm, frame_hbm, gamma_hbm, dzp_hbm), outs, CHUNKS)

    def bz_copy(s, k):
        rows = pl.ds(k * CHUNK, CHUNK)
        return pltpu.make_async_copy(bz_ref.at[s, :, rows], bz_hbm.at[s, :, rows], outs.at[s * (BLK // CHUNK) + k])

    for s in range(CAP):
        _, qb, _ = slot_of(codes_ref, s)

        def some(k, carry, s=s, qb=qb):
            @pl.when(k % (CHUNK // 16) == 0)
            def _():
                rows = pl.ds(pl.multiple_of(s * BLK + k * 16, 16), CHUNK)
                pltpu.make_async_copy(pair_ref.at[rows], held.at[rows], sems.at[s * (BLK // CHUNK) + k // (CHUNK // 16)]).wait()

            first = k * 16
            for i in range(0, 16, 2):
                lhs = dzp_ref[pl.ds(qb * BLK + first + i, 2)].reshape(4 * H, PW).astype(BF16)
                z = held[pl.ds(s * BLK + first + i, 2)].reshape(2 * BLK, PW)
                found = dot(lhs, z, NT)
                bz_ref[s, :, first + i, :] = found[0 : 2 * H, 0:BLK]
                bz_ref[s, :, first + i + 1, :] = found[2 * H :, BLK:]

            @pl.when(k % (CHUNK // 16) == CHUNK // 16 - 1)
            def _():
                bz_copy(s, k // (CHUNK // 16)).start()

            return carry

        lax.fori_loop(0, BLK // 16, some, 0)
    for copy in stores:
        copy.wait()
    for s in range(CAP):
        for k in range(BLK // CHUNK):
            bz_copy(s, k).wait()


def logit_kernel(codes_ref, keys_hbm, qf_hbm, df_hbm, e_hbm, gam_hbm, bz_hbm, mine_hbm, logit_hbm, da_hbm, stat_hbm,
                 keys_ref, qf_ref, df_ref, e_ref, gam_ref, mine_ref, bz_ref, logit_ref, da_ref, ins, outs):
    places = [slot_of(codes_ref, s) for s in range(CAP)]
    small = fetch((e_hbm, gam_hbm), (e_ref, gam_ref), ins)
    loads = []
    for s, (_, qb, kb) in enumerate(places):
        loads.append(fetch(
            (keys_hbm.at[rows_of(kb)], qf_hbm.at[rows_of(qb)], df_hbm.at[rows_of(qb)], bz_hbm.at[s]),
            (keys_ref.at[s], qf_ref.at[s], df_ref.at[s], bz_ref.at[s]), ins, 2 + 4 * s,
        ))
    stores = []
    for copy in small:
        copy.wait()
    e = e_ref[...]
    lane = lax.broadcasted_iota(jnp.int32, (BLK, BLK), 1)
    stats = []
    for s in range(CAP):
        listed, qb, kb = places[s]
        for copy in loads[s][:3]:
            copy.wait()
        kf = keys_ref[s, :, 0:FG]
        vf = keys_ref[s, :, FG:]
        qf = qf_ref[s]
        df = df_ref[s]
        qhi, qlo = split2(jnp.square(qf.astype(F32)))
        khi, klo = split2(jnp.square(kf.astype(F32)))
        ep = e[16:32]
        qn = dot(qhi, ep, NT) + dot(qlo, ep, NT)
        kn = dot(ep, khi, NT) + dot(ep, klo, NT)
        held = jnp.zeros((BLK, BLK), F32)
        loads[s][3].wait()
        for h in range(0, H, 2):
            at = slice(h // GH * GF, h // GH * GF + GF)
            kg = kf[:, at]
            vg = vf[:, at]
            qg = qf[:, at]
            das = dot(df[:, at], jnp.concatenate([vg * e[32 + h : 33 + h, at], vg * e[33 + h : 34 + h, at]], axis=0), NT)
            for n in range(2):
                u = h + n
                both = dot(qg, jnp.concatenate([kg * e[u : u + 1, at], kg * e[16 + u : 17 + u, at]], axis=0), NT)
                dist = qn[:, u : u + 1] + kn[u : u + 1, :] - 2.0 * both[:, BLK:]
                logit = (WL * SC) * both[:, :BLK] + WL * bz_ref[s, u] - (0.5 * WL * WC) * gam_ref[u : u + 1] * dist
                da = bz_ref[s, H + u] + das[:, n * BLK : (n + 1) * BLK]
                logit_ref[s, u] = logit
                da_ref[s, u] = da
                top = jnp.max(logit, axis=1, keepdims=True)
                p = jnp.exp(logit - top)
                total = jnp.sum(p, axis=1, keepdims=True)
                mean = jnp.sum(p * da, axis=1, keepdims=True) / total
                held = jnp.where(lane == u, top + jnp.log(total), held)
                held = jnp.where(lane == 16 + u, mean, held)
            if h % 4 == 2:
                some = pl.ds(h - 2, 4)
                for n, (ref, hbm) in enumerate(((logit_ref, logit_hbm), (da_ref, da_hbm))):
                    at = (2 * s + n) * (H // 4) + h // 4
                    stores.append(pltpu.make_async_copy(ref.at[s, some], hbm.at[s, some], outs.at[at]))
                    stores[-1].start()
        stats.append((listed, qb, jnp.transpose(held)))
    for b in range(2):
        lse = []
        for listed, qb, held in stats:
            lse.append(jnp.where(jnp.logical_and(listed, qb == b), held[0:16], NEG))
        top = jnp.maximum(lse[0], lse[1])
        w0 = jnp.exp(lse[0] - top)
        w1 = jnp.exp(lse[1] - top)
        total = w0 + w1
        merged = jnp.concatenate(
            [top + jnp.log(total), (w0 * stats[0][2][16:32] + w1 * stats[1][2][16:32]) / total], axis=0
        )
        mine_ref[:, b * BLK : (b + 1) * BLK] = merged
    stores.extend(fetch([mine_ref] * (N_COL + 1), [mine_hbm] + [stat_hbm.at[d] for d in range(N_COL)], ins))
    for copy in stores:
        copy.wait()


def out_kernel(codes_ref, pair_ref, logit_hbm, keys_hbm, stat_hbm, e_hbm, o_hbm, held, p_ref, nz_ref, cat_ref, bd_ref, sems,
               logit_ref, keys_ref, stat_ref, e_ref, o_ref, ins):
    places = [slot_of(codes_ref, s) for s in range(CAP)]
    loads = fetch((stat_hbm, e_hbm), (stat_ref, e_ref), ins)
    for s, (_, _, kb) in enumerate(places):
        loads.extend(fetch((logit_hbm.at[s], keys_hbm.at[rows_of(kb), pl.ds(FG, FG)]), (logit_ref.at[s], keys_ref.at[s]), ins, 2 + 2 * s))
    for k in range(CHUNKS):
        pair_copy(pair_ref, held, sems, k).start()
    loads[0].wait()
    loads[1].wait()
    o_ref[...] = jnp.zeros_like(o_ref)
    for s in range(CAP):
        listed, qb, kb = places[s]
        lse = jnp.transpose(jnp.concatenate([stat_ref[:, rows_of(qb)], jnp.zeros((96, BLK), F32)], axis=0))
        lse = jnp.where(listed, lse, -NEG)
        loads[2 + 2 * s].wait()
        loads[3 + 2 * s].wait()
        vf = keys_ref[s]
        for h in range(H):
            at = slice(h // GH * GF, h // GH * GF + GF)
            p = jnp.exp(logit_ref[s, h] - lse[:, h : h + 1])
            p_ref[h] = p
            cat_ref[:, h * BLK : (h + 1) * BLK] = p.astype(BF16)
            bd_ref[h * BLK : (h + 1) * BLK, :] = vf[:, at] * e_ref[32 + h : 33 + h, at]
        for g in range(G):
            at = slice(g * GJ, (g + 1) * GJ)
            o_ref[rows_of(qb), g * GF : (g + 1) * GF] += dot(cat_ref[:, at], bd_ref[at, :])

        def some(k, carry, s=s):
            @pl.when(k % (CHUNK // 16) == 0)
            def _():
                rows = pl.ds(pl.multiple_of(s * BLK + k * 16, 16), CHUNK)
                pltpu.make_async_copy(pair_ref.at[rows], held.at[rows], sems.at[s * (BLK // CHUNK) + k // (CHUNK // 16)]).wait()

            first = k * 16
            zero = jnp.zeros((H, BLK), F32)
            for i in range(0, 16, 2):
                w = jnp.concatenate(
                    [
                        jnp.concatenate([p_ref[:, first + i, :], zero], axis=1),
                        jnp.concatenate([zero, p_ref[:, first + i + 1, :]], axis=1),
                    ],
                    axis=0,
                ).astype(BF16)
                found = dot(w, held[pl.ds(s * BLK + first + i, 2)].reshape(2 * BLK, PW))
                nz_ref[:, first + i, :] = found[0:H]
                nz_ref[:, first + i + 1, :] = found[H:]
            return carry

        lax.fori_loop(0, BLK // 16, some, 0)
        for h in range(H):
            o_ref[rows_of(qb), FG + h * PW : FG + (h + 1) * PW] += nz_ref[h]
    (copy,) = fetch((o_ref,), (o_hbm,), ins)
    copy.wait()


def back_kernel(codes_ref, stat_hbm, stats_hbm, keys_hbm, qf_hbm, df_hbm, e_hbm, gam_hbm, logit_hbm, da_hbm, o_hbm,
                whole_hbm, keep_hbm, kg_hbm, send_hbm,
                mine_ref, all_ref, keys_ref, qf_ref, df_ref, e_ref, gam_ref, logit_ref, da_ref, o_ref, ins,
                whole_ref, keep_ref, kg_ref, send_ref, sems, kg_acc, gcat, gstk, astk, kbd, qbd, dbd, ebd, dq_acc, msg):
    places = [slot_of(codes_ref, s) for s in range(CAP)]
    small = fetch((stat_hbm, stats_hbm, e_hbm, gam_hbm), (mine_ref, all_ref, e_ref, gam_ref), ins)
    loads = []
    for s, (_, qb, kb) in enumerate(places):
        loads.append(fetch(
            (logit_hbm.at[s], da_hbm.at[s], keys_hbm.at[rows_of(kb), pl.ds(0, FG)], qf_hbm.at[rows_of(qb)], df_hbm.at[rows_of(qb)]),
            (logit_ref.at[s], da_ref.at[s], keys_ref.at[s], qf_ref.at[s], df_ref.at[s]), ins, 10 + 5 * s,
        ))
    (o_copy,) = fetch((o_hbm,), (o_ref,), ins, 20)
    for copy in small:
        copy.wait()
    held = [all_ref[d] for d in range(N_COL)]
    top = held[0][0:16]
    for d in range(1, N_COL):
        top = jnp.maximum(top, held[d][0:16])
    total = jnp.zeros((16, QR), F32)
    mean = jnp.zeros((16, QR), F32)
    for d in range(N_COL):
        w = jnp.exp(held[d][0:16] - top)
        total = total + w
        mean = mean + w * held[d][16:32]
    lse = top + jnp.log(total)
    delta = mean / total
    alpha = jnp.exp(mine_ref[0:16] - lse)
    whole_t = jnp.concatenate([lse, delta, alpha, jnp.zeros((80, QR), F32)], axis=0)
    whole = jnp.transpose(whole_t)
    whole_ref[...] = whole
    e = e_ref[32:48]
    gam_f = jnp.sum(e.astype(F32) * gam_ref[:, 0:1], axis=0, keepdims=True)
    point = jnp.sum(e_ref[16:32].astype(F32), axis=0, keepdims=True)
    scalar = jnp.sum(e_ref[0:16].astype(F32), axis=0, keepdims=True)
    fa = WC * gam_f * point + SC * scalar
    fb = -WC * gam_f * point
    kg_acc[...] = jnp.zeros_like(kg_acc)
    dq_acc[...] = jnp.zeros_like(dq_acc)
    for h in range(H):
        at = slice(h // GH * GF, h // GH * GF + GF)
        ebd[h * BLK : (h + 1) * BLK, :] = jnp.broadcast_to(e[h : h + 1, at], (BLK, GF))
    for s in range(CAP):
        listed, qb, kb = places[s]
        for copy in loads[s]:
            copy.wait()
        stat = jnp.where(qb == 0, whole[0:BLK], whole[BLK:])
        lse_s = jnp.where(listed, stat, -NEG)
        kf = keys_ref[s]
        qf = qf_ref[s]
        df = df_ref[s]
        for h in range(H):
            at = slice(h // GH * GF, h // GH * GF + GF)
            block = slice(h * BLK, (h + 1) * BLK)
            a = jnp.exp(logit_ref[s, h] - lse_s[:, h : h + 1])
            g = WL * a * (da_ref[s, h] - stat[:, 16 + h : 17 + h])
            gr = g.astype(BF16)
            gcat[:, block] = gr
            gstk[block, :] = gr
            astk[block, :] = a.astype(BF16)
            eh = e[h : h + 1, at]
            kbd[block, :] = kf[:, at] * eh
            qbd[block, :] = qf[:, at] * eh
            dbd[block, :] = df[:, at] * eh
        for g in range(G):
            at = slice(g * GF, (g + 1) * GF)
            block = slice(g * GJ, (g + 1) * GJ)
            dq_raw = dot(gcat[:, block], kbd[block, :])
            row_sum = dot(gcat[:, block], ebd[block, :])
            dq_acc[rows_of(qb), at] += fa[:, at] * dq_raw + fb[:, at] * row_sum * qf[:, at].astype(F32)
            dk_raw = dot(gstk[block, :], qbd[block, :], TN)
            col_sum = dot(gstk[block, :], ebd[block, :], TN)
            kg_acc[rows_of(kb), at] += fa[:, at] * dk_raw + fb[:, at] * col_sum * kf[:, at].astype(F32)
            kg_acc[rows_of(kb), FG + g * GF : FG + (g + 1) * GF] += dot(astk[block, :], dbd[block, :], TN)
    kg_ref[...] = kg_acc[...].astype(BF16)
    kg_copy = pltpu.make_async_copy(kg_ref, kg_hbm, sems.at[0])
    kg_copy.start()
    o_copy.wait()
    ahi, alo = split2(whole[:, 32:48])
    msg[:, 0:FG] = (o_ref[:, 0:FG] * (dot(ahi, e) + dot(alo, e))).astype(BF16)
    for h in range(H):
        at = slice(FG + h * PW, FG + (h + 1) * PW)
        msg[:, at] = (o_ref[:, at] * whole[:, 32 + h : 33 + h]).astype(BF16)
    msg[:, 2048:] = dq_acc[...].astype(BF16)
    core = lax.axis_index("col") % 2
    for x in range(4):
        keep_ref[x] = msg[pl.ds(pl.multiple_of((2 * x + core) * OWN, OWN), OWN), :]
        send_ref[x] = msg[pl.ds(pl.multiple_of((2 * x + 1 - core) * OWN, OWN), OWN), :]
    copies = fetch((send_ref, keep_ref, whole_ref), (send_hbm, keep_hbm, whole_hbm), sems, 1)
    for copy in [kg_copy] + copies:
        copy.wait()


def fold_kernel(keep_ref, got_ref, own_ref, one_ref, two_ref, three_ref):
    x = lax.axis_index("col") // 2
    for k, ref in enumerate((own_ref, one_ref, two_ref, three_ref)):
        at = (x + k) % 4
        ref[...] = (keep_ref[at].astype(F32) + got_ref[at].astype(F32)).astype(BF16)


def pair_out_kernel(codes_ref, whole_hbm, logit_hbm, da_hbm, dzp_hbm, out_ref, held, ga, sems, logit_ref, da_ref, dzp_ref, whole_ref, ins):
    (whole_copy,) = fetch((whole_hbm,), (whole_ref,), ins, 2 * CAP + 1)
    loads = []
    for s in range(CAP):
        loads.append(pltpu.make_async_copy(logit_hbm.at[s], logit_ref.at[s], ins.at[2 * s]))
        loads.append(pltpu.make_async_copy(da_hbm.at[s], da_ref.at[s], ins.at[2 * s + 1]))
    loads.insert(2, pltpu.make_async_copy(dzp_hbm, dzp_ref, ins.at[2 * CAP]))
    for copy in loads:
        copy.start()
    whole_copy.wait()
    for s in range(CAP):
        listed, qb, _ = slot_of(codes_ref, s)
        stat = whole_ref[rows_of(qb), :]
        lse_s = jnp.where(listed, stat, -NEG)
        for copy in loads[0:2] if s == 0 else loads[3:5]:
            copy.wait()
        for h in range(H):
            a = jnp.exp(logit_ref[s, h] - lse_s[:, h : h + 1])
            ga[h] = WL * a * (da_ref[s, h] - stat[:, 16 + h : 17 + h])
            ga[H + h] = a
        if s == 0:
            loads[2].wait()

        def some(k, carry, s=s, qb=qb):
            first = k * 16
            zero = jnp.zeros((2 * H, PW), BF16)
            for i in range(0, 16, 2):
                lhs = jnp.concatenate([ga[:, first + i, :], ga[:, first + i + 1, :]], axis=0).astype(BF16)
                one = dzp_ref[qb * BLK + first + i].astype(BF16)
                two = dzp_ref[qb * BLK + first + i + 1].astype(BF16)
                rhs = jnp.concatenate(
                    [jnp.concatenate([one, zero], axis=1), jnp.concatenate([zero, two], axis=1)], axis=0
                )
                found = dot(lhs, rhs, TN).astype(BF16)
                held[s * BLK + first + i] = found[:, :PW]
                held[s * BLK + first + i + 1] = found[:, PW:]

            @pl.when(k % (CHUNK // 16) == CHUNK // 16 - 1)
            def _():
                rows = pl.ds(pl.multiple_of(s * BLK + k * 16 + 16 - CHUNK, 16), CHUNK)
                pltpu.make_async_copy(held.at[rows], out_ref.at[rows], sems.at[s * (BLK // CHUNK) + k // (CHUNK // 16)]).start()

            return carry

        lax.fori_loop(0, BLK // 16, some, 0)
    for k in range(CHUNKS):
        pair_copy(held, out_ref, sems, k).wait()


def final_kernel(kg_ref, own_ref, one_ref, two_ref, three_ref, frame_q_ref, frame_k_ref, ow_hbm, up_ref, gq_ref, gk_ref, ow_ref, sems):
    (ow_copy,) = fetch((ow_hbm,), (ow_ref,), sems)
    total = kg_ref[0].astype(F32)
    for d in range(1, N_ROW):
        total = total + kg_ref[d].astype(F32)
    fk = frame_k_ref[...]
    fq = frame_q_ref[pl.ds(pl.multiple_of(lax.axis_index("col") * OWN, OWN), OWN), :]
    dk, dgk = ungrouped(total[:, :FG])
    dv, dgv = ungrouped(total[:, FG:])
    gk_ref[...] = jnp.concatenate(
        [dk, dv] + rotate_back(dgk, fk, False) + rotate_back(dgv, fk, False), axis=1
    ).astype(BF16)
    msg = (own_ref[...].astype(F32) + one_ref[...].astype(F32)) + (two_ref[...].astype(F32) + three_ref[...].astype(F32))
    scalar, parts = ungrouped(msg[:, :FG])
    head = jnp.concatenate([scalar] + rotate_back(parts, fq, True), axis=1).astype(BF16)
    tail = msg[:, FG:2048].astype(BF16)
    ow_copy.wait()
    up_ref[...] = (dot(head, ow_ref[0:F]) + dot(tail, ow_ref[F:])).astype(BF16)
    dq, dgq = ungrouped(msg[:, 2048:])
    gq_ref[...] = jnp.concatenate([dq] + rotate_back(dgq, fq, False), axis=1).astype(BF16)


SMEM = pl.BlockSpec(memory_space=pltpu.SMEM)
FULL = pl.BlockSpec(memory_space=pltpu.VMEM)
HBM = pl.BlockSpec(memory_space=pltpu.HBM)
DMA = pltpu.SemaphoreType.DMA


def call(kernel, name, ins, outs, scratch, mb, flops=0, nbytes=0):
    return pl.pallas_call(
        kernel,
        name=name,
        in_specs=ins,
        out_specs=[spec for _, spec in outs],
        out_shape=[shape for shape, _ in outs],
        scratch_shapes=scratch,
        compiler_params=pltpu.CompilerParams(vmem_limit_bytes=56 * MB if mb > 12 else mb * MB),
        cost_estimate=pl.CostEstimate(flops=flops, bytes_accessed=nbytes, transcendentals=0),
    )


def near(dims, kind):
    return jax.ShapeDtypeStruct(dims, kind), FULL


def far(dims, kind):
    return jax.ShapeDtypeStruct(dims, kind), HBM


def free(dims, kind):
    return jax.ShapeDtypeStruct(dims, kind), FULL


def on_device(queries, keys, frame_table, frame_index, pair_list, pair, pair_weight, point_weight, out_weight, cotangent):
    codes = pair_list.reshape(CAP)
    tiles = pair.reshape(CAP * BLK, BLK, PW)
    e = jnp.asarray(head_rows(), BF16)
    index = frame_index.reshape(1, NRES)
    sems = DMA((CHUNKS,))
    held = pltpu.VMEM((CAP * BLK, BLK, PW), BF16)
    table = pltpu.VMEM((12, NRES), F32)
    where = pltpu.VMEM((1, NRES), jnp.int32)
    planes = (CAP, H, BLK, BLK)

    key_wire, frame_k = call(
        key_kernel, "keys", [HBM] * 3, [far((N_ROW, OWN, 2 * FG), BF16), near((OWN, BLK), F32)],
        [pltpu.VMEM((BLK, BLK), F32), pltpu.VMEM((OWN, 2 * F), BF16), table, where, pltpu.VMEM((OWN, 2 * FG), BF16),
         DMA((3 + N_ROW,))], 56,
    )(keys, frame_table, index)
    key_all = lax.all_to_all(key_wire, "row", split_axis=0, concat_axis=0).reshape(KR, 2 * FG)

    half = pltpu.VMEM((CAP, BLK, FG), BF16)
    marks = pltpu.VMEM((48, FG), BF16)
    gammas = pltpu.VMEM((16, BLK), F32)
    rows = pltpu.VMEM((QR, FG), BF16)
    plane_buf = pltpu.VMEM(planes, F32)
    dzp_buf = pltpu.VMEM((QR, 2 * H, PW), F32)
    bz_buf = pltpu.VMEM((CAP, 2 * H, BLK, BLK), F32)
    qf, df, frame_q, gam, dzp, bz = call(
        prep_kernel, "prep", [SMEM] + [HBM] * 8,
        [far((QR, FG), BF16), far((QR, FG), BF16), far((QR, BLK), F32), far((16, BLK), F32),
         far((QR, 2 * H, PW), F32), far((CAP, 2 * H, BLK, BLK), F32)],
        [held, sems, table, where, pltpu.VMEM((1, H), F32), pltpu.VMEM((F, QR), BF16), pltpu.VMEM((QR, SW), BF16),
         pltpu.VMEM((2016, SW), BF16), pltpu.VMEM((H, PW), BF16), DMA((7,)),
         rows, rows, pltpu.VMEM((QR, BLK), F32), gammas, dzp_buf, bz_buf, DMA((CHUNKS + 5,))],
        56, flops=3_000_000_000, nbytes=30_000_000,
    )(codes, queries.T, pair_weight.T, point_weight.reshape(1, H), frame_table, index, cotangent, out_weight, tiles)

    mine, logit, da, stat = call(
        logit_kernel, "logit", [SMEM] + [HBM] * 6, [far((32, QR), F32), far(planes, F32), far(planes, F32), far((N_COL, 32, QR), F32)],
        [pltpu.VMEM((CAP, BLK, 2 * FG), BF16), half, half, marks, gammas, pltpu.VMEM((32, QR), F32), bz_buf, plane_buf,
         plane_buf, DMA((10,)), DMA((H,))], 56,
    )(codes, key_all, qf, df, e, gam, bz)

    stat_all = lax.all_to_all(stat, "col", split_axis=0, concat_axis=0)

    (out,) = call(
        out_kernel, "local_out", [SMEM] + [HBM] * 5, [far((QR, 2048), F32)],
        [held, pltpu.VMEM((H, BLK, BLK), F32), pltpu.VMEM((H, BLK, PW), F32), pltpu.VMEM((BLK, HJ), BF16),
         pltpu.VMEM((HJ, GF), BF16), sems, plane_buf, half, pltpu.VMEM((32, QR), F32), marks,
         pltpu.VMEM((QR, 2048), F32), DMA((6,))], 56, flops=2_000_000_000, nbytes=20_000_000,
    )(codes, tiles, logit, key_all, mine, e)

    whole, keep, kg, send = call(
        back_kernel, "back", [SMEM] + [HBM] * 10,
        [far((QR, BLK), F32), far((4, OWN, 2560), BF16), far((KR, 2 * FG), BF16), far((4, OWN, 2560), BF16)],
        [pltpu.VMEM((32, QR), F32), pltpu.VMEM((N_COL, 32, QR), F32), half, half, half, marks, gammas, plane_buf, plane_buf,
         pltpu.VMEM((QR, 2048), F32), DMA((21,)),
         pltpu.VMEM((QR, BLK), F32), pltpu.VMEM((4, OWN, 2560), BF16), pltpu.VMEM((KR, 2 * FG), BF16),
         pltpu.VMEM((4, OWN, 2560), BF16), DMA((4,)),
         pltpu.VMEM((KR, 2 * FG), F32), pltpu.VMEM((BLK, HJ), BF16), pltpu.VMEM((HJ, BLK), BF16),
         pltpu.VMEM((HJ, BLK), BF16), pltpu.VMEM((HJ, GF), BF16), pltpu.VMEM((HJ, GF), BF16),
         pltpu.VMEM((HJ, GF), BF16), pltpu.VMEM((HJ, GF), BF16), pltpu.VMEM((QR, FG), F32),
         pltpu.VMEM((QR, 2560), BF16)], 56,
    )(codes, mine, stat_all, key_all, qf, df, e, gam, logit, da, out)

    kg_all = lax.all_to_all(kg.reshape(N_ROW, OWN, 2 * FG), "row", split_axis=0, concat_axis=0)
    got = lax.ppermute(send, "col", [(d, d ^ 1) for d in range(N_COL)])
    own, *away = call(
        fold_kernel, "fold", [FULL] * 2, [near((OWN, 2560), BF16)] + [free((OWN, 2560), BF16)] * 3, [], 4
    )(keep, got)
    came = [
        lax.ppermute(part, "col", [(d, (d + 2 * k) % N_COL) for d in range(N_COL)])
        for k, part in enumerate(away, 1)
    ]

    (grad_tiles,) = call(
        pair_out_kernel, "pair_out", [SMEM] + [HBM] * 4, [far((CAP * BLK, BLK, PW), BF16)],
        [held, pltpu.VMEM((2 * H, BLK, BLK), F32), sems, plane_buf, plane_buf, dzp_buf,
         pltpu.VMEM((QR, BLK), F32), DMA((2 * CAP + 2,))], 56, flops=4_000_000_000, nbytes=30_000_000,
    )(codes, whole, logit, da, dzp)

    update, grad_queries, grad_keys = call(
        final_kernel, "final", [FULL] * 7 + [HBM],
        [free((OWN, SW), BF16), free((OWN, F), BF16), free((OWN, 2 * F), BF16)],
        [pltpu.VMEM((2016, SW), BF16), DMA((1,))], 12,
    )(kg_all, own, *came, frame_q, frame_k, out_weight)
    return update, grad_queries, grad_keys, grad_tiles.reshape(pair.shape)


def solution(mesh):
    in_specs = (
        P("row", None),
        P(("col", "row"), None),
        P(),
        P(),
        P("row", "col", None),
        P("row", "col", None, None, None, None),
        P(),
        P(),
        P(),
        P("row", None),
    )
    out_specs = (
        P(("row", "col"), None),
        P(("row", "col"), None),
        P(("col", "row"), None),
        P("row", "col", None, None, None, None),
    )
    return jax.shard_map(on_device, mesh=mesh, in_specs=in_specs, out_specs=out_specs, check_vma=False)
```

time: 127 us -> 87.3 us (0.69)
  the two profiles are of different devices: /device:TPU:1 before, /device:TPU:2 now
where the time goes in v2:
time: 87.3 us; the launch traced here: 86.8 us
  Pallas kernels  54.7 us (63%)
  starting transfers between devices  21.6 us (25%)
  waiting for transfers between devices  6.84 us (8%)
  local copies, waits for them, and re-layouts  2.76 us (3%)
  between operations  0.92 us (1%)
    pallas_call x1, Pallas kernels, on_device(): call(prep_kernel, 'prep', [SMEM] + [HBM] * 8, [far((QR, FG), BF16), far((...  13.3 us
    pallas_call x1, Pallas kernels, on_device(): call(pair_out_kernel, 'pair_out', [SMEM] + [HBM] * 4, [far((CAP * BLK, BL...  10.6 us
    pallas_call x1, Pallas kernels, on_device(): call(out_kernel, 'local_out', [SMEM] + [HBM] * 5, [far((QR, 2048), F32)],...  10.1 us
    all_to_all x1, starting transfers between devices, on_device(): lax.all_to_all(key_wire, 'row', split_axis=0, concat_axis=0)  8.06 us
    pallas_call x1, Pallas kernels, on_device(): call(logit_kernel, 'logit', [SMEM] + [HBM] * 6, [far((32, QR), F32), far(...  7.52 us
    pallas_call x1, Pallas kernels, on_device(): call(back_kernel, 'back', [SMEM] + [HBM] * 10, [far((QR, BLK), F32), far(...  7.52 us
    all_to_all x1, starting transfers between devices, on_device(): stat_all = lax.all_to_all(stat, 'col', split_axis=0, concat_axis=0)  4.84 us
    ppermute x3, starting transfers between devices, on_device(): lax.ppermute(part, 'col', [(d, (d + 2 * k) % N_COL) for d in range(N_COL)])  4.78 us
  transfers between devices with their start and end apart: 7, of which 2 were waited for; matrix products, arithmetic and copies ran while one was open for 0% of the time, Pallas kernels for 39%

profile of v2, /device:TPU:2, one launch (start us, length us, event | category | flops | bytes accessed | tf_op | source)
XLA Modules:
  0.0 86.8 jit_solution(14786517206525954033)
XLA Ops:
  0.6 3.6 %keys.1 = (bf16[16,32,1024]{2,1,0:T(8,128)(2,1)}, f32[32,128]{1,0:T(8,128)}) custom-call(bf16[32,960]{1,0:T(8,128)(2,1)} %keys_hbm.1, f32[12,4096]{1,0:T(8,128)} %table_hbm.3, s32[1,4096]{1,0:T(1,128)} %bitcast.16), custom_call_target="tpu_custom_call" | custom-call | tf_op jit(solution)/shard_map/keys/pallas_call | solution.py:587
  4.2 8.1 %all-to-all-start = ((bf16[16,32,1024]{2,1,0:T(8,128)(2,1)}), bf16[16,32,1024]{2,1,0:T(8,128)(2,1)S(1)}, u32[]{:S(2)}, u32[]{:S(2)}) async-start(bf16[16,32,1024]{2,1,0:T(8,128)(2,1)} %get-tuple-element.27), calls=%async_computation | async-start | bytes 2097152 | tf_op jit(solution)/shard_map/all_to_all | solution.py:592
  12.3 13.3 %prep.1 = (bf16[256,512]{1,0:T(8,128)(2,1)}, bf16[256,512]{1,0:T(8,128)(2,1)}, f32[256,128]{1,0:T(8,128)}, f32[16,128]{1,0:T(8,128)}, f32[256,24,128]{2,1,0:T(8,128)}, /*index=5*/f32[2,24,128,128]{3,2,1,0:T(8,128)}) custom-call(s32[2]{0:T(128)} %bitcast.18, bf16[480,256]{1,0:T(8,128)(2,1)} %bitcast.23, bf16[12,128]{1,0:T(8,128)(2,1)} %bitcast.24, ...), custom_call_target="tpu_custom_call" | custom-call | flops 3000000000 | bytes 30000000 | tf_op jit(solution)/shard_map/prep/pallas_call | solution.py:601
  25.6 4.3 %all-to-all-done = bf16[16,32,1024]{2,1,0:T(8,128)(2,1)S(1)} async-done(((bf16[16,32,1024]{2,1,0:T(8,128)(2,1)}), bf16[16,32,1024]{2,1,0:T(8,128)(2,1)S(1)}, u32[]{:S(2)}, u32[]{:S(2)}) %all-to-all-start) | async-done | bytes 1048608 | tf_op jit(solution)/shard_map/all_to_all | solution.py:592
  29.9 0.0 copy-start.4
  29.9 1.0 %copy-done.4 = bf16[16,32,1024]{2,1,0:T(8,128)(2,1)} copy-done((bf16[16,32,1024]{2,1,0:T(8,128)(2,1)}, bf16[16,32,1024]{2,1,0:T(8,128)(2,1)S(1)}, u32[]{:S(2)}) %copy-start.4) | copy-done | bytes 1048600
  30.9 7.5 %logit.1 = (f32[32,256]{1,0:T(8,128)}, f32[2,12,128,128]{3,2,1,0:T(8,128)}, f32[2,12,128,128]{3,2,1,0:T(8,128)}, f32[8,32,256]{2,1,0:T(8,128)}) custom-call(s32[2]{0:T(128)} %bitcast.19, bf16[512,1024]{1,0:T(8,128)(2,1)} %bitcast.9, bf16[256,512]{1,0:T(8,128)(2,1)} %get-tuple-element.28.qf_hbm, bf16[256,512]{1,0:T(8,128)(2,1)} %get-tuple-element.29.df_hbm, ...), custom_call_target="tpu_custom_call" | custom-call | tf_op jit(solution)/shard_map/logit/pallas_call | solution.py:611
  38.4 4.8 %all-to-all-start.1 = ((f32[8,32,256]{2,1,0:T(8,128)}), f32[8,32,256]{2,1,0:T(8,128)S(1)}, u32[]{:S(2)}, u32[]{:S(2)}) async-start(f32[8,32,256]{2,1,0:T(8,128)} %get-tuple-element.33), calls=%async_computation.1 | async-start | bytes 524288 | tf_op jit(solution)/shard_map/all_to_all | solution.py:617
  43.3 10.1 %local_out.1.o_hbm = f32[256,2048]{1,0:T(8,128)} custom-call(s32[2]{0:T(128)} %bitcast.20, bf16[256,128,128]{2,1,0:T(8,128)(2,1)} %bitcast.13, f32[2,12,128,128]{3,2,1,0:T(8,128)} %get-tuple-element.34.logit_hbm, bf16[512,1024]{1,0:T(8,128)(2,1)} %bitcast.10, f32[32,256]{1,0:T(8,128)} %get-tuple-element.32.stat_hbm, bf16[48,512]{1,0:T(8,128)(2,1)} %constant.2.clone.e_hbm), custom_call_target="tpu_custom_call" | custom-call | flops 2000000000 | bytes 20000000 | tf_op jit(solution)/shard_map/local_out/pallas_call | solution.py:619
  53.4 0.0 all-to-all-done.1.stats_hbm
  53.4 0.0 copy-start.5
  53.4 0.7 copy-done.5
  54.1 7.5 %back.1 = (f32[256,128]{1,0:T(8,128)}, bf16[4,32,2560]{2,1,0:T(8,128)(2,1)}, bf16[512,1024]{1,0:T(8,128)(2,1)}, bf16[4,32,2560]{2,1,0:T(8,128)(2,1)}) custom-call(s32[2]{0:T(128)} %bitcast.21, f32[32,256]{1,0:T(8,128)} %get-tuple-element.32.stat_hbm, f32[8,32,256]{2,1,0:T(8,128)} %copy-done.5, bf16[512,1024]{1,0:T(8,128)(2,1)} %bitcast.11, ...), custom_call_target="tpu_custom_call" | custom-call | tf_op jit(solution)/shard_map/back/pallas_call | solution.py:626
  61.6 0.2 collective-permute-start
  61.8 3.7 %all-to-all-start.2 = ((bf16[16,32,1024]{2,1,0:T(8,128)(2,1)}), bf16[16,32,1024]{2,1,0:T(8,128)(2,1)S(1)}, u32[]{:S(2)}, u32[]{:S(2)}) async-start(bf16[16,32,1024]{2,1,0:T(8,128)(2,1)} %bitcast.15), calls=%async_computation.2 | async-start | bytes 2097152 | tf_op jit(solution)/shard_map/all_to_all | solution.py:639
  65.5 0.0 collective-permute-done.got_ref
  65.5 0.0 copy-start.1
  65.5 1.1 %copy-done.1 = bf16[4,32,2560]{2,1,0:T(8,128)(2,1)S(1)} copy-done((bf16[4,32,2560]{2,1,0:T(8,128)(2,1)S(1)}, bf16[4,32,2560]{2,1,0:T(8,128)(2,1)}, u32[]{:S(2)}) %copy-start.1) | copy-done | bytes 655384
  66.6 0.2 fold.1
  66.7 1.5 %collective-permute-start.1 = (bf16[32,2560]{1,0:T(8,128)(2,1)S(1)}, bf16[32,2560]{1,0:T(8,128)(2,1)S(1)}, u32[]{:S(2)}, u32[]{:S(2)}) collective-permute-start(bf16[32,2560]{1,0:T(8,128)(2,1)S(1)} %get-tuple-element.40), channel_id=1, source_target_pairs={{0,2},{1,3},{2,4},{3,5},{4,6},{5,7},{6,0},{7,1},{8,10},{9,11},{10,... | collective-permute-start | bytes 491528 | tf_op jit(solution)/shard_map/ppermute | solution.py:645
  68.3 0.9 %collective-permute-start.2 = (bf16[32,2560]{1,0:T(8,128)(2,1)S(1)}, bf16[32,2560]{1,0:T(8,128)(2,1)S(1)}, u32[]{:S(2)}, u32[]{:S(2)}) collective-permute-start(bf16[32,2560]{1,0:T(8,128)(2,1)S(1)} %get-tuple-element.41), channel_id=1, source_target_pairs={{0,4},{1,5},{2,6},{3,7},{4,0},{5,1},{6,2},{7,3},{8,12},{9,13},{10,... | collective-permute-start | bytes 491528 | tf_op jit(solution)/shard_map/ppermute | solution.py:645
  69.2 2.3 %collective-permute-start.3 = (bf16[32,2560]{1,0:T(8,128)(2,1)S(1)}, bf16[32,2560]{1,0:T(8,128)(2,1)S(1)}, u32[]{:S(2)}, u32[]{:S(2)}) collective-permute-start(bf16[32,2560]{1,0:T(8,128)(2,1)S(1)} %get-tuple-element.42), channel_id=1, source_target_pairs={{0,6},{1,7},{2,0},{3,1},{4,2},{5,3},{6,4},{7,5},{8,14},{9,15},{10,... | collective-permute-start | bytes 491528 | tf_op jit(solution)/shard_map/ppermute | solution.py:645
  71.5 0.0 copy-start
  71.5 0.0 copy-start.2
  71.5 0.0 copy-start.3
  71.5 10.6 %pair_out.1 = bf16[256,128,128]{2,1,0:T(8,128)(2,1)} custom-call(s32[2]{0:T(128)} %bitcast.22, f32[256,128]{1,0:T(8,128)} %get-tuple-element.48.whole_hbm, f32[2,12,128,128]{3,2,1,0:T(8,128)} %get-tuple-element.34.logit_hbm, f32[2,12,128,128]{3,2,1,0:T(8,128)} %get-tuple-element.35.da_hbm, f32[256,24,128]{2,1,0:T(8,128)} %get-tuple-element.49.dzp_hbm), custom_call_target="tpu_custom_call" | custom-call | flops 4000000000 | bytes 30000000 | tf_op jit(solution)/shard_map/pair_out/pallas_call | solution.py:649
  82.1 0.0 collective-permute-done.1.one_ref
  82.2 0.0 collective-permute-done.2.two_ref
  82.2 0.0 collective-permute-done.3.three_ref
  82.2 2.5 %all-to-all-done.2.kg_ref = bf16[16,32,1024]{2,1,0:T(8,128)(2,1)S(1)} async-done(((bf16[16,32,1024]{2,1,0:T(8,128)(2,1)}), bf16[16,32,1024]{2,1,0:T(8,128)(2,1)S(1)}, u32[]{:S(2)}, u32[]{:S(2)}) %all-to-all-start.2) | async-done | bytes 1048608 | tf_op jit(solution)/shard_map/all_to_all | solution.py:639
  84.7 0.0 copy-done
  84.7 0.0 copy-done.2
  84.7 0.0 copy-done.3
  84.7 1.9 %final.1 = (bf16[32,384]{1,0:T(8,128)(2,1)}, bf16[32,480]{1,0:T(8,128)(2,1)}, bf16[32,960]{1,0:T(8,128)(2,1)}) custom-call(bf16[16,32,1024]{2,1,0:T(8,128)(2,1)S(1)} %all-to-all-done.2.kg_ref, bf16[32,2560]{1,0:T(8,128)(2,1)S(1)} %get-tuple-element.39.own_ref, bf16[32,2560]{1,0:T(8,128)(2,1)S(1)} %collective-permute-done.1.one_ref, ...), custom_call_target="tpu_custom_call" | custom-call | tf_op jit(solution)/shard_map/final/pallas_call | solution.py:655
Async XLA Ops:
  4.2 25.7 %all-to-all-start = ((bf16[16,32,1024]{2,1,0:T(8,128)(2,1)}), bf16[16,32,1024]{2,1,0:T(8,128)(2,1)S(1)}, u32[]{:S(2)}, u32[]{:S(2)}) async-start(bf16[16,32,1024]{2,1,0:T(8,128)(2,1)} %get-tuple-element.27), calls=%async_computation | async-start | bytes 2097152 | tf_op jit(solution)/shard_map/all_to_all | solution.py:592
  29.9 1.0 %copy-start.4 = (bf16[16,32,1024]{2,1,0:T(8,128)(2,1)}, bf16[16,32,1024]{2,1,0:T(8,128)(2,1)S(1)}, u32[]{:S(2)}) copy-start(bf16[16,32,1024]{2,1,0:T(8,128)(2,1)S(1)} %all-to-all-done) | copy-start | bytes 3145732
  38.4 14.9 %all-to-all-start.1 = ((f32[8,32,256]{2,1,0:T(8,128)}), f32[8,32,256]{2,1,0:T(8,128)S(1)}, u32[]{:S(2)}, u32[]{:S(2)}) async-start(f32[8,32,256]{2,1,0:T(8,128)} %get-tuple-element.33), calls=%async_computation.1 | async-start | bytes 524288 | tf_op jit(solution)/shard_map/all_to_all | solution.py:617
  53.4 0.7 copy-start.5
  61.6 3.9 %collective-permute-start = (bf16[4,32,2560]{2,1,0:T(8,128)(2,1)}, bf16[4,32,2560]{2,1,0:T(8,128)(2,1)S(1)}, u32[]{:S(2)}, u32[]{:S(2)}) collective-permute-start(bf16[4,32,2560]{2,1,0:T(8,128)(2,1)} %get-tuple-element.38), channel_id=1, source_target_pairs={{0,1},{1,0},{2,3},{3,2},{4,5},{5,4},{6,7},{7,6},{8,9},{9,8},{10,11... | collective-permute-start | bytes 1966088 | tf_op jit(solution)/shard_map/ppermute | solution.py:640
  61.8 22.9 %all-to-all-start.2 = ((bf16[16,32,1024]{2,1,0:T(8,128)(2,1)}), bf16[16,32,1024]{2,1,0:T(8,128)(2,1)S(1)}, u32[]{:S(2)}, u32[]{:S(2)}) async-start(bf16[16,32,1024]{2,1,0:T(8,128)(2,1)} %bitcast.15), calls=%async_computation.2 | async-start | bytes 2097152 | tf_op jit(solution)/shard_map/all_to_all | solution.py:639
  65.5 1.1 %copy-start.1 = (bf16[4,32,2560]{2,1,0:T(8,128)(2,1)S(1)}, bf16[4,32,2560]{2,1,0:T(8,128)(2,1)}, u32[]{:S(2)}) copy-start(bf16[4,32,2560]{2,1,0:T(8,128)(2,1)} %get-tuple-element.37.keep_ref) | copy-start | bytes 1966084
  66.7 15.4 %collective-permute-start.1 = (bf16[32,2560]{1,0:T(8,128)(2,1)S(1)}, bf16[32,2560]{1,0:T(8,128)(2,1)S(1)}, u32[]{:S(2)}, u32[]{:S(2)}) collective-permute-start(bf16[32,2560]{1,0:T(8,128)(2,1)S(1)} %get-tuple-element.40), channel_id=1, source_target_pairs={{0,2},{1,3},{2,4},{3,5},{4,6},{5,7},{6,0},{7,1},{8,10},{9,11},{10,... | collective-permute-start | bytes 491528 | tf_op jit(solution)/shard_map/ppermute | solution.py:645
  68.3 13.9 %collective-permute-start.2 = (bf16[32,2560]{1,0:T(8,128)(2,1)S(1)}, bf16[32,2560]{1,0:T(8,128)(2,1)S(1)}, u32[]{:S(2)}, u32[]{:S(2)}) collective-permute-start(bf16[32,2560]{1,0:T(8,128)(2,1)S(1)} %get-tuple-element.41), channel_id=1, source_target_pairs={{0,4},{1,5},{2,6},{3,7},{4,0},{5,1},{6,2},{7,3},{8,12},{9,13},{10,... | collective-permute-start | bytes 491528 | tf_op jit(solution)/shard_map/ppermute | solution.py:645
  69.2 12.9 %collective-permute-start.3 = (bf16[32,2560]{1,0:T(8,128)(2,1)S(1)}, bf16[32,2560]{1,0:T(8,128)(2,1)S(1)}, u32[]{:S(2)}, u32[]{:S(2)}) collective-permute-start(bf16[32,2560]{1,0:T(8,128)(2,1)S(1)} %get-tuple-element.42), channel_id=1, source_target_pairs={{0,6},{1,7},{2,0},{3,1},{4,2},{5,3},{6,4},{7,5},{8,14},{9,15},{10,... | collective-permute-start | bytes 491528 | tf_op jit(solution)/shard_map/ppermute | solution.py:645
  71.5 13.2 %copy-start = (bf16[2016,384]{1,0:T(8,128)(2,1)S(1)}, bf16[2016,384]{1,0:T(8,128)(2,1)}, u32[]{:S(2)}) copy-start(bf16[2016,384]{1,0:T(8,128)(2,1)} %ow_hbm.3) | copy-start | bytes 4644868
  71.5 13.2 %copy-start.2 = (f32[256,128]{1,0:T(8,128)S(1)}, f32[256,128]{1,0:T(8,128)}, u32[]{:S(2)}) copy-start(f32[256,128]{1,0:T(8,128)} %get-tuple-element.43.frame_q_ref) | copy-start | bytes 393220
  71.5 13.2 %copy-start.3 = (f32[32,128]{1,0:T(8,128)S(1)}, f32[32,128]{1,0:T(8,128)}, u32[]{:S(2)}) copy-start(f32[32,128]{1,0:T(8,128)} %get-tuple-element.44.frame_k_ref) | copy-start | bytes 49156

commit v3 on v2

--- a/solution.py
+++ b/solution.py
@@ -41,6 +41,7 @@
 GF = 256
 FG = G * GF
 CHUNK = 32
+STEP = 64
 
 NN = (((1,), (0,)), ((), ()))
 NT = (((1,), (1,)), ((), ()))
@@ -213,26 +214,23 @@
         _, qb, _ = slot_of(codes_ref, s)
 
         def some(k, carry, s=s, qb=qb):
-            @pl.when(k % (CHUNK // 16) == 0)
-            def _():
-                rows = pl.ds(pl.multiple_of(s * BLK + k * 16, 16), CHUNK)
-                pltpu.make_async_copy(pair_ref.at[rows], held.at[rows], sems.at[s * (BLK // CHUNK) + k // (CHUNK // 16)]).wait()
-
-            first = k * 16
-            for i in range(0, 16, 2):
+            for c in range(STEP // CHUNK):
+                rows = pl.ds(pl.multiple_of(s * BLK + k * STEP + c * CHUNK, CHUNK), CHUNK)
+                at = s * (BLK // CHUNK) + k * (STEP // CHUNK) + c
+                pltpu.make_async_copy(pair_ref.at[rows], held.at[rows], sems.at[at]).wait()
+            first = k * STEP
+            for i in range(0, STEP, 2):
                 lhs = dzp_ref[pl.ds(qb * BLK + first + i, 2)].reshape(4 * H, PW).astype(BF16)
                 z = held[pl.ds(s * BLK + first + i, 2)].reshape(2 * BLK, PW)
                 found = dot(lhs, z, NT)
                 bz_ref[s, :, first + i, :] = found[0 : 2 * H, 0:BLK]
                 bz_ref[s, :, first + i + 1, :] = found[2 * H :, BLK:]
 
-            @pl.when(k % (CHUNK // 16) == CHUNK // 16 - 1)
-            def _():
-                bz_copy(s, k // (CHUNK // 16)).start()
-
+            for c in range(STEP // CHUNK):
+                bz_copy(s, k * (STEP // CHUNK) + c).start()
             return carry
 
-        lax.fori_loop(0, BLK // 16, some, 0)
+        lax.fori_loop(0, BLK // STEP, some, 0)
     for copy in stores:
         copy.wait()
     for s in range(CAP):
@@ -344,14 +342,13 @@
             o_ref[rows_of(qb), g * GF : (g + 1) * GF] += dot(cat_ref[:, at], bd_ref[at, :])
 
         def some(k, carry, s=s):
-            @pl.when(k % (CHUNK // 16) == 0)
-            def _():
-                rows = pl.ds(pl.multiple_of(s * BLK + k * 16, 16), CHUNK)
-                pltpu.make_async_copy(pair_ref.at[rows], held.at[rows], sems.at[s * (BLK // CHUNK) + k // (CHUNK // 16)]).wait()
-
-            first = k * 16
+            for c in range(STEP // CHUNK):
+                rows = pl.ds(pl.multiple_of(s * BLK + k * STEP + c * CHUNK, CHUNK), CHUNK)
+                at = s * (BLK // CHUNK) + k * (STEP // CHUNK) + c
+                pltpu.make_async_copy(pair_ref.at[rows], held.at[rows], sems.at[at]).wait()
+            first = k * STEP
             zero = jnp.zeros((H, BLK), F32)
-            for i in range(0, 16, 2):
+            for i in range(0, STEP, 2):
                 w = jnp.concatenate(
                     [
                         jnp.concatenate([p_ref[:, first + i, :], zero], axis=1),
@@ -364,7 +361,7 @@
                 nz_ref[:, first + i + 1, :] = found[H:]
             return carry
 
-        lax.fori_loop(0, BLK // 16, some, 0)
+        lax.fori_loop(0, BLK // STEP, some, 0)
         for h in range(H):
             o_ref[rows_of(qb), FG + h * PW : FG + (h + 1) * PW] += nz_ref[h]
     (copy,) = fetch((o_ref,), (o_hbm,), ins)
@@ -495,9 +492,9 @@
             loads[2].wait()
 
         def some(k, carry, s=s, qb=qb):
-            first = k * 16
+            first = k * STEP
             zero = jnp.zeros((2 * H, PW), BF16)
-            for i in range(0, 16, 2):
+            for i in range(0, STEP, 2):
                 lhs = jnp.concatenate([ga[:, first + i, :], ga[:, first + i + 1, :]], axis=0).astype(BF16)
                 one = dzp_ref[qb * BLK + first + i].astype(BF16)
                 two = dzp_ref[qb * BLK + first + i + 1].astype(BF16)
@@ -508,14 +505,13 @@
                 held[s * BLK + first + i] = found[:, :PW]
                 held[s * BLK + first + i + 1] = found[:, PW:]
 
-            @pl.when(k % (CHUNK // 16) == CHUNK // 16 - 1)
-            def _():
-                rows = pl.ds(pl.multiple_of(s * BLK + k * 16 + 16 - CHUNK, 16), CHUNK)
-                pltpu.make_async_copy(held.at[rows], out_ref.at[rows], sems.at[s * (BLK // CHUNK) + k // (CHUNK // 16)]).start()
-
+                if i % CHUNK == CHUNK - 2:
+                    rows = pl.ds(pl.multiple_of(s * BLK + k * STEP + i + 2 - CHUNK, CHUNK), CHUNK)
+                    at = s * (BLK // CHUNK) + k * (STEP // CHUNK) + i // CHUNK
+                    pltpu.make_async_copy(held.at[rows], out_ref.at[rows], sems.at[at]).start()
             return carry
 
-        lax.fori_loop(0, BLK // 16, some, 0)
+        lax.fori_loop(0, BLK // STEP, some, 0)
     for k in range(CHUNKS):
         pair_copy(held, out_ref, sems, k).wait()
 

time: 87.3 us -> 85.9 us (0.984)
  Pallas kernels: 54.7 us -> 49.2 us
  waiting for transfers between devices: 6.84 us -> 10.9 us
    all_to_all x1, waiting for transfers between devices: 2.52 us -> 5.14 us  [on_device(): lax.all_to_all(kg.reshape(N_ROW, OWN, 2 * FG), 'row', split_axis=0, conca...]
    pallas_call x1, Pallas kernels: 10.6 us -> 8.01 us  [on_device(): call(pair_out_kernel, 'pair_out', [SMEM] + [HBM] * 4, [far((CAP * BLK, BL...]
    pallas_call x1, Pallas kernels: 10.1 us -> 8.58 us  [on_device(): call(out_kernel, 'local_out', [SMEM] + [HBM] * 5, [far((QR, 2048), F32)],...]
    all_to_all x1, waiting for transfers between devices: 4.3 us -> 5.73 us  [on_device(): lax.all_to_all(key_wire, 'row', split_axis=0, concat_axis=0)]
    pallas_call x1, Pallas kernels: 13.3 us -> 11.9 us  [on_device(): call(prep_kernel, 'prep', [SMEM] + [HBM] * 8, [far((QR, FG), BF16), far((...]
  transfers between devices with their start and end apart: 7 -> 7, of which waited for: 2 -> 2; matrix products, arithmetic and copies ran while one was open for 0% -> 0% of each run, Pallas kernels for 39% -> 34%
where the time goes in v3:
time: 85.9 us; the launch traced here: 85.4 us
  Pallas kernels  49.2 us (57%)
  starting transfers between devices  21.6 us (25%)
  waiting for transfers between devices  10.9 us (13%)
  local copies, waits for them, and re-layouts  2.76 us (3%)
  between operations  0.92 us (1%)
    pallas_call x1, Pallas kernels, on_device(): call(prep_kernel, 'prep', [SMEM] + [HBM] * 8, [far((QR, FG), BF16), far((...  11.9 us
    pallas_call x1, Pallas kernels, on_device(): call(out_kernel, 'local_out', [SMEM] + [HBM] * 5, [far((QR, 2048), F32)],...  8.58 us
    all_to_all x1, starting transfers between devices, on_device(): lax.all_to_all(key_wire, 'row', split_axis=0, concat_axis=0)  8.06 us
    pallas_call x1, Pallas kernels, on_device(): call(pair_out_kernel, 'pair_out', [SMEM] + [HBM] * 4, [far((CAP * BLK, BL...  8.01 us
    pallas_call x1, Pallas kernels, on_device(): call(back_kernel, 'back', [SMEM] + [HBM] * 10, [far((QR, BLK), F32), far(...  7.53 us
    pallas_call x1, Pallas kernels, on_device(): call(logit_kernel, 'logit', [SMEM] + [HBM] * 6, [far((32, QR), F32), far(...  7.52 us
    all_to_all x1, waiting for transfers between devices, on_device(): lax.all_to_all(key_wire, 'row', split_axis=0, concat_axis=0)  5.73 us
    all_to_all x1, waiting for transfers between devices, on_device(): lax.all_to_all(kg.reshape(N_ROW, OWN, 2 * FG), 'row', split_axis=0, conca...  5.14 us
  transfers between devices with their start and end apart: 7, of which 2 were waited for; matrix products, arithmetic and copies ran while one was open for 0% of the time, Pallas kernels for 34%

profile of v3, /device:TPU:2, one launch (start us, length us, event | category | flops | bytes accessed | tf_op | source)
XLA Modules:
  0.0 85.4 jit_solution(3423413668498465444)
XLA Ops:
  0.6 3.6 %keys.1 = (bf16[16,32,1024]{2,1,0:T(8,128)(2,1)}, f32[32,128]{1,0:T(8,128)}) custom-call(bf16[32,960]{1,0:T(8,128)(2,1)} %keys_hbm.1, f32[12,4096]{1,0:T(8,128)} %table_hbm.3, s32[1,4096]{1,0:T(1,128)} %bitcast.16), custom_call_target="tpu_custom_call" | custom-call | tf_op jit(solution)/shard_map/keys/pallas_call | solution.py:583
  4.2 8.1 %all-to-all-start = ((bf16[16,32,1024]{2,1,0:T(8,128)(2,1)}), bf16[16,32,1024]{2,1,0:T(8,128)(2,1)S(1)}, u32[]{:S(2)}, u32[]{:S(2)}) async-start(bf16[16,32,1024]{2,1,0:T(8,128)(2,1)} %get-tuple-element.27), calls=%async_computation | async-start | bytes 2097152 | tf_op jit(solution)/shard_map/all_to_all | solution.py:588
  12.3 11.9 %prep.1 = (bf16[256,512]{1,0:T(8,128)(2,1)}, bf16[256,512]{1,0:T(8,128)(2,1)}, f32[256,128]{1,0:T(8,128)}, f32[16,128]{1,0:T(8,128)}, f32[256,24,128]{2,1,0:T(8,128)}, /*index=5*/f32[2,24,128,128]{3,2,1,0:T(8,128)}) custom-call(s32[2]{0:T(128)} %bitcast.18, bf16[480,256]{1,0:T(8,128)(2,1)} %bitcast.23, bf16[12,128]{1,0:T(8,128)(2,1)} %bitcast.24, ...), custom_call_target="tpu_custom_call" | custom-call | flops 3000000000 | bytes 30000000 | tf_op jit(solution)/shard_map/prep/pallas_call | solution.py:597
  24.2 5.7 %all-to-all-done = bf16[16,32,1024]{2,1,0:T(8,128)(2,1)S(1)} async-done(((bf16[16,32,1024]{2,1,0:T(8,128)(2,1)}), bf16[16,32,1024]{2,1,0:T(8,128)(2,1)S(1)}, u32[]{:S(2)}, u32[]{:S(2)}) %all-to-all-start) | async-done | bytes 1048608 | tf_op jit(solution)/shard_map/all_to_all | solution.py:588
  29.9 0.0 copy-start.4
  29.9 1.0 %copy-done.4 = bf16[16,32,1024]{2,1,0:T(8,128)(2,1)} copy-done((bf16[16,32,1024]{2,1,0:T(8,128)(2,1)}, bf16[16,32,1024]{2,1,0:T(8,128)(2,1)S(1)}, u32[]{:S(2)}) %copy-start.4) | copy-done | bytes 1048600
  30.9 7.5 %logit.1 = (f32[32,256]{1,0:T(8,128)}, f32[2,12,128,128]{3,2,1,0:T(8,128)}, f32[2,12,128,128]{3,2,1,0:T(8,128)}, f32[8,32,256]{2,1,0:T(8,128)}) custom-call(s32[2]{0:T(128)} %bitcast.19, bf16[512,1024]{1,0:T(8,128)(2,1)} %bitcast.9, bf16[256,512]{1,0:T(8,128)(2,1)} %get-tuple-element.28.qf_hbm, bf16[256,512]{1,0:T(8,128)(2,1)} %get-tuple-element.29.df_hbm, ...), custom_call_target="tpu_custom_call" | custom-call | tf_op jit(solution)/shard_map/logit/pallas_call | solution.py:607
  38.4 4.8 %all-to-all-start.1 = ((f32[8,32,256]{2,1,0:T(8,128)}), f32[8,32,256]{2,1,0:T(8,128)S(1)}, u32[]{:S(2)}, u32[]{:S(2)}) async-start(f32[8,32,256]{2,1,0:T(8,128)} %get-tuple-element.33), calls=%async_computation.1 | async-start | bytes 524288 | tf_op jit(solution)/shard_map/all_to_all | solution.py:613
  43.3 8.6 %local_out.1.o_hbm = f32[256,2048]{1,0:T(8,128)} custom-call(s32[2]{0:T(128)} %bitcast.20, bf16[256,128,128]{2,1,0:T(8,128)(2,1)} %bitcast.13, f32[2,12,128,128]{3,2,1,0:T(8,128)} %get-tuple-element.34.logit_hbm, bf16[512,1024]{1,0:T(8,128)(2,1)} %bitcast.10, f32[32,256]{1,0:T(8,128)} %get-tuple-element.32.stat_hbm, bf16[48,512]{1,0:T(8,128)(2,1)} %constant.2.clone.e_hbm), custom_call_target="tpu_custom_call" | custom-call | flops 2000000000 | bytes 20000000 | tf_op jit(solution)/shard_map/local_out/pallas_call | solution.py:615
  51.9 0.0 all-to-all-done.1.stats_hbm
  51.9 0.0 copy-start.5
  51.9 0.7 copy-done.5
  52.6 7.5 %back.1 = (f32[256,128]{1,0:T(8,128)}, bf16[4,32,2560]{2,1,0:T(8,128)(2,1)}, bf16[512,1024]{1,0:T(8,128)(2,1)}, bf16[4,32,2560]{2,1,0:T(8,128)(2,1)}) custom-call(s32[2]{0:T(128)} %bitcast.21, f32[32,256]{1,0:T(8,128)} %get-tuple-element.32.stat_hbm, f32[8,32,256]{2,1,0:T(8,128)} %copy-done.5, bf16[512,1024]{1,0:T(8,128)(2,1)} %bitcast.11, ...), custom_call_target="tpu_custom_call" | custom-call | tf_op jit(solution)/shard_map/back/pallas_call | solution.py:622
  60.1 0.2 collective-permute-start
  60.4 3.7 %all-to-all-start.2 = ((bf16[16,32,1024]{2,1,0:T(8,128)(2,1)}), bf16[16,32,1024]{2,1,0:T(8,128)(2,1)S(1)}, u32[]{:S(2)}, u32[]{:S(2)}) async-start(bf16[16,32,1024]{2,1,0:T(8,128)(2,1)} %bitcast.15), calls=%async_computation.2 | async-start | bytes 2097152 | tf_op jit(solution)/shard_map/all_to_all | solution.py:635
  64.0 0.0 collective-permute-done.got_ref
  64.0 0.0 copy-start.1
  64.0 1.1 %copy-done.1 = bf16[4,32,2560]{2,1,0:T(8,128)(2,1)S(1)} copy-done((bf16[4,32,2560]{2,1,0:T(8,128)(2,1)S(1)}, bf16[4,32,2560]{2,1,0:T(8,128)(2,1)}, u32[]{:S(2)}) %copy-start.1) | copy-done | bytes 655384
  65.1 0.2 fold.1
  65.3 1.5 %collective-permute-start.1 = (bf16[32,2560]{1,0:T(8,128)(2,1)S(1)}, bf16[32,2560]{1,0:T(8,128)(2,1)S(1)}, u32[]{:S(2)}, u32[]{:S(2)}) collective-permute-start(bf16[32,2560]{1,0:T(8,128)(2,1)S(1)} %get-tuple-element.40), channel_id=1, source_target_pairs={{0,2},{1,3},{2,4},{3,5},{4,6},{5,7},{6,0},{7,1},{8,10},{9,11},{10,... | collective-permute-start | bytes 491528 | tf_op jit(solution)/shard_map/ppermute | solution.py:641
  66.8 0.7 collective-permute-start.2
  67.5 2.5 %collective-permute-start.3 = (bf16[32,2560]{1,0:T(8,128)(2,1)S(1)}, bf16[32,2560]{1,0:T(8,128)(2,1)S(1)}, u32[]{:S(2)}, u32[]{:S(2)}) collective-permute-start(bf16[32,2560]{1,0:T(8,128)(2,1)S(1)} %get-tuple-element.42), channel_id=1, source_target_pairs={{0,6},{1,7},{2,0},{3,1},{4,2},{5,3},{6,4},{7,5},{8,14},{9,15},{10,... | collective-permute-start | bytes 491528 | tf_op jit(solution)/shard_map/ppermute | solution.py:641
  70.1 0.0 copy-start
  70.1 0.0 copy-start.2
  70.1 0.0 copy-start.3
  70.1 8.0 %pair_out.1 = bf16[256,128,128]{2,1,0:T(8,128)(2,1)} custom-call(s32[2]{0:T(128)} %bitcast.22, f32[256,128]{1,0:T(8,128)} %get-tuple-element.48.whole_hbm, f32[2,12,128,128]{3,2,1,0:T(8,128)} %get-tuple-element.34.logit_hbm, f32[2,12,128,128]{3,2,1,0:T(8,128)} %get-tuple-element.35.da_hbm, f32[256,24,128]{2,1,0:T(8,128)} %get-tuple-element.49.dzp_hbm), custom_call_target="tpu_custom_call" | custom-call | flops 4000000000 | bytes 30000000 | tf_op jit(solution)/shard_map/pair_out/pallas_call | solution.py:645
  78.1 0.0 collective-permute-done.1.one_ref
  78.1 0.0 collective-permute-done.2.two_ref
  78.1 0.0 collective-permute-done.3.three_ref
  78.1 5.1 %all-to-all-done.2.kg_ref = bf16[16,32,1024]{2,1,0:T(8,128)(2,1)S(1)} async-done(((bf16[16,32,1024]{2,1,0:T(8,128)(2,1)}), bf16[16,32,1024]{2,1,0:T(8,128)(2,1)S(1)}, u32[]{:S(2)}, u32[]{:S(2)}) %all-to-all-start.2) | async-done | bytes 1048608 | tf_op jit(solution)/shard_map/all_to_all | solution.py:635
  83.2 0.0 copy-done
  83.2 0.0 copy-done.2
  83.2 0.0 copy-done.3
  83.3 1.9 %final.1 = (bf16[32,384]{1,0:T(8,128)(2,1)}, bf16[32,480]{1,0:T(8,128)(2,1)}, bf16[32,960]{1,0:T(8,128)(2,1)}) custom-call(bf16[16,32,1024]{2,1,0:T(8,128)(2,1)S(1)} %all-to-all-done.2.kg_ref, bf16[32,2560]{1,0:T(8,128)(2,1)S(1)} %get-tuple-element.39.own_ref, bf16[32,2560]{1,0:T(8,128)(2,1)S(1)} %collective-permute-done.1.one_ref, ...), custom_call_target="tpu_custom_call" | custom-call | tf_op jit(solution)/shard_map/final/pallas_call | solution.py:651
Async XLA Ops:
  4.2 25.7 %all-to-all-start = ((bf16[16,32,1024]{2,1,0:T(8,128)(2,1)}), bf16[16,32,1024]{2,1,0:T(8,128)(2,1)S(1)}, u32[]{:S(2)}, u32[]{:S(2)}) async-start(bf16[16,32,1024]{2,1,0:T(8,128)(2,1)} %get-tuple-element.27), calls=%async_computation | async-start | bytes 2097152 | tf_op jit(solution)/shard_map/all_to_all | solution.py:588
  29.9 1.0 %copy-start.4 = (bf16[16,32,1024]{2,1,0:T(8,128)(2,1)}, bf16[16,32,1024]{2,1,0:T(8,128)(2,1)S(1)}, u32[]{:S(2)}) copy-start(bf16[16,32,1024]{2,1,0:T(8,128)(2,1)S(1)} %all-to-all-done) | copy-start | bytes 3145732
  38.4 13.4 %all-to-all-start.1 = ((f32[8,32,256]{2,1,0:T(8,128)}), f32[8,32,256]{2,1,0:T(8,128)S(1)}, u32[]{:S(2)}, u32[]{:S(2)}) async-start(f32[8,32,256]{2,1,0:T(8,128)} %get-tuple-element.33), calls=%async_computation.1 | async-start | bytes 524288 | tf_op jit(solution)/shard_map/all_to_all | solution.py:613
  51.9 0.7 copy-start.5
  60.1 3.9 %collective-permute-start = (bf16[4,32,2560]{2,1,0:T(8,128)(2,1)}, bf16[4,32,2560]{2,1,0:T(8,128)(2,1)S(1)}, u32[]{:S(2)}, u32[]{:S(2)}) collective-permute-start(bf16[4,32,2560]{2,1,0:T(8,128)(2,1)} %get-tuple-element.38), channel_id=1, source_target_pairs={{0,1},{1,0},{2,3},{3,2},{4,5},{5,4},{6,7},{7,6},{8,9},{9,8},{10,11... | collective-permute-start | bytes 1966088 | tf_op jit(solution)/shard_map/ppermute | solution.py:636
  60.4 22.9 %all-to-all-start.2 = ((bf16[16,32,1024]{2,1,0:T(8,128)(2,1)}), bf16[16,32,1024]{2,1,0:T(8,128)(2,1)S(1)}, u32[]{:S(2)}, u32[]{:S(2)}) async-start(bf16[16,32,1024]{2,1,0:T(8,128)(2,1)} %bitcast.15), calls=%async_computation.2 | async-start | bytes 2097152 | tf_op jit(solution)/shard_map/all_to_all | solution.py:635
  64.0 1.1 %copy-start.1 = (bf16[4,32,2560]{2,1,0:T(8,128)(2,1)S(1)}, bf16[4,32,2560]{2,1,0:T(8,128)(2,1)}, u32[]{:S(2)}) copy-start(bf16[4,32,2560]{2,1,0:T(8,128)(2,1)} %get-tuple-element.37.keep_ref) | copy-start | bytes 1966084
  65.3 12.8 %collective-permute-start.1 = (bf16[32,2560]{1,0:T(8,128)(2,1)S(1)}, bf16[32,2560]{1,0:T(8,128)(2,1)S(1)}, u32[]{:S(2)}, u32[]{:S(2)}) collective-permute-start(bf16[32,2560]{1,0:T(8,128)(2,1)S(1)} %get-tuple-element.40), channel_id=1, source_target_pairs={{0,2},{1,3},{2,4},{3,5},{4,6},{5,7},{6,0},{7,1},{8,10},{9,11},{10,... | collective-permute-start | bytes 491528 | tf_op jit(solution)/shard_map/ppermute | solution.py:641
  66.8 11.3 %collective-permute-start.2 = (bf16[32,2560]{1,0:T(8,128)(2,1)S(1)}, bf16[32,2560]{1,0:T(8,128)(2,1)S(1)}, u32[]{:S(2)}, u32[]{:S(2)}) collective-permute-start(bf16[32,2560]{1,0:T(8,128)(2,1)S(1)} %get-tuple-element.41), channel_id=1, source_target_pairs={{0,4},{1,5},{2,6},{3,7},{4,0},{5,1},{6,2},{7,3},{8,12},{9,13},{10,... | collective-permute-start | bytes 491528 | tf_op jit(solution)/shard_map/ppermute | solution.py:641
  67.5 10.6 %collective-permute-start.3 = (bf16[32,2560]{1,0:T(8,128)(2,1)S(1)}, bf16[32,2560]{1,0:T(8,128)(2,1)S(1)}, u32[]{:S(2)}, u32[]{:S(2)}) collective-permute-start(bf16[32,2560]{1,0:T(8,128)(2,1)S(1)} %get-tuple-element.42), channel_id=1, source_target_pairs={{0,6},{1,7},{2,0},{3,1},{4,2},{5,3},{6,4},{7,5},{8,14},{9,15},{10,... | collective-permute-start | bytes 491528 | tf_op jit(solution)/shard_map/ppermute | solution.py:641
  70.1 13.2 %copy-start = (bf16[2016,384]{1,0:T(8,128)(2,1)S(1)}, bf16[2016,384]{1,0:T(8,128)(2,1)}, u32[]{:S(2)}) copy-start(bf16[2016,384]{1,0:T(8,128)(2,1)} %ow_hbm.3) | copy-start | bytes 4644868
  70.1 13.2 %copy-start.2 = (f32[256,128]{1,0:T(8,128)S(1)}, f32[256,128]{1,0:T(8,128)}, u32[]{:S(2)}) copy-start(f32[256,128]{1,0:T(8,128)} %get-tuple-element.43.frame_q_ref) | copy-start | bytes 393220
  70.1 13.2 %copy-start.3 = (f32[32,128]{1,0:T(8,128)S(1)}, f32[32,128]{1,0:T(8,128)}, u32[]{:S(2)}) copy-start(f32[32,128]{1,0:T(8,128)} %get-tuple-element.44.frame_k_ref) | copy-start | bytes 49156

commit v4 on v3

--- a/solution.py
+++ b/solution.py
@@ -158,8 +158,9 @@
     gk = rotate(components(keys[:, 2 * WS : 2 * WS + WP]), frame, True)
     gv = rotate(components(keys[:, 2 * WS + WP :]), frame, True)
     wire = jnp.concatenate([grouped(keys[:, :WS], gk), grouped(keys[:, WS : 2 * WS], gv)], axis=1)
-    wire_ref[...] = wire
-    copies = [pltpu.make_async_copy(wire_ref, wire_hbm.at[d], sems.at[3 + d]) for d in range(N_ROW)]
+    for d in range(N_ROW):
+        wire_ref[d] = wire
+    copies = [pltpu.make_async_copy(wire_ref.at[pl.ds(4 * d, 4)], wire_hbm.at[pl.ds(4 * d, 4)], sems.at[3 + d]) for d in range(4)]
     for copy in copies:
         copy.start()
     for copy in copies:
@@ -314,7 +315,7 @@
 
 
 def out_kernel(codes_ref, pair_ref, logit_hbm, keys_hbm, stat_hbm, e_hbm, o_hbm, held, p_ref, nz_ref, cat_ref, bd_ref, sems,
-               logit_ref, keys_ref, stat_ref, e_ref, o_ref, ins):
+               logit_ref, keys_ref, stat_ref, e_ref, o_ref, low_ref, ins):
     places = [slot_of(codes_ref, s) for s in range(CAP)]
     loads = fetch((stat_hbm, e_hbm), (stat_ref, e_ref), ins)
     for s, (_, _, kb) in enumerate(places):
@@ -364,7 +365,8 @@
         lax.fori_loop(0, BLK // STEP, some, 0)
         for h in range(H):
             o_ref[rows_of(qb), FG + h * PW : FG + (h + 1) * PW] += nz_ref[h]
-    (copy,) = fetch((o_ref,), (o_hbm,), ins)
+    low_ref[...] = o_ref[...].astype(BF16)
+    (copy,) = fetch((low_ref,), (o_hbm,), ins)
     copy.wait()
 
 
@@ -447,10 +449,10 @@
     kg_copy.start()
     o_copy.wait()
     ahi, alo = split2(whole[:, 32:48])
-    msg[:, 0:FG] = (o_ref[:, 0:FG] * (dot(ahi, e) + dot(alo, e))).astype(BF16)
+    msg[:, 0:FG] = (o_ref[:, 0:FG].astype(F32) * (dot(ahi, e) + dot(alo, e))).astype(BF16)
     for h in range(H):
         at = slice(FG + h * PW, FG + (h + 1) * PW)
-        msg[:, at] = (o_ref[:, at] * whole[:, 32 + h : 33 + h]).astype(BF16)
+        msg[:, at] = (o_ref[:, at].astype(F32) * whole[:, 32 + h : 33 + h]).astype(BF16)
     msg[:, 2048:] = dq_acc[...].astype(BF16)
     core = lax.axis_index("col") % 2
     for x in range(4):
@@ -582,7 +584,7 @@
 
     key_wire, frame_k = call(
         key_kernel, "keys", [HBM] * 3, [far((N_ROW, OWN, 2 * FG), BF16), near((OWN, BLK), F32)],
-        [pltpu.VMEM((BLK, BLK), F32), pltpu.VMEM((OWN, 2 * F), BF16), table, where, pltpu.VMEM((OWN, 2 * FG), BF16),
+        [pltpu.VMEM((BLK, BLK), F32), pltpu.VMEM((OWN, 2 * F), BF16), table, where, pltpu.VMEM((N_ROW, OWN, 2 * FG), BF16),
          DMA((3 + N_ROW,))], 56,
     )(keys, frame_table, index)
     key_all = lax.all_to_all(key_wire, "row", split_axis=0, concat_axis=0).reshape(KR, 2 * FG)
@@ -613,17 +615,17 @@
     stat_all = lax.all_to_all(stat, "col", split_axis=0, concat_axis=0)
 
     (out,) = call(
-        out_kernel, "local_out", [SMEM] + [HBM] * 5, [far((QR, 2048), F32)],
+        out_kernel, "local_out", [SMEM] + [HBM] * 5, [far((QR, 2048), BF16)],
         [held, pltpu.VMEM((H, BLK, BLK), F32), pltpu.VMEM((H, BLK, PW), F32), pltpu.VMEM((BLK, HJ), BF16),
          pltpu.VMEM((HJ, GF), BF16), sems, plane_buf, half, pltpu.VMEM((32, QR), F32), marks,
-         pltpu.VMEM((QR, 2048), F32), DMA((6,))], 56, flops=2_000_000_000, nbytes=20_000_000,
+         pltpu.VMEM((QR, 2048), F32), pltpu.VMEM((QR, 2048), BF16), DMA((6,))], 56, flops=2_000_000_000, nbytes=20_000_000,
     )(codes, tiles, logit, key_all, mine, e)
 
     whole, keep, kg, send = call(
         back_kernel, "back", [SMEM] + [HBM] * 10,
         [far((QR, BLK), F32), far((4, OWN, 2560), BF16), far((KR, 2 * FG), BF16), far((4, OWN, 2560), BF16)],
         [pltpu.VMEM((32, QR), F32), pltpu.VMEM((N_COL, 32, QR), F32), half, half, half, marks, gammas, plane_buf, plane_buf,
-         pltpu.VMEM((QR, 2048), F32), DMA((21,)),
+         pltpu.VMEM((QR, 2048), BF16), DMA((21,)),
          pltpu.VMEM((QR, BLK), F32), pltpu.VMEM((4, OWN, 2560), BF16), pltpu.VMEM((KR, 2 * FG), BF16),
          pltpu.VMEM((4, OWN, 2560), BF16), DMA((4,)),
          pltpu.VMEM((KR, 2 * FG), F32), pltpu.VMEM((BLK, HJ), BF16), pltpu.VMEM((HJ, BLK), BF16),

time: 85.9 us -> 85.5 us (level)
  transfers between devices with their start and end apart: 7 -> 7, of which waited for: 2 -> 2; matrix products, arithmetic and copies ran while one was open for 0% -> 0% of each run, Pallas kernels for 34% -> 33%
where the time goes in v4:
time: 85.5 us; the launch traced here: 85 us
  Pallas kernels  48.8 us (57%)
  starting transfers between devices  21.6 us (25%)
  waiting for transfers between devices  10.9 us (13%)
  local copies, waits for them, and re-layouts  2.76 us (3%)
  between operations  0.92 us (1%)
    pallas_call x1, Pallas kernels, on_device(): call(prep_kernel, 'prep', [SMEM] + [HBM] * 8, [far((QR, FG), BF16), far((...  11.9 us
    pallas_call x1, Pallas kernels, on_device(): call(out_kernel, 'local_out', [SMEM] + [HBM] * 5, [far((QR, 2048), BF16)]...  8.33 us
    all_to_all x1, starting transfers between devices, on_device(): lax.all_to_all(key_wire, 'row', split_axis=0, concat_axis=0)  8.06 us
    pallas_call x1, Pallas kernels, on_device(): call(pair_out_kernel, 'pair_out', [SMEM] + [HBM] * 4, [far((CAP * BLK, BL...  8.01 us
    pallas_call x1, Pallas kernels, on_device(): call(logit_kernel, 'logit', [SMEM] + [HBM] * 6, [far((32, QR), F32), far(...  7.52 us
    pallas_call x1, Pallas kernels, on_device(): call(back_kernel, 'back', [SMEM] + [HBM] * 10, [far((QR, BLK), F32), far(...  7.29 us
    all_to_all x1, waiting for transfers between devices, on_device(): lax.all_to_all(key_wire, 'row', split_axis=0, concat_axis=0)  5.74 us
    all_to_all x1, waiting for transfers between devices, on_device(): lax.all_to_all(kg.reshape(N_ROW, OWN, 2 * FG), 'row', split_axis=0, conca...  5.16 us
  transfers between devices with their start and end apart: 7, of which 2 were waited for; matrix products, arithmetic and copies ran while one was open for 0% of the time, Pallas kernels for 33%

profile of v4, /device:TPU:2, one launch (start us, length us, event | category | flops | bytes accessed | tf_op | source)
XLA Modules:
  0.0 85.0 jit_solution(8018288827377342637)
XLA Ops:
  0.6 3.7 %keys.1 = (bf16[16,32,1024]{2,1,0:T(8,128)(2,1)}, f32[32,128]{1,0:T(8,128)}) custom-call(bf16[32,960]{1,0:T(8,128)(2,1)} %keys_hbm.1, f32[12,4096]{1,0:T(8,128)} %table_hbm.3, s32[1,4096]{1,0:T(1,128)} %bitcast.16), custom_call_target="tpu_custom_call" | custom-call | tf_op jit(solution)/shard_map/keys/pallas_call | solution.py:585
  4.3 8.1 %all-to-all-start = ((bf16[16,32,1024]{2,1,0:T(8,128)(2,1)}), bf16[16,32,1024]{2,1,0:T(8,128)(2,1)S(1)}, u32[]{:S(2)}, u32[]{:S(2)}) async-start(bf16[16,32,1024]{2,1,0:T(8,128)(2,1)} %get-tuple-element.27), calls=%async_computation | async-start | bytes 2097152 | tf_op jit(solution)/shard_map/all_to_all | solution.py:590
  12.4 11.9 %prep.1 = (bf16[256,512]{1,0:T(8,128)(2,1)}, bf16[256,512]{1,0:T(8,128)(2,1)}, f32[256,128]{1,0:T(8,128)}, f32[16,128]{1,0:T(8,128)}, f32[256,24,128]{2,1,0:T(8,128)}, /*index=5*/f32[2,24,128,128]{3,2,1,0:T(8,128)}) custom-call(s32[2]{0:T(128)} %bitcast.18, bf16[480,256]{1,0:T(8,128)(2,1)} %bitcast.23, bf16[12,128]{1,0:T(8,128)(2,1)} %bitcast.24, ...), custom_call_target="tpu_custom_call" | custom-call | flops 3000000000 | bytes 30000000 | tf_op jit(solution)/shard_map/prep/pallas_call | solution.py:599
  24.3 5.7 %all-to-all-done = bf16[16,32,1024]{2,1,0:T(8,128)(2,1)S(1)} async-done(((bf16[16,32,1024]{2,1,0:T(8,128)(2,1)}), bf16[16,32,1024]{2,1,0:T(8,128)(2,1)S(1)}, u32[]{:S(2)}, u32[]{:S(2)}) %all-to-all-start) | async-done | bytes 1048608 | tf_op jit(solution)/shard_map/all_to_all | solution.py:590
  30.0 0.0 copy-start.4
  30.0 1.0 %copy-done.4 = bf16[16,32,1024]{2,1,0:T(8,128)(2,1)} copy-done((bf16[16,32,1024]{2,1,0:T(8,128)(2,1)}, bf16[16,32,1024]{2,1,0:T(8,128)(2,1)S(1)}, u32[]{:S(2)}) %copy-start.4) | copy-done | bytes 1048600
  31.0 7.5 %logit.1 = (f32[32,256]{1,0:T(8,128)}, f32[2,12,128,128]{3,2,1,0:T(8,128)}, f32[2,12,128,128]{3,2,1,0:T(8,128)}, f32[8,32,256]{2,1,0:T(8,128)}) custom-call(s32[2]{0:T(128)} %bitcast.19, bf16[512,1024]{1,0:T(8,128)(2,1)} %bitcast.9, bf16[256,512]{1,0:T(8,128)(2,1)} %get-tuple-element.28.qf_hbm, bf16[256,512]{1,0:T(8,128)(2,1)} %get-tuple-element.29.df_hbm, ...), custom_call_target="tpu_custom_call" | custom-call | tf_op jit(solution)/shard_map/logit/pallas_call | solution.py:609
  38.5 4.8 %all-to-all-start.1 = ((f32[8,32,256]{2,1,0:T(8,128)}), f32[8,32,256]{2,1,0:T(8,128)S(1)}, u32[]{:S(2)}, u32[]{:S(2)}) async-start(f32[8,32,256]{2,1,0:T(8,128)} %get-tuple-element.33), calls=%async_computation.1 | async-start | bytes 524288 | tf_op jit(solution)/shard_map/all_to_all | solution.py:615
  43.4 8.3 %local_out.1.o_hbm = bf16[256,2048]{1,0:T(8,128)(2,1)} custom-call(s32[2]{0:T(128)} %bitcast.20, bf16[256,128,128]{2,1,0:T(8,128)(2,1)} %bitcast.13, f32[2,12,128,128]{3,2,1,0:T(8,128)} %get-tuple-element.34.logit_hbm, bf16[512,1024]{1,0:T(8,128)(2,1)} %bitcast.10, f32[32,256]{1,0:T(8,128)} %get-tuple-element.32.stat_hbm, bf16[48,512]{1,0:T(8,128)(2,1)} %constant.2.clone.e_hbm), custom_call_target="tpu_custom_call" | custom-call | flops 2000000000 | bytes 20000000 | tf_op jit(solution)/shard_map/local_out/pallas_call | solution.py:617
  51.7 0.0 all-to-all-done.1.stats_hbm
  51.7 0.0 copy-start.5
  51.7 0.7 copy-done.5
  52.4 7.3 %back.1 = (f32[256,128]{1,0:T(8,128)}, bf16[4,32,2560]{2,1,0:T(8,128)(2,1)}, bf16[512,1024]{1,0:T(8,128)(2,1)}, bf16[4,32,2560]{2,1,0:T(8,128)(2,1)}) custom-call(s32[2]{0:T(128)} %bitcast.21, f32[32,256]{1,0:T(8,128)} %get-tuple-element.32.stat_hbm, f32[8,32,256]{2,1,0:T(8,128)} %copy-done.5, bf16[512,1024]{1,0:T(8,128)(2,1)} %bitcast.11, ...), custom_call_target="tpu_custom_call" | custom-call | tf_op jit(solution)/shard_map/back/pallas_call | solution.py:624
  59.7 0.2 collective-permute-start
  59.9 3.7 %all-to-all-start.2 = ((bf16[16,32,1024]{2,1,0:T(8,128)(2,1)}), bf16[16,32,1024]{2,1,0:T(8,128)(2,1)S(1)}, u32[]{:S(2)}, u32[]{:S(2)}) async-start(bf16[16,32,1024]{2,1,0:T(8,128)(2,1)} %bitcast.15), calls=%async_computation.2 | async-start | bytes 2097152 | tf_op jit(solution)/shard_map/all_to_all | solution.py:637
  63.6 0.0 collective-permute-done.got_ref
  63.6 0.0 copy-start.1
  63.6 1.1 %copy-done.1 = bf16[4,32,2560]{2,1,0:T(8,128)(2,1)S(1)} copy-done((bf16[4,32,2560]{2,1,0:T(8,128)(2,1)S(1)}, bf16[4,32,2560]{2,1,0:T(8,128)(2,1)}, u32[]{:S(2)}) %copy-start.1) | copy-done | bytes 655384
  64.7 0.2 fold.1
  64.9 1.5 %collective-permute-start.1 = (bf16[32,2560]{1,0:T(8,128)(2,1)S(1)}, bf16[32,2560]{1,0:T(8,128)(2,1)S(1)}, u32[]{:S(2)}, u32[]{:S(2)}) collective-permute-start(bf16[32,2560]{1,0:T(8,128)(2,1)S(1)} %get-tuple-element.40), channel_id=1, source_target_pairs={{0,2},{1,3},{2,4},{3,5},{4,6},{5,7},{6,0},{7,1},{8,10},{9,11},{10,... | collective-permute-start | bytes 491528 | tf_op jit(solution)/shard_map/ppermute | solution.py:643
  66.4 0.9 %collective-permute-start.2 = (bf16[32,2560]{1,0:T(8,128)(2,1)S(1)}, bf16[32,2560]{1,0:T(8,128)(2,1)S(1)}, u32[]{:S(2)}, u32[]{:S(2)}) collective-permute-start(bf16[32,2560]{1,0:T(8,128)(2,1)S(1)} %get-tuple-element.41), channel_id=1, source_target_pairs={{0,4},{1,5},{2,6},{3,7},{4,0},{5,1},{6,2},{7,3},{8,12},{9,13},{10,... | collective-permute-start | bytes 491528 | tf_op jit(solution)/shard_map/ppermute | solution.py:643
  67.3 2.3 %collective-permute-start.3 = (bf16[32,2560]{1,0:T(8,128)(2,1)S(1)}, bf16[32,2560]{1,0:T(8,128)(2,1)S(1)}, u32[]{:S(2)}, u32[]{:S(2)}) collective-permute-start(bf16[32,2560]{1,0:T(8,128)(2,1)S(1)} %get-tuple-element.42), channel_id=1, source_target_pairs={{0,6},{1,7},{2,0},{3,1},{4,2},{5,3},{6,4},{7,5},{8,14},{9,15},{10,... | collective-permute-start | bytes 491528 | tf_op jit(solution)/shard_map/ppermute | solution.py:643
  69.6 0.0 copy-start
  69.7 0.0 copy-start.2
  69.7 0.0 copy-start.3
  69.7 8.0 %pair_out.1 = bf16[256,128,128]{2,1,0:T(8,128)(2,1)} custom-call(s32[2]{0:T(128)} %bitcast.22, f32[256,128]{1,0:T(8,128)} %get-tuple-element.48.whole_hbm, f32[2,12,128,128]{3,2,1,0:T(8,128)} %get-tuple-element.34.logit_hbm, f32[2,12,128,128]{3,2,1,0:T(8,128)} %get-tuple-element.35.da_hbm, f32[256,24,128]{2,1,0:T(8,128)} %get-tuple-element.49.dzp_hbm), custom_call_target="tpu_custom_call" | custom-call | flops 4000000000 | bytes 30000000 | tf_op jit(solution)/shard_map/pair_out/pallas_call | solution.py:647
  77.7 0.0 collective-permute-done.1.one_ref
  77.7 0.0 collective-permute-done.2.two_ref
  77.7 0.0 collective-permute-done.3.three_ref
  77.7 5.2 %all-to-all-done.2.kg_ref = bf16[16,32,1024]{2,1,0:T(8,128)(2,1)S(1)} async-done(((bf16[16,32,1024]{2,1,0:T(8,128)(2,1)}), bf16[16,32,1024]{2,1,0:T(8,128)(2,1)S(1)}, u32[]{:S(2)}, u32[]{:S(2)}) %all-to-all-start.2) | async-done | bytes 1048608 | tf_op jit(solution)/shard_map/all_to_all | solution.py:637
  82.9 0.0 copy-done
  82.9 0.0 copy-done.2
  82.9 0.0 copy-done.3
  82.9 1.9 %final.1 = (bf16[32,384]{1,0:T(8,128)(2,1)}, bf16[32,480]{1,0:T(8,128)(2,1)}, bf16[32,960]{1,0:T(8,128)(2,1)}) custom-call(bf16[16,32,1024]{2,1,0:T(8,128)(2,1)S(1)} %all-to-all-done.2.kg_ref, bf16[32,2560]{1,0:T(8,128)(2,1)S(1)} %get-tuple-element.39.own_ref, bf16[32,2560]{1,0:T(8,128)(2,1)S(1)} %collective-permute-done.1.one_ref, ...), custom_call_target="tpu_custom_call" | custom-call | tf_op jit(solution)/shard_map/final/pallas_call | solution.py:653
Async XLA Ops:
  4.3 25.7 %all-to-all-start = ((bf16[16,32,1024]{2,1,0:T(8,128)(2,1)}), bf16[16,32,1024]{2,1,0:T(8,128)(2,1)S(1)}, u32[]{:S(2)}, u32[]{:S(2)}) async-start(bf16[16,32,1024]{2,1,0:T(8,128)(2,1)} %get-tuple-element.27), calls=%async_computation | async-start | bytes 2097152 | tf_op jit(solution)/shard_map/all_to_all | solution.py:590
  30.0 1.0 %copy-start.4 = (bf16[16,32,1024]{2,1,0:T(8,128)(2,1)}, bf16[16,32,1024]{2,1,0:T(8,128)(2,1)S(1)}, u32[]{:S(2)}) copy-start(bf16[16,32,1024]{2,1,0:T(8,128)(2,1)S(1)} %all-to-all-done) | copy-start | bytes 3145732
  38.5 13.2 %all-to-all-start.1 = ((f32[8,32,256]{2,1,0:T(8,128)}), f32[8,32,256]{2,1,0:T(8,128)S(1)}, u32[]{:S(2)}, u32[]{:S(2)}) async-start(f32[8,32,256]{2,1,0:T(8,128)} %get-tuple-element.33), calls=%async_computation.1 | async-start | bytes 524288 | tf_op jit(solution)/shard_map/all_to_all | solution.py:615
  51.7 0.7 copy-start.5
  59.7 3.9 %collective-permute-start = (bf16[4,32,2560]{2,1,0:T(8,128)(2,1)}, bf16[4,32,2560]{2,1,0:T(8,128)(2,1)S(1)}, u32[]{:S(2)}, u32[]{:S(2)}) collective-permute-start(bf16[4,32,2560]{2,1,0:T(8,128)(2,1)} %get-tuple-element.38), channel_id=1, source_target_pairs={{0,1},{1,0},{2,3},{3,2},{4,5},{5,4},{6,7},{7,6},{8,9},{9,8},{10,11... | collective-permute-start | bytes 1966088 | tf_op jit(solution)/shard_map/ppermute | solution.py:638
  59.9 22.9 %all-to-all-start.2 = ((bf16[16,32,1024]{2,1,0:T(8,128)(2,1)}), bf16[16,32,1024]{2,1,0:T(8,128)(2,1)S(1)}, u32[]{:S(2)}, u32[]{:S(2)}) async-start(bf16[16,32,1024]{2,1,0:T(8,128)(2,1)} %bitcast.15), calls=%async_computation.2 | async-start | bytes 2097152 | tf_op jit(solution)/shard_map/all_to_all | solution.py:637
  63.6 1.1 %copy-start.1 = (bf16[4,32,2560]{2,1,0:T(8,128)(2,1)S(1)}, bf16[4,32,2560]{2,1,0:T(8,128)(2,1)}, u32[]{:S(2)}) copy-start(bf16[4,32,2560]{2,1,0:T(8,128)(2,1)} %get-tuple-element.37.keep_ref) | copy-start | bytes 1966084
  64.9 12.8 %collective-permute-start.1 = (bf16[32,2560]{1,0:T(8,128)(2,1)S(1)}, bf16[32,2560]{1,0:T(8,128)(2,1)S(1)}, u32[]{:S(2)}, u32[]{:S(2)}) collective-permute-start(bf16[32,2560]{1,0:T(8,128)(2,1)S(1)} %get-tuple-element.40), channel_id=1, source_target_pairs={{0,2},{1,3},{2,4},{3,5},{4,6},{5,7},{6,0},{7,1},{8,10},{9,11},{10,... | collective-permute-start | bytes 491528 | tf_op jit(solution)/shard_map/ppermute | solution.py:643
  66.4 11.3 %collective-permute-start.2 = (bf16[32,2560]{1,0:T(8,128)(2,1)S(1)}, bf16[32,2560]{1,0:T(8,128)(2,1)S(1)}, u32[]{:S(2)}, u32[]{:S(2)}) collective-permute-start(bf16[32,2560]{1,0:T(8,128)(2,1)S(1)} %get-tuple-element.41), channel_id=1, source_target_pairs={{0,4},{1,5},{2,6},{3,7},{4,0},{5,1},{6,2},{7,3},{8,12},{9,13},{10,... | collective-permute-start | bytes 491528 | tf_op jit(solution)/shard_map/ppermute | solution.py:643
  67.3 10.4 %collective-permute-start.3 = (bf16[32,2560]{1,0:T(8,128)(2,1)S(1)}, bf16[32,2560]{1,0:T(8,128)(2,1)S(1)}, u32[]{:S(2)}, u32[]{:S(2)}) collective-permute-start(bf16[32,2560]{1,0:T(8,128)(2,1)S(1)} %get-tuple-element.42), channel_id=1, source_target_pairs={{0,6},{1,7},{2,0},{3,1},{4,2},{5,3},{6,4},{7,5},{8,14},{9,15},{10,... | collective-permute-start | bytes 491528 | tf_op jit(solution)/shard_map/ppermute | solution.py:643
  69.6 13.2 %copy-start = (bf16[2016,384]{1,0:T(8,128)(2,1)S(1)}, bf16[2016,384]{1,0:T(8,128)(2,1)}, u32[]{:S(2)}) copy-start(bf16[2016,384]{1,0:T(8,128)(2,1)} %ow_hbm.3) | copy-start | bytes 4644868
  69.7 13.2 %copy-start.2 = (f32[256,128]{1,0:T(8,128)S(1)}, f32[256,128]{1,0:T(8,128)}, u32[]{:S(2)}) copy-start(f32[256,128]{1,0:T(8,128)} %get-tuple-element.43.frame_q_ref) | copy-start | bytes 393220
  69.7 13.2 %copy-start.3 = (f32[32,128]{1,0:T(8,128)S(1)}, f32[32,128]{1,0:T(8,128)}, u32[]{:S(2)}) copy-start(f32[32,128]{1,0:T(8,128)} %get-tuple-element.44.frame_k_ref) | copy-start | bytes 49156

commit v5 on v4

--- a/solution.py
+++ b/solution.py
@@ -41,7 +41,7 @@
 GF = 256
 FG = G * GF
 CHUNK = 32
-STEP = 64
+STEP = 128
 
 NN = (((1,), (0,)), ((), ()))
 NT = (((1,), (1,)), ((), ()))

time: 85.5 us -> 85.2 us (level)
  transfers between devices with their start and end apart: 7 -> 7, of which waited for: 2 -> 2; matrix products, arithmetic and copies ran while one was open for 0% -> 0% of each run, Pallas kernels for 33% -> 34%
where the time goes in v5:
time: 85.2 us; the launch traced here: 84.7 us
  Pallas kernels  49 us (58%)
  starting transfers between devices  21.6 us (25%)
  waiting for transfers between devices  10.4 us (12%)
  local copies, waits for them, and re-layouts  2.76 us (3%)
  between operations  0.94 us (1%)
    pallas_call x1, Pallas kernels, on_device(): call(prep_kernel, 'prep', [SMEM] + [HBM] * 8, [far((QR, FG), BF16), far((...  11.9 us
    pallas_call x1, Pallas kernels, on_device(): call(pair_out_kernel, 'pair_out', [SMEM] + [HBM] * 4, [far((CAP * BLK, BL...  8.4 us
    pallas_call x1, Pallas kernels, on_device(): call(out_kernel, 'local_out', [SMEM] + [HBM] * 5, [far((QR, 2048), BF16)]...  8.07 us
    all_to_all x1, starting transfers between devices, on_device(): lax.all_to_all(key_wire, 'row', split_axis=0, concat_axis=0)  8.06 us
    pallas_call x1, Pallas kernels, on_device(): call(logit_kernel, 'logit', [SMEM] + [HBM] * 6, [far((32, QR), F32), far(...  7.52 us
    pallas_call x1, Pallas kernels, on_device(): call(back_kernel, 'back', [SMEM] + [HBM] * 10, [far((QR, BLK), F32), far(...  7.29 us
    all_to_all x1, waiting for transfers between devices, on_device(): lax.all_to_all(key_wire, 'row', split_axis=0, concat_axis=0)  5.71 us
    all_to_all x1, starting transfers between devices, on_device(): stat_all = lax.all_to_all(stat, 'col', split_axis=0, concat_axis=0)  4.84 us
  transfers between devices with their start and end apart: 7, of which 2 were waited for; matrix products, arithmetic and copies ran while one was open for 0% of the time, Pallas kernels for 34%

profile of v5, /device:TPU:2, one launch (start us, length us, event | category | flops | bytes accessed | tf_op | source)
XLA Modules:
  0.0 84.7 jit_solution(8435937850047191186)
XLA Ops:
  0.6 3.7 %keys.1 = (bf16[16,32,1024]{2,1,0:T(8,128)(2,1)}, f32[32,128]{1,0:T(8,128)}) custom-call(bf16[32,960]{1,0:T(8,128)(2,1)} %keys_hbm.1, f32[12,4096]{1,0:T(8,128)} %table_hbm.3, s32[1,4096]{1,0:T(1,128)} %bitcast.16), custom_call_target="tpu_custom_call" | custom-call | tf_op jit(solution)/shard_map/keys/pallas_call | solution.py:585
  4.3 8.1 %all-to-all-start = ((bf16[16,32,1024]{2,1,0:T(8,128)(2,1)}), bf16[16,32,1024]{2,1,0:T(8,128)(2,1)S(1)}, u32[]{:S(2)}, u32[]{:S(2)}) async-start(bf16[16,32,1024]{2,1,0:T(8,128)(2,1)} %get-tuple-element.27), calls=%async_computation | async-start | bytes 2097152 | tf_op jit(solution)/shard_map/all_to_all | solution.py:590
  12.4 11.9 %prep.1 = (bf16[256,512]{1,0:T(8,128)(2,1)}, bf16[256,512]{1,0:T(8,128)(2,1)}, f32[256,128]{1,0:T(8,128)}, f32[16,128]{1,0:T(8,128)}, f32[256,24,128]{2,1,0:T(8,128)}, /*index=5*/f32[2,24,128,128]{3,2,1,0:T(8,128)}) custom-call(s32[2]{0:T(128)} %bitcast.18, bf16[480,256]{1,0:T(8,128)(2,1)} %bitcast.23, bf16[12,128]{1,0:T(8,128)(2,1)} %bitcast.24, ...), custom_call_target="tpu_custom_call" | custom-call | flops 3000000000 | bytes 30000000 | tf_op jit(solution)/shard_map/prep/pallas_call | solution.py:599
  24.3 5.7 %all-to-all-done = bf16[16,32,1024]{2,1,0:T(8,128)(2,1)S(1)} async-done(((bf16[16,32,1024]{2,1,0:T(8,128)(2,1)}), bf16[16,32,1024]{2,1,0:T(8,128)(2,1)S(1)}, u32[]{:S(2)}, u32[]{:S(2)}) %all-to-all-start) | async-done | bytes 1048608 | tf_op jit(solution)/shard_map/all_to_all | solution.py:590
  30.0 0.0 copy-start.4
  30.0 1.0 %copy-done.4 = bf16[16,32,1024]{2,1,0:T(8,128)(2,1)} copy-done((bf16[16,32,1024]{2,1,0:T(8,128)(2,1)}, bf16[16,32,1024]{2,1,0:T(8,128)(2,1)S(1)}, u32[]{:S(2)}) %copy-start.4) | copy-done | bytes 1048600
  31.0 7.5 %logit.1 = (f32[32,256]{1,0:T(8,128)}, f32[2,12,128,128]{3,2,1,0:T(8,128)}, f32[2,12,128,128]{3,2,1,0:T(8,128)}, f32[8,32,256]{2,1,0:T(8,128)}) custom-call(s32[2]{0:T(128)} %bitcast.19, bf16[512,1024]{1,0:T(8,128)(2,1)} %bitcast.9, bf16[256,512]{1,0:T(8,128)(2,1)} %get-tuple-element.28.qf_hbm, bf16[256,512]{1,0:T(8,128)(2,1)} %get-tuple-element.29.df_hbm, ...), custom_call_target="tpu_custom_call" | custom-call | tf_op jit(solution)/shard_map/logit/pallas_call | solution.py:609
  38.5 4.8 %all-to-all-start.1 = ((f32[8,32,256]{2,1,0:T(8,128)}), f32[8,32,256]{2,1,0:T(8,128)S(1)}, u32[]{:S(2)}, u32[]{:S(2)}) async-start(f32[8,32,256]{2,1,0:T(8,128)} %get-tuple-element.33), calls=%async_computation.1 | async-start | bytes 524288 | tf_op jit(solution)/shard_map/all_to_all | solution.py:615
  43.4 8.1 %local_out.1.o_hbm = bf16[256,2048]{1,0:T(8,128)(2,1)} custom-call(s32[2]{0:T(128)} %bitcast.20, bf16[256,128,128]{2,1,0:T(8,128)(2,1)} %bitcast.13, f32[2,12,128,128]{3,2,1,0:T(8,128)} %get-tuple-element.34.logit_hbm, bf16[512,1024]{1,0:T(8,128)(2,1)} %bitcast.10, f32[32,256]{1,0:T(8,128)} %get-tuple-element.32.stat_hbm, bf16[48,512]{1,0:T(8,128)(2,1)} %constant.2.clone.e_hbm), custom_call_target="tpu_custom_call" | custom-call | flops 2000000000 | bytes 20000000 | tf_op jit(solution)/shard_map/local_out/pallas_call | solution.py:617
  51.5 0.0 all-to-all-done.1.stats_hbm
  51.5 0.0 copy-start.5
  51.5 0.7 copy-done.5
  52.2 7.3 %back.1 = (f32[256,128]{1,0:T(8,128)}, bf16[4,32,2560]{2,1,0:T(8,128)(2,1)}, bf16[512,1024]{1,0:T(8,128)(2,1)}, bf16[4,32,2560]{2,1,0:T(8,128)(2,1)}) custom-call(s32[2]{0:T(128)} %bitcast.21, f32[32,256]{1,0:T(8,128)} %get-tuple-element.32.stat_hbm, f32[8,32,256]{2,1,0:T(8,128)} %copy-done.5, bf16[512,1024]{1,0:T(8,128)(2,1)} %bitcast.11, ...), custom_call_target="tpu_custom_call" | custom-call | tf_op jit(solution)/shard_map/back/pallas_call | solution.py:624
  59.5 0.2 collective-permute-start
  59.7 3.7 %all-to-all-start.2 = ((bf16[16,32,1024]{2,1,0:T(8,128)(2,1)}), bf16[16,32,1024]{2,1,0:T(8,128)(2,1)S(1)}, u32[]{:S(2)}, u32[]{:S(2)}) async-start(bf16[16,32,1024]{2,1,0:T(8,128)(2,1)} %bitcast.15), calls=%async_computation.2 | async-start | bytes 2097152 | tf_op jit(solution)/shard_map/all_to_all | solution.py:637
  63.4 0.0 collective-permute-done.got_ref
  63.4 0.0 copy-start.1
  63.4 1.1 %copy-done.1 = bf16[4,32,2560]{2,1,0:T(8,128)(2,1)S(1)} copy-done((bf16[4,32,2560]{2,1,0:T(8,128)(2,1)S(1)}, bf16[4,32,2560]{2,1,0:T(8,128)(2,1)}, u32[]{:S(2)}) %copy-start.1) | copy-done | bytes 655384
  64.5 0.2 fold.1
  64.6 1.5 %collective-permute-start.1 = (bf16[32,2560]{1,0:T(8,128)(2,1)S(1)}, bf16[32,2560]{1,0:T(8,128)(2,1)S(1)}, u32[]{:S(2)}, u32[]{:S(2)}) collective-permute-start(bf16[32,2560]{1,0:T(8,128)(2,1)S(1)} %get-tuple-element.40), channel_id=1, source_target_pairs={{0,2},{1,3},{2,4},{3,5},{4,6},{5,7},{6,0},{7,1},{8,10},{9,11},{10,... | collective-permute-start | bytes 491528 | tf_op jit(solution)/shard_map/ppermute | solution.py:643
  66.2 0.9 %collective-permute-start.2 = (bf16[32,2560]{1,0:T(8,128)(2,1)S(1)}, bf16[32,2560]{1,0:T(8,128)(2,1)S(1)}, u32[]{:S(2)}, u32[]{:S(2)}) collective-permute-start(bf16[32,2560]{1,0:T(8,128)(2,1)S(1)} %get-tuple-element.41), channel_id=1, source_target_pairs={{0,4},{1,5},{2,6},{3,7},{4,0},{5,1},{6,2},{7,3},{8,12},{9,13},{10,... | collective-permute-start | bytes 491528 | tf_op jit(solution)/shard_map/ppermute | solution.py:643
  67.1 2.3 %collective-permute-start.3 = (bf16[32,2560]{1,0:T(8,128)(2,1)S(1)}, bf16[32,2560]{1,0:T(8,128)(2,1)S(1)}, u32[]{:S(2)}, u32[]{:S(2)}) collective-permute-start(bf16[32,2560]{1,0:T(8,128)(2,1)S(1)} %get-tuple-element.42), channel_id=1, source_target_pairs={{0,6},{1,7},{2,0},{3,1},{4,2},{5,3},{6,4},{7,5},{8,14},{9,15},{10,... | collective-permute-start | bytes 491528 | tf_op jit(solution)/shard_map/ppermute | solution.py:643
  69.4 0.0 copy-start
  69.4 0.0 copy-start.2
  69.4 0.0 copy-start.3
  69.4 8.4 %pair_out.1 = bf16[256,128,128]{2,1,0:T(8,128)(2,1)} custom-call(s32[2]{0:T(128)} %bitcast.22, f32[256,128]{1,0:T(8,128)} %get-tuple-element.48.whole_hbm, f32[2,12,128,128]{3,2,1,0:T(8,128)} %get-tuple-element.34.logit_hbm, f32[2,12,128,128]{3,2,1,0:T(8,128)} %get-tuple-element.35.da_hbm, f32[256,24,128]{2,1,0:T(8,128)} %get-tuple-element.49.dzp_hbm), custom_call_target="tpu_custom_call" | custom-call | flops 4000000000 | bytes 30000000 | tf_op jit(solution)/shard_map/pair_out/pallas_call | solution.py:647
  77.8 0.0 collective-permute-done.1.one_ref
  77.8 0.0 collective-permute-done.2.two_ref
  77.8 0.0 collective-permute-done.3.three_ref
  77.8 4.7 %all-to-all-done.2.kg_ref = bf16[16,32,1024]{2,1,0:T(8,128)(2,1)S(1)} async-done(((bf16[16,32,1024]{2,1,0:T(8,128)(2,1)}), bf16[16,32,1024]{2,1,0:T(8,128)(2,1)S(1)}, u32[]{:S(2)}, u32[]{:S(2)}) %all-to-all-start.2) | async-done | bytes 1048608 | tf_op jit(solution)/shard_map/all_to_all | solution.py:637
  82.6 0.0 copy-done
  82.6 0.0 copy-done.2
  82.6 0.0 copy-done.3
  82.6 1.9 %final.1 = (bf16[32,384]{1,0:T(8,128)(2,1)}, bf16[32,480]{1,0:T(8,128)(2,1)}, bf16[32,960]{1,0:T(8,128)(2,1)}) custom-call(bf16[16,32,1024]{2,1,0:T(8,128)(2,1)S(1)} %all-to-all-done.2.kg_ref, bf16[32,2560]{1,0:T(8,128)(2,1)S(1)} %get-tuple-element.39.own_ref, bf16[32,2560]{1,0:T(8,128)(2,1)S(1)} %collective-permute-done.1.one_ref, ...), custom_call_target="tpu_custom_call" | custom-call | tf_op jit(solution)/shard_map/final/pallas_call | solution.py:653
Async XLA Ops:
  4.3 25.7 %all-to-all-start = ((bf16[16,32,1024]{2,1,0:T(8,128)(2,1)}), bf16[16,32,1024]{2,1,0:T(8,128)(2,1)S(1)}, u32[]{:S(2)}, u32[]{:S(2)}) async-start(bf16[16,32,1024]{2,1,0:T(8,128)(2,1)} %get-tuple-element.27), calls=%async_computation | async-start | bytes 2097152 | tf_op jit(solution)/shard_map/all_to_all | solution.py:590
  30.0 1.0 %copy-start.4 = (bf16[16,32,1024]{2,1,0:T(8,128)(2,1)}, bf16[16,32,1024]{2,1,0:T(8,128)(2,1)S(1)}, u32[]{:S(2)}) copy-start(bf16[16,32,1024]{2,1,0:T(8,128)(2,1)S(1)} %all-to-all-done) | copy-start | bytes 3145732
  38.5 12.9 %all-to-all-start.1 = ((f32[8,32,256]{2,1,0:T(8,128)}), f32[8,32,256]{2,1,0:T(8,128)S(1)}, u32[]{:S(2)}, u32[]{:S(2)}) async-start(f32[8,32,256]{2,1,0:T(8,128)} %get-tuple-element.33), calls=%async_computation.1 | async-start | bytes 524288 | tf_op jit(solution)/shard_map/all_to_all | solution.py:615
  51.5 0.7 copy-start.5
  59.5 3.9 %collective-permute-start = (bf16[4,32,2560]{2,1,0:T(8,128)(2,1)}, bf16[4,32,2560]{2,1,0:T(8,128)(2,1)S(1)}, u32[]{:S(2)}, u32[]{:S(2)}) collective-permute-start(bf16[4,32,2560]{2,1,0:T(8,128)(2,1)} %get-tuple-element.38), channel_id=1, source_target_pairs={{0,1},{1,0},{2,3},{3,2},{4,5},{5,4},{6,7},{7,6},{8,9},{9,8},{10,11... | collective-permute-start | bytes 1966088 | tf_op jit(solution)/shard_map/ppermute | solution.py:638
  59.7 22.9 %all-to-all-start.2 = ((bf16[16,32,1024]{2,1,0:T(8,128)(2,1)}), bf16[16,32,1024]{2,1,0:T(8,128)(2,1)S(1)}, u32[]{:S(2)}, u32[]{:S(2)}) async-start(bf16[16,32,1024]{2,1,0:T(8,128)(2,1)} %bitcast.15), calls=%async_computation.2 | async-start | bytes 2097152 | tf_op jit(solution)/shard_map/all_to_all | solution.py:637
  63.4 1.1 %copy-start.1 = (bf16[4,32,2560]{2,1,0:T(8,128)(2,1)S(1)}, bf16[4,32,2560]{2,1,0:T(8,128)(2,1)}, u32[]{:S(2)}) copy-start(bf16[4,32,2560]{2,1,0:T(8,128)(2,1)} %get-tuple-element.37.keep_ref) | copy-start | bytes 1966084
  64.6 13.2 %collective-permute-start.1 = (bf16[32,2560]{1,0:T(8,128)(2,1)S(1)}, bf16[32,2560]{1,0:T(8,128)(2,1)S(1)}, u32[]{:S(2)}, u32[]{:S(2)}) collective-permute-start(bf16[32,2560]{1,0:T(8,128)(2,1)S(1)} %get-tuple-element.40), channel_id=1, source_target_pairs={{0,2},{1,3},{2,4},{3,5},{4,6},{5,7},{6,0},{7,1},{8,10},{9,11},{10,... | collective-permute-start | bytes 491528 | tf_op jit(solution)/shard_map/ppermute | solution.py:643
  66.2 11.7 %collective-permute-start.2 = (bf16[32,2560]{1,0:T(8,128)(2,1)S(1)}, bf16[32,2560]{1,0:T(8,128)(2,1)S(1)}, u32[]{:S(2)}, u32[]{:S(2)}) collective-permute-start(bf16[32,2560]{1,0:T(8,128)(2,1)S(1)} %get-tuple-element.41), channel_id=1, source_target_pairs={{0,4},{1,5},{2,6},{3,7},{4,0},{5,1},{6,2},{7,3},{8,12},{9,13},{10,... | collective-permute-start | bytes 491528 | tf_op jit(solution)/shard_map/ppermute | solution.py:643
  67.1 10.7 %collective-permute-start.3 = (bf16[32,2560]{1,0:T(8,128)(2,1)S(1)}, bf16[32,2560]{1,0:T(8,128)(2,1)S(1)}, u32[]{:S(2)}, u32[]{:S(2)}) collective-permute-start(bf16[32,2560]{1,0:T(8,128)(2,1)S(1)} %get-tuple-element.42), channel_id=1, source_target_pairs={{0,6},{1,7},{2,0},{3,1},{4,2},{5,3},{6,4},{7,5},{8,14},{9,15},{10,... | collective-permute-start | bytes 491528 | tf_op jit(solution)/shard_map/ppermute | solution.py:643
  69.4 13.2 %copy-start = (bf16[2016,384]{1,0:T(8,128)(2,1)S(1)}, bf16[2016,384]{1,0:T(8,128)(2,1)}, u32[]{:S(2)}) copy-start(bf16[2016,384]{1,0:T(8,128)(2,1)} %ow_hbm.3) | copy-start | bytes 4644868
  69.4 13.2 %copy-start.2 = (f32[256,128]{1,0:T(8,128)S(1)}, f32[256,128]{1,0:T(8,128)}, u32[]{:S(2)}) copy-start(f32[256,128]{1,0:T(8,128)} %get-tuple-element.43.frame_q_ref) | copy-start | bytes 393220
  69.4 13.2 %copy-start.3 = (f32[32,128]{1,0:T(8,128)S(1)}, f32[32,128]{1,0:T(8,128)}, u32[]{:S(2)}) copy-start(f32[32,128]{1,0:T(8,128)} %get-tuple-element.44.frame_k_ref) | copy-start | bytes 49156
